TPU v7x, 128 devices: a whole 4x4x4 slice. The times are simulated.
128 devices in a mesh: fsdp: 16 (over z_hi, y, core), tp: 8 (over x, z_lo).
Axes of the slice: x: 4, y: 4, z: 4 (z_hi: 2, z_lo: 2; z = z_hi * 2 + z_lo), core: 2. Of those that a mesh axis runs over, the one named last changes fastest.
Arguments:
- tokens: bfloat16 [16384, 7168], P('fsdp', 'tp'), may hold values from -200 to 200
- gain: float32 [7168], P('tp'), may hold values from 0.1 to 1.9
- rollout_weight: bfloat16 [7168, 9216], P(None, 'tp'), may hold values from -0.0625 to 0.0625
- delta_values: bfloat16 [7168, 9216], P(('fsdp', 'tp')), may hold values from -6 to 6
- scale_exponents: int32 [7168, 72], P(('fsdp', 'tp')), may hold values from -8 to -5
Outputs:
- activated: bfloat16 [16384, 9216], P('fsdp', 'tp')
All inputs are finite; a program needn't handle non-finite values.
Results may differ from a plain program's by a relative error of at most 0.015.
Values may be sent and summed in bfloat16 or wider, within the bound.
No kernel may reach another device: no remote copies, remote signals or barrier semaphores. Data moves between devices by JAX's collectives and lax.ppermute only.
A program may use at most 256 MiB of HBM per device.

v0:
```python
import jax
import jax.numpy as jnp
from jax import lax
from jax.sharding import PartitionSpec as P

D = 7168


def power_two(exps):
    total = jnp.zeros(exps.shape, jnp.float32)
    for level in range(-8, -4):
        total = total + jnp.where(exps == level, jnp.float32(2.0**level), jnp.float32(0.0))
    return total


def refreshed_rows(base_rows, delta_rows, exp_rows):
    scale = power_two(exp_rows)
    count, blocks = scale.shape
    group_width = delta_rows.shape[1] // blocks
    wide = jnp.broadcast_to(scale[:, :, None], (count, blocks, group_width)).reshape(
        count, blocks * group_width
    )
    return (base_rows.astype(jnp.float32) + delta_rows.astype(jnp.float32) * wide).astype(
        jnp.bfloat16
    )


def local(tokens, gain, rollout_weight, delta_values, scale_exponents):
    values = tokens.astype(jnp.float32)
    partial_sq = jnp.sum(values * values, axis=1, keepdims=True)
    total_sq = lax.psum(partial_sq, "tp")
    normed = (values * lax.rsqrt(total_sq / D + 1e-06) * gain[None, :]).astype(jnp.bfloat16)
    whole = lax.all_gather(normed, "tp", axis=1, tiled=True)
    gathered = (
        lax.all_gather(delta_values, "fsdp", axis=0, tiled=True),
        lax.all_gather(scale_exponents, "fsdp", axis=0, tiled=True),
    )
    parted = (
        lax.all_to_all(gathered[0], "tp", split_axis=1, concat_axis=0, tiled=True),
        lax.all_to_all(gathered[1], "tp", split_axis=1, concat_axis=0, tiled=True),
    )
    fsdp_count = lax.axis_size("fsdp")
    tp_count = lax.axis_size("tp")

    def restore(array):
        block = array.shape[0] // (fsdp_count * tp_count)
        shaped = array.reshape(tp_count, fsdp_count, block, array.shape[1])
        return jnp.swapaxes(shaped, 0, 1).reshape(-1, array.shape[1])

    fresh = refreshed_rows(rollout_weight, restore(parted[0]), restore(parted[1]))
    hidden = jnp.dot(whole, fresh, preferred_element_type=jnp.float32)
    return jax.nn.silu(hidden).astype(jnp.bfloat16)


def solution(mesh):
    in_specs = (
        P("fsdp", "tp"),
        P("tp"),
        P(None, "tp"),
        P(("fsdp", "tp"), None),
        P(("fsdp", "tp"), None),
    )
    out_specs = P("fsdp", "tp")
    return jax.shard_map(local, mesh=mesh, in_specs=in_specs, out_specs=out_specs, check_vma=False)
```

profile of v0, /device:TPU:1, one launch (start us, length us, event | category | flops | bytes accessed | tf_op | source)
XLA Modules:
  0.0 641.5 jit_solution(3234945590372838144)
XLA Ops:
  7.4 0.7 all-gather.5.cloned.1.call-update
  8.1 29.1 %all_gather.11 = s32[896,72]{1,0:T(8,128)S(1)} all-gather(s32[56,72]{1,0:T(8,128)} %param.9), channel_id=1, replica_groups=mesh['fsdp'=16,'tp'=8] {'fsdp'}, dimensions={0}, use_global_device_ids=true | all-gather | bytes 274176 | tf_op jit(solution)/shard_map/all_gather | solution.py:36
  37.2 0.2 copy.25
  37.4 0.8 all_to_all.22
  38.2 4.3 all-to-all-start.1
  42.5 2.0 fusion.2
  44.5 16.1 %psum.7 = f32[1024,1]{0,1:T(1,128)S(1)} all-reduce(f32[1024,1]{0,1:T(1,128)S(1)} %bitcast.33), channel_id=1, replica_groups=mesh['fsdp'=16,'tp'=8] {'tp'}, use_global_device_ids=true, to_apply=%region_1.0 | all-reduce | flops 1024 | bytes 8192 | tf_op jit(solution)/shard_map/psum | solution.py:31
  60.6 64.8 %all-gather.5.cloned.1.call-done = bf16[896,9216]{1,0:T(8,128)(2,1)} async-done(((bf16[56,9216]{1,0:T(8,128)(2,1)}), bf16[896,9216]{1,0:T(8,128)(2,1)}) %all-gather.5.cloned.1.call-update) | async-done | bytes 16515088 | tf_op jit(solution)/shard_map/all_gather | solution.py:35
  125.5 20.3 %copy.22 = bf16[896,9216]{0,1:T(8,128)(2,1)} copy(bf16[896,9216]{1,0:T(8,128)(2,1)} %all-gather.5.cloned.1.call-done) | data formatting | bytes 33030144 | tf_op jit(solution)/shard_map/all_gather | solution.py:35
  145.8 5.9 all-to-all-start
  151.7 1.7 fusion.4
  153.5 0.2 add_bitcast_fusion
  153.7 0.4 reshape.92
  154.2 0.2 copy.27
  154.4 0.4 reshape.89
  154.8 11.2 %broadcast_in_dim.36 = f32[7168,9,128]{0,2,1:T(8,128)} broadcast(f32[7168,9]{0,1:T(8,128)S(1)} %reshape.89), dimensions={0,1} | broadcast | bytes 33288192 | tf_op jit(solution)/shard_map/broadcast_in_dim | solution.py:20
  166.0 33.3 %copy.28 = f32[7168,1152]{1,0:T(8,128)} copy(f32[7168,1152]{0,1:T(8,128)} %bitcast.28) | data formatting | bytes 66060288 | tf_op jit(solution)/shard_map/reshape | solution.py:20
  199.3 228.2 %all-to-all-done = bf16[896,8,1152]{0,2,1:T(8,128)(2,1)} async-done(((bf16[896,8,1152]{0,2,1:T(8,128)(2,1)}), bf16[896,8,1152]{0,2,1:T(8,128)(2,1)}, u32[]{:S(2)}, u32[]{:S(2)}) %all-to-all-start) | async-done | bytes 16515104 | tf_op jit(solution)/shard_map/all_to_all | solution.py:39
  427.5 18.2 %convert_bitcast_fusion = f32[8,896,1152]{1,2,0:T(8,128)} fusion(bf16[896,8,1152]{0,2,1:T(8,128)(2,1)} %all-to-all-done), kind=kLoop, calls=%fused_computation.3 | loop fusion | flops 8257536 | bytes 49545216 | tf_op jit(solution)/shard_map/convert_element_type | solution.py:23
  445.7 33.8 %copy.23 = f32[8,896,1152]{2,1,0:T(8,128)} copy(f32[8,896,1152]{1,2,0:T(8,128)} %convert_bitcast_fusion) | data formatting | bytes 66060288 | tf_op jit(solution)/shard_map/convert_element_type | solution.py:23
  479.5 22.6 %copy.24 = f32[16,8,56,1152]{3,2,1,0:T(8,128)} copy(f32[16,8,56,1152]{3,2,0,1:T(8,128)} %bitcast.29) | data formatting | bytes 66060288 | tf_op jit(solution)/shard_map/convert_element_type | solution.py:23
  502.1 32.1 %fusion.1 = bf16[7168,1152]{1,0:T(8,128)(2,1)} fusion(f32[7168,1152]{1,0:T(8,128)} %copy.28, f32[16,8,56,1152]{3,2,1,0:T(8,128)} %copy.24, bf16[7168,1152]{1,0:T(8,128)(2,1)} %param.7), kind=kLoop, calls=%fused_computation.2 | loop fusion | flops 33030144 | bytes 99090432 | tf_op jit(solution)/shard_map/convert_element_type | solution.py:23
  534.2 72.9 %all-gather.3.cloned.1.call-done = bf16[1024,7168]{1,0:T(8,128)(2,1)} async-done(((bf16[1024,896]{1,0:T(8,128)(2,1)}), bf16[1024,7168]{1,0:T(8,128)(2,1)}) %all-gather.3.cloned.1.call-update) | async-done | bytes 14680080 | tf_op jit(solution)/shard_map/all_gather | solution.py:33
  607.1 26.9 %multiply_convert_fusion = bf16[1024,1152]{1,0:T(8,128)(2,1)} fusion(bf16[1024,7168]{1,0:T(8,128)(2,1)} %all-gather.3.cloned.1.call-done, bf16[7168,1152]{1,0:T(8,128)(2,1)} %fusion.1), kind=kOutput, calls=%fused_computation.4 | convolution fusion | flops 16917331968 | bytes 33554432 | tf_op jit(solution)/shard_map/dot_general | solution.py:51
  (10 shorter events, 0.2 us)
Async XLA Ops:
  7.4 118.1 %all-gather.5.cloned.1.call-start = ((), (), s32[]{:S(2)}) async-start(), calls=%async_computation.3 | async-start | bytes 17547264 | tf_op jit(solution)/shard_map/all_gather | solution.py:35
  38.2 107.6 %all-to-all-start.1 = ((s32[896,8,9]{0,2,1:T(8,128)}), s32[896,8,9]{0,2,1:T(8,128)S(1)}, u32[]{:S(2)}, u32[]{:S(2)}) async-start(s32[896,8,9]{0,2,1:T(8,128)} %all_to_all.22), calls=%async_computation.1 | async-start | bytes 917504 | tf_op jit(solution)/shard_map/all_to_all | solution.py:40
  145.8 5.9 copy-start
  145.8 5.9 copy-start.1
  145.8 281.8 %all-to-all-start = ((bf16[896,8,1152]{0,2,1:T(8,128)(2,1)}), bf16[896,8,1152]{0,2,1:T(8,128)(2,1)}, u32[]{:S(2)}, u32[]{:S(2)}) async-start(bf16[896,8,1152]{0,2,1:T(8,128)(2,1)} %bitcast.30), calls=%async_computation | async-start | bytes 33030144 | tf_op jit(solution)/shard_map/all_to_all | solution.py:39
  151.6 455.5 %all-gather.3.cloned.1.call-start = ((), (), s32[]{:S(2)}) async-start(), calls=%async_computation.2 | async-start | bytes 16515072 | tf_op jit(solution)/shard_map/all_gather | solution.py:33
Sparse Core Ops, SparseCore 0:
  10.6 114.7 all-gather.4
Sparse Core Ops, SparseCore 1:
  153.8 453.3 all-gather.2
where the time goes:
time: 643 us; the launch traced here: 641 us
  waiting for transfers between devices  367 us (57%)
  local copies, waits for them, and re-layouts  123 us (19%)
  other arithmetic  54.2 us (8%)
  blocking collectives  45.3 us (7%)
  matrix products  26.9 us (4%)
  between operations  14.9 us (2%)
  starting transfers between devices  10.2 us (2%)
    all_to_all x1, waiting for transfers between devices, local(): lax.all_to_all(gathered[0], 'tp', split_axis=1, concat_axis=0, tiled=True)  228 us
    all_gather x1, waiting for transfers between devices, local(): whole = lax.all_gather(normed, 'tp', axis=1, tiled=True)  72.9 us
    all_gather x1, waiting for transfers between devices, local(): lax.all_gather(delta_values, 'fsdp', axis=0, tiled=True)  64.8 us
    convert_element_type x2, local copies, waits for them, and re-layouts, refreshed_rows(): delta_rows.astype(jnp.float32) * wide  56.4 us
    reshape x1, local copies, waits for them, and re-layouts, refreshed_rows(): jnp.broadcast_to(scale[:, :, None], (count, blocks, group_width))  33.3 us
    convert_element_type x1, other arithmetic, refreshed_rows(): (base_rows.astype(jnp.float32) + delta_rows.astype(jnp.float32) * wide).a...  32.1 us
    all_gather x1, blocking collectives, local(): lax.all_gather(scale_exponents, 'fsdp', axis=0, tiled=True)  29.1 us
    dot_general x1, matrix products, local(): hidden = jnp.dot(whole, fresh, preferred_element_type=jnp.float32)  26.9 us
  transfers between devices with their start and end apart: 4, of which 3 were waited for; matrix products, arithmetic and copies ran while one was open for 28% of the time, Pallas kernels for 0%

commit v1 on v0

v1 whole, which is shorter than its diff:
```python
import functools

import jax
import jax.numpy as jnp
from jax import lax
from jax.experimental import pallas as pl
from jax.experimental.pallas import tpu as pltpu
from jax.sharding import PartitionSpec as P


def links(x=0, z_lo=0, z_hi=0, y=0, core=0):
    pairs = []
    for f in range(16):
        for t in range(8):
            f2 = (((f // 8) + z_hi) % 2) * 8 + (((f // 2) % 4 + y) % 4) * 2 + (f + core) % 2
            t2 = ((t // 2 + x) % 4) * 2 + (t + z_lo) % 2
            pairs.append((f * 8 + t, f2 * 8 + t2))
    return pairs


def shift(value, **step):
    return lax.ppermute(value, ("fsdp", "tp"), links(**step))


def power_two(exps):
    total = jnp.zeros(exps.shape, jnp.float32)
    for level in range(-8, -4):
        total = total + jnp.where(exps == level, jnp.float32(2.0**level), jnp.float32(0.0))
    return total


def scale_kernel(place, exps, delta, *outs):
    groups = exps.shape[1]
    scale = power_two(exps[...])
    x, z_lo = place[0], place[1]
    width = outs[0].shape[2]
    per = width // 128
    scaled = []
    for owner in range(8):
        columns = []
        for g in range(per):
            at = owner * per + g
            piece = delta[:, at * 128 : (at + 1) * 128].astype(jnp.float32) * scale[:, at : at + 1]
            columns.append(piece.astype(jnp.bfloat16))
        block = jnp.concatenate(columns, axis=1)
        j = lax.rem(owner // 2 - x + 4, 4)
        half = jnp.where(z_lo == owner % 2, 0, 1)
        for k in range(4):
            @pl.when(j == k)
            def _(k=k, block=block, half=half):
                outs[k][half] = block


def scaled_delta(place, exps, delta):
    rows, wide = delta.shape
    width = wide // 8
    return pl.pallas_call(
        scale_kernel,
        out_shape=[jax.ShapeDtypeStruct((2, rows, width), jnp.bfloat16)] * 4,
        in_specs=[
            pl.BlockSpec(memory_space=pltpu.SMEM),
            pl.BlockSpec(memory_space=pltpu.VMEM),
            pl.BlockSpec(memory_space=pltpu.VMEM),
        ],
        out_specs=[pl.BlockSpec(memory_space=pltpu.VMEM)] * 4,
        name="scaled_delta",
    )(place, exps, delta)


def refresh_kernel(place, same, other, base, out):
    x, z_lo = place[0], place[1]
    for t in range(8):
        j = lax.rem(x - t // 2 + 4, 4)
        delta = jnp.where(z_lo == t % 2, same[j].astype(jnp.float32), other[j].astype(jnp.float32))
        out[t] = (base[t].astype(jnp.float32) + delta).astype(jnp.bfloat16)


def refresh(place, same, other, base, name):
    return pl.pallas_call(
        refresh_kernel,
        out_shape=jax.ShapeDtypeStruct(base.shape, jnp.bfloat16),
        in_specs=[pl.BlockSpec(memory_space=pltpu.SMEM)] + [pl.BlockSpec(memory_space=pltpu.VMEM)] * 3,
        out_specs=pl.BlockSpec(memory_space=pltpu.VMEM),
        name=name,
    )(place, same, other, base)


def gate(*values):
    return lax.optimization_barrier(values)


def assemble_kernel(spots, place, *refs):
    count = len(spots)
    pieces, out, held, sem, out_sem = refs[:count], refs[count], refs[count + 1], refs[count + 2], refs[count + 3]
    y, z_hi, core = place[2], place[3], place[4]
    full = out.shape[0] // 16
    copies = []
    for at, (step, other_core, other_hi) in enumerate(spots):
        y2 = lax.rem(y + step + 4, 4)
        hi = lax.rem(z_hi + other_hi, 2)
        c = lax.rem(core + other_core, 2)
        row = pl.multiple_of((hi * 8 + y2 * 2 + c) * full, 16)
        copy = pltpu.make_async_copy(pieces[at], held.at[pl.ds(row, full)], sem.at[at])
        copy.start()
        copies.append(copy)
    for copy in copies:
        copy.wait()
    copy = pltpu.make_async_copy(held, out, out_sem)
    copy.start()
    copy.wait()


def assemble(place, pieces, spots):
    full, width = pieces[0].shape
    count = len(pieces)
    return pl.pallas_call(
        functools.partial(assemble_kernel, spots),
        out_shape=jax.ShapeDtypeStruct((full * 16, width), jnp.bfloat16),
        in_specs=[pl.BlockSpec(memory_space=pltpu.SMEM)] + [pl.BlockSpec(memory_space=pl.ANY)] * count,
        out_specs=pl.BlockSpec(memory_space=pl.ANY),
        scratch_shapes=[
            pltpu.VMEM((full * 16, width), jnp.bfloat16),
            pltpu.SemaphoreType.DMA((count,)),
            pltpu.SemaphoreType.DMA,
        ],
        compiler_params=pltpu.CompilerParams(vmem_limit_bytes=30 * 2**20),
        cost_estimate=pl.CostEstimate(flops=0, bytes_accessed=64 * full * width, transcendentals=0),
        name="assemble_weight",
    )(place, *pieces)


STEPS = (0, -1, 1, 2)
TILE = 256


def product_kernel(spots, start, fresh_out, place, *refs):
    count = len(spots)
    pieces, inv, w = refs[:count], refs[count], refs[count + 1]
    out, xbuf, wbuf, acc, result, xsem, wsem, osem = refs[count + (2 if fresh_out else 3) :]
    x, z_lo = place[0], place[1]
    depth = wbuf.shape[1]
    rows = acc.shape[0]
    waits = [[], [], [], []]
    for j in range(4):
        for at, (k, row, column) in enumerate(spots):
            if k != j:
                continue
            ref = pieces[at]
            target = xbuf.at[j, pl.ds(row, ref.shape[0])]
            if column is not None:
                half = depth // 2
                side = jnp.where(z_lo == 0, column, 1 - column)
                target = xbuf.at[j, pl.ds(row, ref.shape[0]), pl.ds(pl.multiple_of(side * half, 128), half)]
            copy = pltpu.make_async_copy(ref, target, xsem.at[at])
            copy.start()
            waits[j].append(copy)
        block = pl.multiple_of(lax.rem(x + STEPS[j] + 4, 4) * depth, 16)
        copy = pltpu.make_async_copy(w.at[pl.ds(block, depth)], wbuf.at[j], wsem.at[j])
        copy.start()
        waits[j].append(copy)
    for j in range(4):
        for copy in waits[j]:
            copy.wait()

        @pl.loop(0, rows // TILE)
        def _(i, j=j):
            here = pl.ds(pl.multiple_of(i * TILE, TILE), TILE)
            part = jnp.dot(xbuf[j, here], wbuf[j], preferred_element_type=jnp.float32)
            if j == 0:
                acc[here] = part
            elif j < 3:
                acc[here] += part
            else:
                hidden = (acc[here] + part) * inv[here]
                result[here] = (hidden / (1.0 + jnp.exp(-hidden))).astype(result.dtype)

    copy = pltpu.make_async_copy(result, out.at[pl.ds(start, rows)], osem)
    copy.start()
    copy.wait()


def product(place, pieces, spots, inv, w, start, total, out, name):
    rows = inv.shape[0]
    depth, width = w.shape[0] // 4, w.shape[1]
    anywhere = pl.BlockSpec(memory_space=pl.ANY)
    vmem = pl.BlockSpec(memory_space=pltpu.VMEM)
    count = len(pieces)
    operands = [place, *pieces, inv, w] + ([] if out is None else [out])
    return pl.pallas_call(
        functools.partial(product_kernel, spots, start, out is None),
        out_shape=jax.ShapeDtypeStruct((total, width), jnp.bfloat16),
        in_specs=[pl.BlockSpec(memory_space=pltpu.SMEM)]
        + [anywhere] * count
        + [vmem, anywhere]
        + ([] if out is None else [anywhere]),
        out_specs=anywhere,
        input_output_aliases={} if out is None else {count + 3: 0},
        scratch_shapes=[
            pltpu.VMEM((4, rows, depth), jnp.bfloat16),
            pltpu.VMEM((4, depth, width), jnp.bfloat16),
            pltpu.VMEM((rows, width), jnp.float32),
            pltpu.VMEM((rows, width), jnp.bfloat16),
            pltpu.SemaphoreType.DMA((count,)),
            pltpu.SemaphoreType.DMA((4,)),
            pltpu.SemaphoreType.DMA,
        ],
        compiler_params=pltpu.CompilerParams(vmem_limit_bytes=50 * 2**20),
        cost_estimate=pl.CostEstimate(
            flops=2 * rows * 4 * depth * width,
            bytes_accessed=2 * (4 * depth * (rows + width) + rows * width),
            transcendentals=rows * width,
        ),
        name=name,
    )(*operands)


def local(tokens, gain, rollout_weight, delta_values, scale_exponents):
    f, t = lax.axis_index("fsdp"), lax.axis_index("tp")
    x, z_lo = t // 2, t % 2
    z_hi, y, core = f // 8, (f // 2) % 4, f % 2
    place = jnp.stack([x, z_lo, y, z_hi, core]).astype(jnp.int32)
    count, features = tokens.shape
    total = features * 8
    block = rollout_weight.shape[0] // 16

    values = tokens.astype(jnp.float32)
    scaled = (values * gain[None, :]).astype(jnp.bfloat16)
    square = jnp.sum(values * values, axis=1)
    rows = count // 4
    mine = [scaled[m * rows : (m + 1) * rows] for m in (0, 1, 3)]
    last = scaled[2 * rows : 3 * rows]
    half = rows // 2

    def pair(m, theirs):
        return jnp.where(
            z_lo == 0,
            jnp.concatenate([mine[m], theirs], axis=1),
            jnp.concatenate([theirs, mine[m]], axis=1),
        )

    parts = scaled_delta(place, scale_exponents, delta_values)
    got = [parts[0]] + [shift(parts[j], x=j) for j in (1, 2, 3)]
    left_c, right_c = shift(last, x=1), shift(last, x=-1)
    theirs = [shift(mine[0], z_lo=1), shift(mine[1], z_lo=1)]

    got[1], got[2], got[3], theirs[0] = gate(got[1], got[2], got[3], theirs[0])
    same = jnp.stack([g[0] for g in got])
    other = jnp.stack([g[1] for g in got])
    near = shift(other, z_lo=1)
    across = shift(other, z_lo=1, z_hi=1)
    far = shift(same, z_hi=1)
    pairs = [pair(0, theirs[0])]
    left, right = [shift(pairs[0], x=1)], [shift(pairs[0], x=-1)]
    base = rollout_weight.reshape(16, 8, block // 8, rollout_weight.shape[1])
    base_own = lax.dynamic_index_in_dim(base, f, 0, keepdims=False)
    base_far = lax.dynamic_index_in_dim(base, (f + 8) % 16, 0, keepdims=False)
    near, theirs[1], left_c, right_c = gate(near, theirs[1], left_c, right_c)
    fresh_own = refresh(place, same, near, base_own, "refresh_own").reshape(block, -1)

    pairs.append(pair(1, theirs[1]))
    left.append(shift(pairs[1], x=1))
    right.append(shift(pairs[1], x=-1))
    own_left, own_right = shift(fresh_own, y=1), shift(fresh_own, y=-1)
    far_ca, far_cb = shift(left_c[:half], x=1), shift(right_c[half:], x=-1)
    theirs.append(shift(mine[2], z_lo=1))
    theirs_c = shift(last, z_lo=1)

    far, across, left[0], right[0], theirs[2] = gate(far, across, left[0], right[0], theirs[2])
    fresh_far = refresh(place, far, across, base_far, "refresh_far").reshape(block, -1)
    far_left, far_right = shift(fresh_far, y=1), shift(fresh_far, y=-1)
    pairs.append(pair(2, theirs[2]))
    left.append(shift(pairs[2], x=1))
    right.append(shift(pairs[2], x=-1))
    theirs_l, theirs_r = shift(left_c, z_lo=1), shift(right_c, z_lo=1)

    own_left, own_right, left[1], right[1], left[0], far_ca, far_cb = gate(
        own_left, own_right, left[1], right[1], left[0], far_ca, far_cb
    )
    own_opposite = shift(own_left, y=1)
    opposite_0 = shift(left[0], x=1)
    opposite_1 = shift(right[1], x=-1)
    theirs_fa, theirs_fb = shift(far_ca, z_lo=1), shift(far_cb, z_lo=1)

    far_left, far_right, left[2], right[2], own_left = gate(far_left, far_right, left[2], right[2], own_left)
    far_opposite = shift(far_right, y=-1)
    opposite_2a = shift(left[2][:half], x=1)
    opposite_2b = shift(right[2][half:], x=-1)

    rings = [[fresh_own, own_left, own_right, own_opposite], [fresh_far, far_left, far_right, far_opposite]]
    pieces, spots = [], []
    for hi, ring in enumerate(rings):
        for step, piece in zip(STEPS, ring):
            pieces += [piece, shift(piece, core=1)]
            spots += [(step, 0, hi), (step, 1, hi)]
    weight = assemble(place, pieces, spots)

    for step in ({"z_lo": 1}, {"x": 1}, {"x": 2}):
        square = square + shift(square, **step)
    inv = lax.rsqrt(square / total + 1e-06)[:, None]

    tokens_a = [pairs[0], left[0], right[0], opposite_0, pairs[1], left[1], right[1], opposite_1]
    spots_a = [(j, m * rows, None) for m in (0, 1) for j in range(4)]
    tokens_a += [last, theirs_c, left_c, theirs_l, right_c, theirs_r, far_ca, theirs_fa, far_cb, theirs_fb]
    at = 2 * rows
    spots_a += [(j, at, side) for j in range(3) for side in (0, 1)]
    spots_a += [(3, at, 0), (3, at, 1), (3, at + half, 0), (3, at + half, 1)]
    first = product(place, tokens_a, spots_a, inv[: 3 * rows], weight, 0, count, None, "product_a")
    tokens_b = [pairs[2], left[2], right[2], opposite_2a, opposite_2b]
    spots_b = [(0, 0, None), (1, 0, None), (2, 0, None), (3, 0, None), (3, half, None)]
    return product(
        place, tokens_b, spots_b, inv[3 * rows :], weight, 3 * rows, count, first, "product_b"
    )


def solution(mesh):
    in_specs = (
        P("fsdp", "tp"),
        P("tp"),
        P(None, "tp"),
        P(("fsdp", "tp"), None),
        P(("fsdp", "tp"), None),
    )
    out_specs = P("fsdp", "tp")
    return jax.shard_map(local, mesh=mesh, in_specs=in_specs, out_specs=out_specs, check_vma=False)
```

time: 643 us -> 241 us (0.37)
  waiting for transfers between devices: 367 us -> 57.9 us
  local copies, waits for them, and re-layouts: 123 us -> 36.9 us
  starting transfers between devices: 10.2 us -> 79 us
  Pallas kernels: 0 us -> 53.1 us
  blocking collectives: 45.3 us -> 0 us
  other arithmetic: 54.2 us -> 8.92 us
  matrix products: 26.9 us -> 0 us
  between operations: 14.9 us -> 0.56 us
    all_to_all x2 -> x0, waiting for transfers between devices: 228 us -> none  [the longest x1 228 us: local(): lax.all_to_all(gathered[0], 'tp', split_axis=1, concat_axis=0, tiled=True)]
    all_gather x2 -> x0, waiting for transfers between devices: 138 us -> none  [the longest x1 72.9 us: local(): whole = lax.all_gather(normed, 'tp', axis=1, tiled=True)]
    ppermute x0 -> x45, starting transfers between devices: none -> 79 us  [shift(): return lax.ppermute(value, ('fsdp', 'tp'), links(**step))]
    ppermute x0 -> x45, waiting for transfers between devices: none -> 57.9 us  [shift(): return lax.ppermute(value, ('fsdp', 'tp'), links(**step))]
    convert_element_type x2 -> x0, local copies, waits for them, and re-layouts: 56.4 us -> none  [refreshed_rows(): delta_rows.astype(jnp.float32) * wide]
    pallas_call x0 -> x6, Pallas kernels: none -> 53.1 us  [the longest x2 31.5 us: product(): pl.pallas_call(functools.partial(product_kernel, spots, start, out is Non...]
    convert_element_type x3 -> x0, other arithmetic: 52 us -> none  [the longest x1 32.1 us: refreshed_rows(): (base_rows.astype(jnp.float32) + delta_rows.astype(jnp.float32) * wide).a...]
    reshape x1 -> x0, local copies, waits for them, and re-layouts: 33.3 us -> none  [refreshed_rows(): jnp.broadcast_to(scale[:, :, None], (count, blocks, group_width))]
  transfers between devices with their start and end apart: 4 -> 45, of which waited for: 3 -> 11; matrix products, arithmetic and copies ran while one was open for 28% -> 7% of each run, Pallas kernels for 0% -> 17%
where the time goes in v1:
time: 241 us; the launch traced here: 236 us
  starting transfers between devices  79 us (33%)
  waiting for transfers between devices  57.9 us (24%)
  Pallas kernels  53.1 us (22%)
  local copies, waits for them, and re-layouts  36.9 us (15%)
  other arithmetic  8.92 us (4%)
    ppermute x45, starting transfers between devices, shift(): return lax.ppermute(value, ('fsdp', 'tp'), links(**step))  79 us
    ppermute x45, waiting for transfers between devices, shift(): return lax.ppermute(value, ('fsdp', 'tp'), links(**step))  57.9 us
    pallas_call x2, Pallas kernels, product(): pl.pallas_call(functools.partial(product_kernel, spots, start, out is Non...  31.5 us
    unnamed x98, local copies, waits for them, and re-layouts  28.4 us
    pallas_call x1, Pallas kernels, assemble(): pl.pallas_call(functools.partial(assemble_kernel, spots), out_shape=jax.S...  12.3 us
    pallas_call x2, Pallas kernels, refresh(): pl.pallas_call(refresh_kernel, out_shape=jax.ShapeDtypeStruct(base.shape,...  5.85 us
    select_n x3, other arithmetic, pair(): jnp.where(z_lo == 0, jnp.concatenate([mine[m], theirs], axis=1), jnp.conc...  4.85 us
  transfers between devices with their start and end apart: 45, of which 11 were waited for; matrix products, arithmetic and copies ran while one was open for 7% of the time, Pallas kernels for 17%

profile of v1, /device:TPU:1, one launch (start us, length us, event | category | flops | bytes accessed | tf_op | source)
XLA Modules:
  0.0 236.3 jit_solution(7146272012910901492)
XLA Ops:
  0.7 3.5 %scaled_delta.1 = (bf16[2,56,1152]{2,1,0:T(8,128)(2,1)}, bf16[2,56,1152]{2,1,0:T(8,128)(2,1)}, bf16[2,56,1152]{2,1,0:T(8,128)(2,1)}, bf16[2,56,1152]{2,1,0:T(8,128)(2,1)}) custom-call(s32[5]{0:T(128)} %stack.29.place, s32[56,72]{1,0:T(8,128)} %exps.1, bf16[56,9216]{1,0:T(8,128)(2,1)} %delta.1), custom_call_target="tpu_custom_call" | custom-call | tf_op jit(solution)/shard_map/scaled_delta/pallas_call | solution.py:57
  17.2 2.9 %collective-permute-done.1 = bf16[2,56,1152]{2,1,0:T(8,128)(2,1)S(1)} collective-permute-done((bf16[2,56,1152]{2,1,0:T(8,128)(2,1)}, bf16[2,56,1152]{2,1,0:T(8,128)(2,1)S(1)}, u32[]{:S(2)}, u32[]{:S(2)}) %collective-permute-start.1) | collective-permute-done | bytes 258080 | tf_op jit(solution)/shard_map/ppermute | solution.py:22
  20.1 3.1 %collective-permute-done.3 = bf16[256,896]{1,0:T(8,128)(2,1)} collective-permute-done((bf16[256,896]{1,0:T(8,128)(2,1)S(1)}, bf16[256,896]{1,0:T(8,128)(2,1)}, u32[]{:S(2)}, u32[]{:S(2)}) %collective-permute-start.3) | collective-permute-done | bytes 458784 | tf_op jit(solution)/shard_map/ppermute | solution.py:22
  28.2 8.5 %collective-permute-done.25 = f32[1024]{0:T(1024)S(1)} collective-permute-done((f32[1024]{0:T(1024)S(1)}, f32[1024]{0:T(1024)S(1)}, u32[]{:S(2)}, u32[]{:S(2)}) %collective-permute-start.25) | collective-permute-done | bytes 4128 | tf_op jit(solution)/shard_map/ppermute | solution.py:22
  41.6 5.0 %collective-permute-done.14 = bf16[256,896]{1,0:T(8,128)(2,1)} collective-permute-done((bf16[256,896]{1,0:T(8,128)(2,1)S(1)}, bf16[256,896]{1,0:T(8,128)(2,1)}, u32[]{:S(2)}, u32[]{:S(2)}) %collective-permute-start.14) | collective-permute-done | bytes 458784 | tf_op jit(solution)/shard_map/ppermute | solution.py:22
  47.2 3.2 %collective-permute-start.5 = (bf16[4,56,1152]{2,1,0:T(8,128)(2,1)}, bf16[4,56,1152]{2,1,0:T(8,128)(2,1)}, u32[]{:S(2)}, u32[]{:S(2)}) collective-permute-start(bf16[4,56,1152]{2,1,0:T(8,128)(2,1)} %pad_maximum_fusion.1), channel_id=1, source_target_pairs={{0,65},{1,64},{2,67},{3,66},{4,69},{5,68},{6,71},{7,70},{8,73},{9,... | collective-permute-start | bytes 1548296 | tf_op jit(solution)/shard_map/ppermute | solution.py:22
  52.8 3.7 %collective-permute-done.8 = bf16[256,896]{1,0:T(8,128)(2,1)S(1)} collective-permute-done((bf16[256,896]{1,0:T(8,128)(2,1)S(1)}, bf16[256,896]{1,0:T(8,128)(2,1)S(1)}, u32[]{:S(2)}, u32[]{:S(2)}) %collective-permute-start.8) | collective-permute-done | bytes 458784 | tf_op jit(solution)/shard_map/ppermute | solution.py:22
  57.6 3.0 %dynamic-slice_bitcast_fusion = (bf16[8,56,1152]{2,1,0:T(8,128)(2,1)}, bf16[8,56,1152]{2,1,0:T(8,128)(2,1)}) fusion(bf16[16,8,56,1152]{3,2,1,0:T(8,128)(2,1)} %bitcast.22, s32[]{:T(128)S(6)} %select_n.63, s32[]{:T(128)S(6)} %select_n.62), kind=kLoop, calls=%fused_computation.4 | loop fusion | bytes 4128776 | tf_op jit(solution)/shard_map/jit(dynamic_index_in_dim)/squeeze | solution.py:255
  60.6 2.9 %refresh_own.1 = bf16[8,56,1152]{2,1,0:T(8,128)(2,1)} custom-call(s32[5]{0:T(128)} %stack.29.place, bf16[4,56,1152]{2,1,0:T(8,128)(2,1)} %copy-done.41, bf16[4,56,1152]{2,1,0:T(8,128)(2,1)} %copy-done.42, bf16[8,56,1152]{2,1,0:T(8,128)(2,1)} %get-tuple-element.63.base), custom_call_target="tpu_custom_call" | custom-call | tf_op jit(solution)/shard_map/refresh_own/pallas_call | solution.py:79
  65.9 4.6 %collective-permute-done.4.same = bf16[4,56,1152]{2,1,0:T(8,128)(2,1)} collective-permute-done((bf16[4,56,1152]{2,1,0:T(8,128)(2,1)S(1)}, bf16[4,56,1152]{2,1,0:T(8,128)(2,1)}, u32[]{:S(2)}, u32[]{:S(2)}) %collective-permute-start.4) | collective-permute-done | bytes 516128 | tf_op jit(solution)/shard_map/ppermute | solution.py:22
  73.7 11.2 %collective-permute-done.27 = f32[1024]{0:T(1024)S(1)} collective-permute-done((f32[1024]{0:T(1024)S(1)}, f32[1024]{0:T(1024)S(1)}, u32[]{:S(2)}, u32[]{:S(2)}) %collective-permute-start.27) | collective-permute-done | bytes 4128 | tf_op jit(solution)/shard_map/ppermute | solution.py:22
  84.9 2.7 %collective-permute-start.18 = (bf16[448,1152]{1,0:T(8,128)(2,1)}, bf16[448,1152]{1,0:T(8,128)(2,1)}, u32[]{:S(2)}, u32[]{:S(2)}) collective-permute-start(bf16[448,1152]{1,0:T(8,128)(2,1)} %bitcast.15), channel_id=1, source_target_pairs={{0,48},{1,49},{2,50},{3,51},{4,52},{5,53},{6,54},{7,55},{8,56},{9,... | collective-permute-start | bytes 3096584 | tf_op jit(solution)/shard_map/ppermute | solution.py:22
  87.9 5.0 %collective-permute-done.22.refs_16_ = bf16[128,896]{1,0:T(8,128)(2,1)S(1)} collective-permute-done((bf16[128,896]{1,0:T(8,128)(2,1)S(1)}, bf16[128,896]{1,0:T(8,128)(2,1)S(1)}, u32[]{:S(2)}, u32[]{:S(2)}) %collective-permute-start.22) | collective-permute-done | bytes 229408 | tf_op jit(solution)/shard_map/ppermute | solution.py:22
  93.6 2.9 %refresh_far.1 = bf16[8,56,1152]{2,1,0:T(8,128)(2,1)} custom-call(s32[5]{0:T(128)} %stack.29.place, bf16[4,56,1152]{2,1,0:T(8,128)(2,1)} %collective-permute-done.4.same, bf16[4,56,1152]{2,1,0:T(8,128)(2,1)} %collective-permute-done.5.other, bf16[8,56,1152]{2,1,0:T(8,128)(2,1)} %get-tuple-element.64.base), custom_call_target="tpu_custom_call" | custom-call | tf_op jit(solution)/shard_map/refresh_far/pallas_call | solution.py:79
  100.0 4.7 %collective-permute-done.18.refs_4_ = bf16[448,1152]{1,0:T(8,128)(2,1)} collective-permute-done((bf16[448,1152]{1,0:T(8,128)(2,1)}, bf16[448,1152]{1,0:T(8,128)(2,1)}, u32[]{:S(2)}, u32[]{:S(2)}) %collective-permute-start.18) | collective-permute-done | bytes 1032224 | tf_op jit(solution)/shard_map/ppermute | solution.py:22
  104.7 12.1 %collective-permute-start.28 = (bf16[448,1152]{1,0:T(8,128)(2,1)S(1)}, bf16[448,1152]{1,0:T(8,128)(2,1)S(1)}, u32[]{:S(2)}, u32[]{:S(2)}) collective-permute-start(bf16[448,1152]{1,0:T(8,128)(2,1)S(1)} %bitcast.16), channel_id=1, source_target_pairs={{0,8},{1,9},{2,10},{3,11},{4,12},{5,13},{6,14},{7,15},{8,0},{9,1},... | collective-permute-start | bytes 3096584 | tf_op jit(solution)/shard_map/ppermute | solution.py:22
  118.2 8.7 %collective-permute-done.10.refs_12_ = bf16[448,1152]{1,0:T(8,128)(2,1)S(1)} collective-permute-done((bf16[448,1152]{1,0:T(8,128)(2,1)}, bf16[448,1152]{1,0:T(8,128)(2,1)S(1)}, u32[]{:S(2)}, u32[]{:S(2)}) %collective-permute-start.10) | collective-permute-done | bytes 1032224 | tf_op jit(solution)/shard_map/ppermute | solution.py:22
  130.1 6.1 %collective-permute-start.30 = (bf16[448,1152]{1,0:T(8,128)(2,1)}, bf16[448,1152]{1,0:T(8,128)(2,1)S(1)}, u32[]{:S(2)}, u32[]{:S(2)}) collective-permute-start(bf16[448,1152]{1,0:T(8,128)(2,1)} %collective-permute-done.18.refs_4_), channel_id=1, source_target_pairs={{0,8},{1,9},{2,10},{3,11},{4,12},{5,13},{6,14},{7,15},{8,0},{9,1},... | collective-permute-start | bytes 3096584 | tf_op jit(solution)/shard_map/ppermute | solution.py:22
  140.3 6.8 %collective-permute-start.29 = (bf16[448,1152]{1,0:T(8,128)(2,1)}, bf16[448,1152]{1,0:T(8,128)(2,1)S(1)}, u32[]{:S(2)}, u32[]{:S(2)}) collective-permute-start(bf16[448,1152]{1,0:T(8,128)(2,1)} %collective-permute-done.17.refs_2_), channel_id=1, source_target_pairs={{0,8},{1,9},{2,10},{3,11},{4,12},{5,13},{6,14},{7,15},{8,0},{9,1},... | collective-permute-start | bytes 3096584 | tf_op jit(solution)/shard_map/ppermute | solution.py:22
  149.5 6.5 %collective-permute-start.35 = (bf16[448,1152]{1,0:T(8,128)(2,1)S(1)}, bf16[448,1152]{1,0:T(8,128)(2,1)S(1)}, u32[]{:S(2)}, u32[]{:S(2)}) collective-permute-start(bf16[448,1152]{1,0:T(8,128)(2,1)S(1)} %collective-permute-done.10.refs_12_), channel_id=1, source_target_pairs={{0,8},{1,9},{2,10},{3,11},{4,12},{5,13},{6,14},{7,15},{8,0},{9,1},... | collective-permute-start | bytes 3096584 | tf_op jit(solution)/shard_map/ppermute | solution.py:22
  159.0 3.4 %collective-permute-start.37 = (bf16[448,1152]{1,0:T(8,128)(2,1)S(1)}, bf16[448,1152]{1,0:T(8,128)(2,1)S(1)}, u32[]{:S(2)}, u32[]{:S(2)}) collective-permute-start(bf16[448,1152]{1,0:T(8,128)(2,1)S(1)} %collective-permute-done.36.refs_14_), channel_id=1, source_target_pairs={{0,8},{1,9},{2,10},{3,11},{4,12},{5,13},{6,14},{7,15},{8,0},{9,1},... | collective-permute-start | bytes 3096584 | tf_op jit(solution)/shard_map/ppermute | solution.py:22
  189.5 12.3 %assemble_weight.1.refs_19_.refs_6_ = bf16[7168,1152]{1,0:T(8,128)(2,1)} custom-call(s32[5]{0:T(128)S(1)} %copy-done.34, bf16[448,1152]{1,0:T(8,128)(2,1)S(1)} %bitcast.17, bf16[448,1152]{1,0:T(8,128)(2,1)S(1)} %copy-done.9, bf16[448,1152]{1,0:T(8,128)(2,1)} %collective-permute-done.17.refs_2_, bf16[448,1152]{1,0:T(8,128)(2,1)S(1)} %copy-done.19, ...), custom_call_target="tpu_custom_call" | custom-call | bytes 33030144 | tf_op jit(solution)/shard_map/assemble_weight/pallas_call | solution.py:116
  204.6 21.8 %product_a.1.refs_7_ = bf16[1024,1152]{1,0:T(8,128)(2,1)} custom-call(s32[5]{0:T(128)S(1)} %copy-done.34, bf16[256,1792]{1,0:T(8,128)(2,1)} %maximum_select_fusion.refs_0_, bf16[256,1792]{1,0:T(8,128)(2,1)} %collective-permute-done.6.refs_1_, bf16[256,1792]{1,0:T(8,128)(2,1)} %collective-permute-done.7.refs_2_, ...), custom_call_target="tpu_custom_call" | custom-call | flops 12683575296 | bytes 29294592 | tf_op jit(solution)/shard_map/product_a/pallas_call | solution.py:189
  226.4 9.7 %product_b.1 = bf16[1024,1152]{1,0:T(8,128)(2,1)} custom-call(s32[5]{0:T(128)S(1)} %copy-done.34, bf16[256,1792]{1,0:T(8,128)(2,1)S(1)} %maximum_select_fusion.1.refs_0_, bf16[256,1792]{1,0:T(8,128)(2,1)} %collective-permute-done.11.refs_1_, bf16[256,1792]{1,0:T(8,128)(2,1)S(1)} %copy-done.3, ...), custom_call_target="tpu_custom_call", output_to_operand_aliasing={{}: (8, {})} | custom-call | flops 4227858432 | bytes 20774912 | tf_op jit(solution)/shard_map/product_b/pallas_call | solution.py:189
  (192 shorter events, 81.5 us)
Async XLA Ops:
  13.8 26.3 %collective-permute-start.15 = (bf16[256,896]{1,0:T(8,128)(2,1)S(1)}, bf16[256,896]{1,0:T(8,128)(2,1)S(1)}, u32[]{:S(2)}, u32[]{:S(2)}) collective-permute-start(bf16[256,896]{1,0:T(8,128)(2,1)S(1)} %get-tuple-element.67.refs_8_), channel_id=1, source_target_pairs={{0,2},{1,3},{2,4},{3,5},{4,6},{5,7},{6,0},{7,1},{8,10},{9,11},{10,... | collective-permute-start | bytes 1376264 | tf_op jit(solution)/shard_map/ppermute | solution.py:22
  14.8 25.7 %collective-permute-start.16 = (bf16[256,896]{1,0:T(8,128)(2,1)S(1)}, bf16[256,896]{1,0:T(8,128)(2,1)S(1)}, u32[]{:S(2)}, u32[]{:S(2)}) collective-permute-start(bf16[256,896]{1,0:T(8,128)(2,1)S(1)} %get-tuple-element.67.refs_8_), channel_id=1, source_target_pairs={{0,6},{1,7},{2,0},{3,1},{4,2},{5,3},{6,4},{7,5},{8,14},{9,15},{10,... | collective-permute-start | bytes 1376264 | tf_op jit(solution)/shard_map/ppermute | solution.py:22
  25.4 21.8 %collective-permute-start.13 = (bf16[4,56,1152]{2,1,0:T(8,128)(2,1)}, bf16[4,56,1152]{2,1,0:T(8,128)(2,1)S(1)}, u32[]{:S(2)}, u32[]{:S(2)}) collective-permute-start(bf16[4,56,1152]{2,1,0:T(8,128)(2,1)} %pad_maximum_fusion.1), channel_id=1, source_target_pairs={{0,1},{1,0},{2,3},{3,2},{4,5},{5,4},{6,7},{7,6},{8,9},{9,8},{10,11... | collective-permute-start | bytes 1548296 | tf_op jit(solution)/shard_map/ppermute | solution.py:22
  40.5 31.4 %collective-permute-start.6 = (bf16[256,1792]{1,0:T(8,128)(2,1)}, bf16[256,1792]{1,0:T(8,128)(2,1)}, u32[]{:S(2)}, u32[]{:S(2)}) collective-permute-start(bf16[256,1792]{1,0:T(8,128)(2,1)} %maximum_select_fusion.refs_0_), channel_id=1, source_target_pairs={{0,2},{1,3},{2,4},{3,5},{4,6},{5,7},{6,0},{7,1},{8,10},{9,11},{10,... | collective-permute-start | bytes 2752520 | tf_op jit(solution)/shard_map/ppermute | solution.py:22
  46.7 25.6 %collective-permute-start.7 = (bf16[256,1792]{1,0:T(8,128)(2,1)}, bf16[256,1792]{1,0:T(8,128)(2,1)}, u32[]{:S(2)}, u32[]{:S(2)}) collective-permute-start(bf16[256,1792]{1,0:T(8,128)(2,1)} %maximum_select_fusion.refs_0_), channel_id=1, source_target_pairs={{0,6},{1,7},{2,0},{3,1},{4,2},{5,3},{6,4},{7,5},{8,14},{9,15},{10,... | collective-permute-start | bytes 2752520 | tf_op jit(solution)/shard_map/ppermute | solution.py:22
  57.3 39.3 %collective-permute-start.19 = (bf16[256,1792]{1,0:T(8,128)(2,1)}, bf16[256,1792]{1,0:T(8,128)(2,1)}, u32[]{:S(2)}, u32[]{:S(2)}) collective-permute-start(bf16[256,1792]{1,0:T(8,128)(2,1)} %maximum_select_fusion.2.refs_4_), channel_id=1, source_target_pairs={{0,2},{1,3},{2,4},{3,5},{4,6},{5,7},{6,0},{7,1},{8,10},{9,11},{10,... | collective-permute-start | bytes 2752520 | tf_op jit(solution)/shard_map/ppermute | solution.py:22
  63.5 34.4 %collective-permute-start.20 = (bf16[256,1792]{1,0:T(8,128)(2,1)}, bf16[256,1792]{1,0:T(8,128)(2,1)}, u32[]{:S(2)}, u32[]{:S(2)}) collective-permute-start(bf16[256,1792]{1,0:T(8,128)(2,1)} %maximum_select_fusion.2.refs_4_), channel_id=1, source_target_pairs={{0,6},{1,7},{2,0},{3,1},{4,2},{5,3},{6,4},{7,5},{8,14},{9,15},{10,... | collective-permute-start | bytes 2752520 | tf_op jit(solution)/shard_map/ppermute | solution.py:22
  70.5 29.4 %collective-permute-start.17 = (bf16[448,1152]{1,0:T(8,128)(2,1)}, bf16[448,1152]{1,0:T(8,128)(2,1)}, u32[]{:S(2)}, u32[]{:S(2)}) collective-permute-start(bf16[448,1152]{1,0:T(8,128)(2,1)} %bitcast.14), channel_id=1, source_target_pairs={{0,16},{1,17},{2,18},{3,19},{4,20},{5,21},{6,22},{7,23},{8,24},{9,... | collective-permute-start | bytes 3096584 | tf_op jit(solution)/shard_map/ppermute | solution.py:22
  92.9 23.9 %collective-permute-start.11 = (bf16[256,1792]{1,0:T(8,128)(2,1)S(1)}, bf16[256,1792]{1,0:T(8,128)(2,1)}, u32[]{:S(2)}, u32[]{:S(2)}) collective-permute-start(bf16[256,1792]{1,0:T(8,128)(2,1)S(1)} %maximum_select_fusion.1.refs_0_), channel_id=1, source_target_pairs={{0,2},{1,3},{2,4},{3,5},{4,6},{5,7},{6,0},{7,1},{8,10},{9,11},{10,... | collective-permute-start | bytes 2752520 | tf_op jit(solution)/shard_map/ppermute | solution.py:22
  96.5 30.3 %collective-permute-start.10 = (bf16[448,1152]{1,0:T(8,128)(2,1)}, bf16[448,1152]{1,0:T(8,128)(2,1)S(1)}, u32[]{:S(2)}, u32[]{:S(2)}) collective-permute-start(bf16[448,1152]{1,0:T(8,128)(2,1)} %bitcast.18), channel_id=1, source_target_pairs={{0,48},{1,49},{2,50},{3,51},{4,52},{5,53},{6,54},{7,55},{8,56},{9,... | collective-permute-start | bytes 3096584 | tf_op jit(solution)/shard_map/ppermute | solution.py:22
  100.0 28.7 %collective-permute-start.9 = (bf16[448,1152]{1,0:T(8,128)(2,1)}, bf16[448,1152]{1,0:T(8,128)(2,1)S(1)}, u32[]{:S(2)}, u32[]{:S(2)}) collective-permute-start(bf16[448,1152]{1,0:T(8,128)(2,1)} %bitcast.19), channel_id=1, source_target_pairs={{0,16},{1,17},{2,18},{3,19},{4,20},{5,21},{6,22},{7,23},{8,24},{9,... | collective-permute-start | bytes 3096584 | tf_op jit(solution)/shard_map/ppermute | solution.py:22
  104.7 34.6 %collective-permute-start.28 = (bf16[448,1152]{1,0:T(8,128)(2,1)S(1)}, bf16[448,1152]{1,0:T(8,128)(2,1)S(1)}, u32[]{:S(2)}, u32[]{:S(2)}) collective-permute-start(bf16[448,1152]{1,0:T(8,128)(2,1)S(1)} %bitcast.16), channel_id=1, source_target_pairs={{0,8},{1,9},{2,10},{3,11},{4,12},{5,13},{6,14},{7,15},{8,0},{9,1},... | collective-permute-start | bytes 3096584 | tf_op jit(solution)/shard_map/ppermute | solution.py:22
  116.8 30.3 %collective-permute-start.33 = (bf16[448,1152]{1,0:T(8,128)(2,1)}, bf16[448,1152]{1,0:T(8,128)(2,1)S(1)}, u32[]{:S(2)}, u32[]{:S(2)}) collective-permute-start(bf16[448,1152]{1,0:T(8,128)(2,1)} %bitcast.20), channel_id=1, source_target_pairs={{0,8},{1,9},{2,10},{3,11},{4,12},{5,13},{6,14},{7,15},{8,0},{9,1},... | collective-permute-start | bytes 3096584 | tf_op jit(solution)/shard_map/ppermute | solution.py:22
  128.7 20.8 %collective-permute-start.31 = (bf16[448,1152]{1,0:T(8,128)(2,1)}, bf16[448,1152]{1,0:T(8,128)(2,1)S(1)}, u32[]{:S(2)}, u32[]{:S(2)}) collective-permute-start(bf16[448,1152]{1,0:T(8,128)(2,1)} %collective-permute-done.17.refs_2_), channel_id=1, source_target_pairs={{0,16},{1,17},{2,18},{3,19},{4,20},{5,21},{6,22},{7,23},{8,24},{9,... | collective-permute-start | bytes 3096584 | tf_op jit(solution)/shard_map/ppermute | solution.py:22
  130.1 26.8 %collective-permute-start.30 = (bf16[448,1152]{1,0:T(8,128)(2,1)}, bf16[448,1152]{1,0:T(8,128)(2,1)S(1)}, u32[]{:S(2)}, u32[]{:S(2)}) collective-permute-start(bf16[448,1152]{1,0:T(8,128)(2,1)} %collective-permute-done.18.refs_4_), channel_id=1, source_target_pairs={{0,8},{1,9},{2,10},{3,11},{4,12},{5,13},{6,14},{7,15},{8,0},{9,1},... | collective-permute-start | bytes 3096584 | tf_op jit(solution)/shard_map/ppermute | solution.py:22
  137.0 22.0 %collective-permute-start.36 = (bf16[448,1152]{1,0:T(8,128)(2,1)S(1)}, bf16[448,1152]{1,0:T(8,128)(2,1)S(1)}, u32[]{:S(2)}, u32[]{:S(2)}) collective-permute-start(bf16[448,1152]{1,0:T(8,128)(2,1)S(1)} %collective-permute-done.10.refs_12_), channel_id=1, source_target_pairs={{0,48},{1,49},{2,50},{3,51},{4,52},{5,53},{6,54},{7,55},{8,56},{9,... | collective-permute-start | bytes 3096584 | tf_op jit(solution)/shard_map/ppermute | solution.py:22
  140.3 23.0 %collective-permute-start.29 = (bf16[448,1152]{1,0:T(8,128)(2,1)}, bf16[448,1152]{1,0:T(8,128)(2,1)S(1)}, u32[]{:S(2)}, u32[]{:S(2)}) collective-permute-start(bf16[448,1152]{1,0:T(8,128)(2,1)} %collective-permute-done.17.refs_2_), channel_id=1, source_target_pairs={{0,8},{1,9},{2,10},{3,11},{4,12},{5,13},{6,14},{7,15},{8,0},{9,1},... | collective-permute-start | bytes 3096584 | tf_op jit(solution)/shard_map/ppermute | solution.py:22
  164.3 40.2 %collective-permute-start.38 = (bf16[256,1792]{1,0:T(8,128)(2,1)}, bf16[256,1792]{1,0:T(8,128)(2,1)}, u32[]{:S(2)}, u32[]{:S(2)}) collective-permute-start(bf16[256,1792]{1,0:T(8,128)(2,1)} %collective-permute-done.6.refs_1_), channel_id=1, source_target_pairs={{0,2},{1,3},{2,4},{3,5},{4,6},{5,7},{6,0},{7,1},{8,10},{9,11},{10,... | collective-permute-start | bytes 2752520 | tf_op jit(solution)/shard_map/ppermute | solution.py:22
  165.4 39.1 %collective-permute-start.39 = (bf16[256,1792]{1,0:T(8,128)(2,1)}, bf16[256,1792]{1,0:T(8,128)(2,1)}, u32[]{:S(2)}, u32[]{:S(2)}) collective-permute-start(bf16[256,1792]{1,0:T(8,128)(2,1)} %collective-permute-done.20.refs_6_), channel_id=1, source_target_pairs={{0,6},{1,7},{2,0},{3,1},{4,2},{5,3},{6,4},{7,5},{8,14},{9,15},{10,... | collective-permute-start | bytes 2752520 | tf_op jit(solution)/shard_map/ppermute | solution.py:22
  169.0 32.7 %collective-permute-start.42 = (bf16[256,896]{1,0:T(8,128)(2,1)}, bf16[256,896]{1,0:T(8,128)(2,1)}, u32[]{:S(2)}, u32[]{:S(2)}) collective-permute-start(bf16[256,896]{1,0:T(8,128)(2,1)} %copy-done.32), channel_id=1, source_target_pairs={{0,1},{1,0},{2,3},{3,2},{4,5},{5,4},{6,7},{7,6},{8,9},{9,8},{10,11... | collective-permute-start | bytes 1376264 | tf_op jit(solution)/shard_map/ppermute | solution.py:22
  171.0 30.9 %collective-permute-start.43 = (bf16[128,896]{1,0:T(8,128)(2,1)}, bf16[128,896]{1,0:T(8,128)(2,1)}, u32[]{:S(2)}, u32[]{:S(2)}) collective-permute-start(bf16[128,896]{1,0:T(8,128)(2,1)} %collective-permute-done.21.refs_14_), channel_id=1, source_target_pairs={{0,1},{1,0},{2,3},{3,2},{4,5},{5,4},{6,7},{7,6},{8,9},{9,8},{10,11... | collective-permute-start | bytes 688136 | tf_op jit(solution)/shard_map/ppermute | solution.py:22
  172.5 32.0 %collective-permute-start.44 = (bf16[128,896]{1,0:T(8,128)(2,1)}, bf16[128,896]{1,0:T(8,128)(2,1)}, u32[]{:S(2)}, u32[]{:S(2)}) collective-permute-start(bf16[128,896]{1,0:T(8,128)(2,1)} %copy-done.39), channel_id=1, source_target_pairs={{0,1},{1,0},{2,3},{3,2},{4,5},{5,4},{6,7},{7,6},{8,9},{9,8},{10,11... | collective-permute-start | bytes 688136 | tf_op jit(solution)/shard_map/ppermute | solution.py:22
  201.8 24.6 %collective-permute-start.23 = (bf16[128,1792]{1,0:T(8,128)(2,1)S(1)}, bf16[128,1792]{1,0:T(8,128)(2,1)S(1)}, u32[]{:S(2)}, u32[]{:S(2)}) collective-permute-start(bf16[128,1792]{1,0:T(8,128)(2,1)S(1)} %slice.74), channel_id=1, source_target_pairs={{0,2},{1,3},{2,4},{3,5},{4,6},{5,7},{6,0},{7,1},{8,10},{9,11},{10,... | collective-permute-start | bytes 1376264 | tf_op jit(solution)/shard_map/ppermute | solution.py:22
  201.9 24.5 %collective-permute-start.24 = (bf16[128,1792]{1,0:T(8,128)(2,1)S(1)}, bf16[128,1792]{1,0:T(8,128)(2,1)S(1)}, u32[]{:S(2)}, u32[]{:S(2)}) collective-permute-start(bf16[128,1792]{1,0:T(8,128)(2,1)S(1)} %slice.75), channel_id=1, source_target_pairs={{0,6},{1,7},{2,0},{3,1},{4,2},{5,3},{6,4},{7,5},{8,14},{9,15},{10,... | collective-permute-start | bytes 1376264 | tf_op jit(solution)/shard_map/ppermute | solution.py:22
  (70 other events, 911.3 us)

commit v2 on v0

v2 whole, which is shorter than its diff:
```python
import functools

import jax
import jax.numpy as jnp
from jax import lax
from jax.experimental import pallas as pl
from jax.experimental.pallas import tpu as pltpu
from jax.sharding import PartitionSpec as P


SCOPED = 60 * 2**20
FREE = pl.CostEstimate(flops=0, bytes_accessed=0, transcendentals=0)


def links(x=0, z_lo=0, z_hi=0, y_by_core=0, core=0):
    pairs = []
    for f in range(16):
        for t in range(8):
            along = y_by_core if f % 2 == 0 else -y_by_core
            f2 = (((f // 8) + z_hi) % 2) * 8 + (((f // 2) % 4 + along) % 4) * 2 + (f + core) % 2
            t2 = ((t // 2 + x) % 4) * 2 + (t + z_lo) % 2
            pairs.append((f * 8 + t, f2 * 8 + t2))
    return pairs


def shift(value, **step):
    return lax.ppermute(value, ("fsdp", "tp"), links(**step))


def position():
    f, t = lax.axis_index("fsdp"), lax.axis_index("tp")
    return t // 2, t % 2, (f // 2) % 4, f // 8, f % 2


def power_two(exps):
    total = jnp.zeros(exps.shape, jnp.float32)
    for level in range(-8, -4):
        total = total + jnp.where(exps == level, jnp.float32(2.0**level), jnp.float32(0.0))
    return total


def scale_kernel(exps, delta, *outs):
    groups = exps.shape[1]
    scale = power_two(exps[...])
    x, z_lo, _, _, _ = position()
    width = outs[0].shape[2]
    per = width // 128
    scaled = []
    for owner in range(8):
        columns = []
        for g in range(per):
            at = owner * per + g
            piece = delta[:, at * 128 : (at + 1) * 128].astype(jnp.float32) * scale[:, at : at + 1]
            columns.append(piece.astype(jnp.bfloat16))
        block = jnp.concatenate(columns, axis=1)
        j = lax.rem(owner // 2 - x + 4, 4)
        half = jnp.where(z_lo == owner % 2, 0, 1)
        for k in range(4):
            @pl.when(j == k)
            def _(k=k, block=block, half=half):
                outs[k][half] = block


def scaled_delta(exps, delta):
    rows, wide = delta.shape
    width = wide // 8
    return pl.pallas_call(
        scale_kernel,
        out_shape=[jax.ShapeDtypeStruct((2, rows, width), jnp.bfloat16)] * 4,
        in_specs=[pl.BlockSpec(memory_space=pltpu.VMEM)] * 2,
        out_specs=[pl.BlockSpec(memory_space=pltpu.VMEM)] * 4,
        compiler_params=pltpu.CompilerParams(vmem_limit_bytes=SCOPED),
        cost_estimate=FREE,
        name="scaled_delta",
    )(exps, delta)


def refresh_kernel(other_hi, same, other, base, out, held, sem):
    x, z_lo, y, z_hi, core = position()
    owner = lax.rem(z_hi + other_hi, 2) * 8 + y * 2 + core
    copy = pltpu.make_async_copy(base.at[pl.ds(owner * 8, 8)], held, sem)
    copy.start()
    copy.wait()
    for t in range(8):
        j = lax.rem(x - t // 2 + 4, 4)
        delta = jnp.where(z_lo == t % 2, same[j].astype(jnp.float32), other[j].astype(jnp.float32))
        out[t] = (held[t].astype(jnp.float32) + delta).astype(jnp.bfloat16)


def refresh(same, other, base, other_hi, name):
    shape = (8, *base.shape[1:])
    vmem = pl.BlockSpec(memory_space=pltpu.VMEM)
    out = pl.pallas_call(
        functools.partial(refresh_kernel, other_hi),
        out_shape=jax.ShapeDtypeStruct(shape, jnp.bfloat16),
        in_specs=[vmem, vmem, pl.BlockSpec(memory_space=pltpu.HBM)],
        out_specs=vmem,
        scratch_shapes=[pltpu.VMEM(shape, jnp.bfloat16), pltpu.SemaphoreType.DMA],
        compiler_params=pltpu.CompilerParams(vmem_limit_bytes=SCOPED),
        cost_estimate=FREE,
        name=name,
    )(same, other, base)
    return out.reshape(8 * shape[1], shape[2])


def gate(*values):
    return lax.optimization_barrier(values)


STEPS = (0, -1, 1, 2)
TILE = 256
HBM = pl.BlockSpec(memory_space=pltpu.HBM)
VMEM = pl.BlockSpec(memory_space=pltpu.VMEM)


def silu(hidden):
    return hidden / (1.0 + jnp.exp(-hidden))


def start_weights(block, held, pieces, spots, sem):
    _, _, y, z_hi, core = position()
    piece = held.shape[0] // 4
    for which, index, step, other_core, other_hi in spots:
        y2 = lax.rem(y + jnp.where(core == 0, step, -step) + 4, 4)
        part = lax.rem(y2, 2) * 2 + lax.rem(core + other_core, 2)

        @pl.when(lax.rem(z_hi + other_hi, 2) * 2 + y2 // 2 == block)
        def _(which=which, index=index, part=part):
            source = pieces[which] if index is None else pieces[which].at[index]
            target = held.at[pl.ds(pl.multiple_of(part * piece, 16), piece)]
            pltpu.make_async_copy(source, target, sem).start()


def start_tokens(held, pieces, spots, sem):
    z_lo = position()[1]
    half = held.shape[1] // 2
    for which, row, side, first, size in spots:
        column = jnp.where(z_lo == 0, side, 1 - side)
        target = held.at[pl.ds(row, size), pl.ds(pl.multiple_of(column * half, 128), half)]
        pltpu.make_async_copy(pieces[which].at[pl.ds(first, size)], target, sem).start()


def wait_all(held, sem):
    pltpu.make_async_copy(held, held, sem).wait()


def product_kernel(own_half, n_tok, n_wt, token_spots, weight_spots, *refs):
    tokens, weights = refs[:n_tok], refs[n_tok : n_tok + n_wt]
    before = None if own_half else refs[n_tok + n_wt]
    out, xbuf, wbuf, acc, xsem, wsem, asem = refs[n_tok + n_wt + (0 if own_half else 1) :]
    x, _, y, _, _ = position()
    blocks = [2 * k + (y // 2 if own_half else 1 - y // 2) for k in range(2)]
    wanted = [block != lax.rem(x + 2, 4) for block in blocks]
    if not own_half:
        load = pltpu.make_async_copy(before, acc, asem)
        load.start()
    for k in range(2):

        @pl.when(wanted[k])
        def _(k=k):
            start_weights(blocks[k], wbuf.at[k], weights, weight_spots, wsem.at[k])

        for j in range(3):

            @pl.when(blocks[k] == lax.rem(x + STEPS[j] + 4, 4))
            def _(k=k, j=j):
                start_tokens(xbuf.at[k], tokens, token_spots[j], xsem.at[k])

    if not own_half:
        load.wait()
    else:

        @pl.when(jnp.logical_not(wanted[0]))
        def _():
            acc[...] = jnp.zeros_like(acc)

    for k in range(2):

        @pl.when(wanted[k])
        def _(k=k):
            wait_all(xbuf.at[k], xsem.at[k])
            wait_all(wbuf.at[k], wsem.at[k])

            @pl.loop(0, acc.shape[0] // TILE)
            def _(i):
                here = pl.ds(pl.multiple_of(i * TILE, TILE), TILE)
                part = jnp.dot(xbuf[k, here], wbuf[k], preferred_element_type=jnp.float32)
                if k == 0 and own_half:
                    acc[here] = part
                else:
                    acc[here] += part

    store = pltpu.make_async_copy(acc, out, asem)
    store.start()
    store.wait()


def product(own_half, before, tokens, token_spots, weights, weight_spots, rows, depth, name):
    width = weights[0].shape[-1]
    operands = [*tokens, *weights] + ([] if own_half else [before])
    return pl.pallas_call(
        functools.partial(product_kernel, own_half, len(tokens), len(weights), token_spots, weight_spots),
        out_shape=jax.ShapeDtypeStruct((rows, width), jnp.float32),
        in_specs=[HBM] * len(operands),
        out_specs=HBM,
        scratch_shapes=[
            pltpu.VMEM((2, rows, depth), jnp.bfloat16),
            pltpu.VMEM((2, depth, width), jnp.bfloat16),
            pltpu.VMEM((rows, width), jnp.float32),
            pltpu.SemaphoreType.DMA((2,)),
            pltpu.SemaphoreType.DMA((2,)),
            pltpu.SemaphoreType.DMA,
        ],
        compiler_params=pltpu.CompilerParams(vmem_limit_bytes=SCOPED),
        cost_estimate=FREE,
        name=name,
    )(*operands)


def finish_kernel(n_tok, n_wt, token_spots, weight_spots, *refs):
    tokens, weights = refs[:n_tok], refs[n_tok : n_tok + n_wt]
    inv, before, out, xbuf, wbuf, acc, xsem, wsem, asem = refs[n_tok + n_wt :]
    x = position()[0]
    start_weights(lax.rem(x + 2, 4), wbuf, weights, weight_spots, wsem)
    tiles = acc.shape[0] // TILE
    loads = []
    for i in range(tiles):
        spots = []
        for which, row, side, first, size in token_spots:
            low, high = max(row, i * TILE), min(row + size, (i + 1) * TILE)
            if low < high:
                spots.append((which, low, side, first + low - row, high - low))
        start_tokens(xbuf, tokens, spots, xsem.at[i])
        here = pl.ds(i * TILE, TILE)
        loads.append(pltpu.make_async_copy(before.at[here], acc.at[here], asem.at[i]))
        loads[i].start()
    wait_all(wbuf, wsem)
    for i in range(tiles):
        here = pl.ds(i * TILE, TILE)
        wait_all(xbuf.at[here], xsem.at[i])
        loads[i].wait()
        part = jnp.dot(xbuf[here], wbuf[...], preferred_element_type=jnp.float32)
        out[here] = silu((acc[here] + part) * inv[here]).astype(out.dtype)


def finish(tokens, token_spots, weights, weight_spots, inv, before, depth):
    rows, width = before.shape
    return pl.pallas_call(
        functools.partial(finish_kernel, len(tokens), len(weights), token_spots, weight_spots),
        out_shape=jax.ShapeDtypeStruct((rows, width), jnp.bfloat16),
        in_specs=[HBM] * (len(tokens) + len(weights)) + [VMEM, HBM],
        out_specs=VMEM,
        scratch_shapes=[
            pltpu.VMEM((rows, depth), jnp.bfloat16),
            pltpu.VMEM((depth, width), jnp.bfloat16),
            pltpu.VMEM((rows, width), jnp.float32),
            pltpu.SemaphoreType.DMA((rows // TILE,)),
            pltpu.SemaphoreType.DMA,
            pltpu.SemaphoreType.DMA((rows // TILE,)),
        ],
        compiler_params=pltpu.CompilerParams(vmem_limit_bytes=SCOPED),
        cost_estimate=FREE,
        name="product_rest",
    )(*tokens, *weights, inv, before)


def packed(square, columns):
    lead = lax.reduce_precision(square, 8, 7)
    fill = jnp.zeros((2 * columns - square.shape[0],), jnp.float32)
    flat = jnp.concatenate([lead, fill, square - lead, fill]).reshape(4, columns)
    return jnp.concatenate([flat, jnp.zeros((12, columns), jnp.float32)], axis=0).astype(jnp.bfloat16)


def local(tokens, gain, rollout_weight, delta_values, scale_exponents):
    count, features = tokens.shape
    total = features * 8
    block, width = rollout_weight.shape[0] // 16, rollout_weight.shape[1]
    base = rollout_weight.reshape(128, block // 8, width)
    n_a, n_b, n_c = 3 * count // 8, 3 * count // 8, count // 4
    at_b, at_c, extra = n_a, n_a + n_b, 16
    depth = 2 * features

    parts = scaled_delta(scale_exponents, delta_values)
    got = [parts[0]] + [shift(parts[j], x=j) for j in (1, 2, 3)]
    values = tokens.astype(jnp.float32)
    scaled = (values * gain[None, :]).astype(jnp.bfloat16)
    square = jnp.sum(values * values, axis=1)
    mine_a = jnp.concatenate([scaled[:n_a], packed(square, features)], axis=0)
    mine_b, mine_c = scaled[at_b:at_c], scaled[at_c:]
    mine_a, *_ = gate(mine_a, *parts)
    theirs_a = shift(mine_a, z_lo=1)

    got[1], got[2], got[3], mine_c = gate(got[1], got[2], got[3], mine_c)
    same = jnp.stack([g[0] for g in got])
    other = jnp.stack([g[1] for g in got])
    near, across = shift(other, z_lo=1), shift(other, z_lo=1, z_hi=1)
    left_c, right_c = shift(mine_c, x=1), shift(mine_c, x=-1)

    pair_a = jnp.concatenate([mine_a, theirs_a], axis=0)
    near, across, left_c, right_c, same_z, pair_a = gate(near, across, left_c, right_c, same, pair_a)
    left_a, right_a = shift(pair_a, x=1), shift(pair_a, x=-1)
    far = shift(same_z, z_hi=1)
    own = refresh(same, near, base, 0, "refresh_own")
    own_pair = [own, shift(own, core=1)]
    own_next = [shift(v, y_by_core=1) for v in own_pair]
    mine_bz, far = gate(mine_b, far)
    theirs_b = shift(mine_bz, z_lo=1)
    other_hi = refresh(far, across, base, 1, "refresh_far")
    far_pair = jnp.stack([other_hi, shift(other_hi, core=1)])

    left_a, right_a, *own_next, theirs_b = gate(left_a, right_a, *own_next, theirs_b)
    pair_b = jnp.concatenate([mine_b, theirs_b], axis=0)
    left_b, right_b = shift(pair_b, x=1), shift(pair_b, x=-1)
    far_next = shift(far_pair, y_by_core=1)
    own_opp = shift(own_next[0], y_by_core=1)
    theirs_c = shift(jnp.concatenate([mine_c, left_c, right_c], axis=0), z_lo=1)

    left_b, right_b, far_next, theirs_c, own_opp, *own_next = gate(
        left_b, right_b, far_next, theirs_c, own_opp, *own_next
    )
    up = shift(jnp.concatenate([left_a, theirs_c[n_c : 2 * n_c]], axis=0), x=1)
    down = shift(jnp.concatenate([right_b, right_c], axis=0), x=-1)
    far_opp = shift(far_next[0], y_by_core=1)
    far_swap = shift(far_next, core=1)
    own_swap = [shift(v, core=1) for v in own_next]

    tokens_all = [pair_a, left_a, right_a, pair_b, left_b, right_b, mine_c, left_c, right_c, theirs_c]
    token_spots = []
    for j in range(3):
        spots = [(j, 0, side, side * (n_a + extra), n_a) for side in (0, 1)]
        spots += [(3 + j, at_b, side, side * n_b, n_b) for side in (0, 1)]
        token_spots.append(spots + [(6 + j, at_c, 0, 0, n_c), (9, at_c, 1, j * n_c, n_c)])
    weights = [*own_pair, *own_next, *own_swap, far_pair, far_next, far_swap]
    weight_spots = []
    for k, (step, cores) in enumerate(((0, (0, 1)), (-1, (0, 1)), (1, (1, 0)))):
        for index in (0, 1):
            weight_spots.append((2 * k + index, None, step, cores[index], 0))
            weight_spots.append((6 + k, index, step, cores[index], 1))
    partial = product(True, None, tokens_all, token_spots, weights, weight_spots, count, depth, "product_own_half")

    own_opp, far_opp, partial, far_swap, *own_swap = gate(own_opp, far_opp, partial, far_swap, *own_swap)
    weights = [*own_pair, *own_next, *own_swap, far_pair, far_next, far_swap]
    weights += [own_opp, shift(own_opp, core=1), far_opp, shift(far_opp, core=1)]
    weight_spots += [(9 + 2 * hi + c, None, 2, c, hi) for hi in (0, 1) for c in (0, 1)]
    partial = product(
        False, partial, tokens_all, token_spots, weights, weight_spots, count, depth, "product_other_half"
    )

    partial, up = gate(partial, up)
    tail = sum(
        v[at : at + 4].astype(jnp.float32)
        for v in (pair_a, left_a, right_a, up)
        for at in (n_a, 2 * n_a + extra)
    ).reshape(2, 2 * features)
    inv = lax.rsqrt((tail[0] + tail[1])[:count] / total + 1e-06)[:, None]
    spots = [(0, 0, side, side * (n_a + extra), n_a) for side in (0, 1)]
    spots += [(1, at_b, side, side * n_b, n_b) for side in (0, 1)]
    spots += [(1, at_c, 0, 2 * n_b, n_c), (0, at_c, 1, 2 * (n_a + extra), n_c)]
    return finish([up, down], spots, weights, weight_spots, inv, partial, depth)


def solution(mesh):
    in_specs = (
        P("fsdp", "tp"),
        P("tp"),
        P(None, "tp"),
        P(("fsdp", "tp"), None),
        P(("fsdp", "tp"), None),
    )
    out_specs = P("fsdp", "tp")
    return jax.shard_map(local, mesh=mesh, in_specs=in_specs, out_specs=out_specs, check_vma=False)
```

time: 643 us -> 193 us (0.30)
  waiting for transfers between devices: 367 us -> 85.2 us
  local copies, waits for them, and re-layouts: 123 us -> 5.97 us
  Pallas kernels: 0 us -> 51.1 us
  blocking collectives: 45.3 us -> 0 us
  other arithmetic: 54.2 us -> 8.98 us
  starting transfers between devices: 10.2 us -> 40.9 us
  matrix products: 26.9 us -> 0 us
  between operations: 14.9 us -> 0.53 us
    all_to_all x2 -> x0, waiting for transfers between devices: 228 us -> none  [the longest x1 228 us: local(): lax.all_to_all(gathered[0], 'tp', split_axis=1, concat_axis=0, tiled=True)]
    all_gather x2 -> x0, waiting for transfers between devices: 138 us -> none  [the longest x1 72.9 us: local(): whole = lax.all_gather(normed, 'tp', axis=1, tiled=True)]
    ppermute x0 -> x29, waiting for transfers between devices: none -> 85.2 us  [shift(): return lax.ppermute(value, ('fsdp', 'tp'), links(**step))]
    convert_element_type x2 -> x0, local copies, waits for them, and re-layouts: 56.4 us -> none  [refreshed_rows(): delta_rows.astype(jnp.float32) * wide]
    convert_element_type x3 -> x0, other arithmetic: 52 us -> none  [the longest x1 32.1 us: refreshed_rows(): (base_rows.astype(jnp.float32) + delta_rows.astype(jnp.float32) * wide).a...]
    pallas_call x0 -> x6, Pallas kernels: none -> 51.1 us  [the longest x2 28.6 us: product(): pl.pallas_call(functools.partial(product_kernel, own_half, len(tokens), l...]
    ppermute x0 -> x29, starting transfers between devices: none -> 40.9 us  [shift(): return lax.ppermute(value, ('fsdp', 'tp'), links(**step))]
    reshape x1, local copies, waits for them, and re-layouts: 33.3 us -> 0.02 us  [packed(): jnp.concatenate([lead, fill, square - lead, fill]).reshape(4, columns)]
  transfers between devices with their start and end apart: 4 -> 29, of which waited for: 3 -> 15; matrix products, arithmetic and copies ran while one was open for 28% -> 5% of each run, Pallas kernels for 0% -> 19%
where the time goes in v2:
time: 193 us
  waiting for transfers between devices  85.2 us (44%)
  Pallas kernels  51.1 us (26%)
  starting transfers between devices  40.9 us (21%)
  other arithmetic  8.98 us (5%)
  local copies, waits for them, and re-layouts  5.97 us (3%)
    ppermute x29, waiting for transfers between devices, shift(): return lax.ppermute(value, ('fsdp', 'tp'), links(**step))  85.2 us
    ppermute x29, starting transfers between devices, shift(): return lax.ppermute(value, ('fsdp', 'tp'), links(**step))  40.9 us
    pallas_call x2, Pallas kernels, product(): pl.pallas_call(functools.partial(product_kernel, own_half, len(tokens), l...  28.6 us
    pallas_call x1, Pallas kernels, finish(): pl.pallas_call(functools.partial(finish_kernel, len(tokens), len(weights)...  11.4 us
    pallas_call x2, Pallas kernels, refresh(): pl.pallas_call(functools.partial(refresh_kernel, other_hi), out_shape=jax...  7.66 us
    unnamed x54, local copies, waits for them, and re-layouts  4.53 us
  transfers between devices with their start and end apart: 29, of which 15 were waited for; matrix products, arithmetic and copies ran while one was open for 5% of the time, Pallas kernels for 19%

profile of v2, /device:TPU:1, one launch (start us, length us, event | category | flops | bytes accessed | tf_op | source)
XLA Modules:
  0.0 192.7 jit_solution(11530741849624360028)
XLA Ops:
  0.0 3.5 %scaled_delta.1 = (bf16[2,56,1152]{2,1,0:T(8,128)(2,1)}, bf16[2,56,1152]{2,1,0:T(8,128)(2,1)}, bf16[2,56,1152]{2,1,0:T(8,128)(2,1)}, bf16[2,56,1152]{2,1,0:T(8,128)(2,1)}) custom-call(s32[56,72]{1,0:T(8,128)} %exps.1, bf16[56,9216]{1,0:T(8,128)(2,1)} %delta.1), custom_call_target="tpu_custom_call" | custom-call | tf_op jit(solution)/shard_map/scaled_delta/pallas_call | solution.py:67
  13.3 6.0 %collective-permute-done.1 = bf16[2,56,1152]{2,1,0:T(8,128)(2,1)S(1)} collective-permute-done((bf16[2,56,1152]{2,1,0:T(8,128)(2,1)}, bf16[2,56,1152]{2,1,0:T(8,128)(2,1)S(1)}, u32[]{:S(2)}, u32[]{:S(2)}) %collective-permute-start.1) | collective-permute-done | bytes 258080 | tf_op jit(solution)/shard_map/ppermute | solution.py:27
  29.2 6.1 %collective-permute-done.5.refs_7_ = bf16[256,896]{1,0:T(8,128)(2,1)S(1)} collective-permute-done((bf16[256,896]{1,0:T(8,128)(2,1)S(1)}, bf16[256,896]{1,0:T(8,128)(2,1)S(1)}, u32[]{:S(2)}, u32[]{:S(2)}) %collective-permute-start.5) | collective-permute-done | bytes 458784 | tf_op jit(solution)/shard_map/ppermute | solution.py:27
  35.3 3.7 %collective-permute-done.3.other = bf16[4,56,1152]{2,1,0:T(8,128)(2,1)S(1)} collective-permute-done((bf16[4,56,1152]{2,1,0:T(8,128)(2,1)S(1)}, bf16[4,56,1152]{2,1,0:T(8,128)(2,1)S(1)}, u32[]{:S(2)}, u32[]{:S(2)}) %collective-permute-start.3) | collective-permute-done | bytes 516128 | tf_op jit(solution)/shard_map/ppermute | solution.py:27
  39.0 3.3 %collective-permute-start.13 = (bf16[4,56,1152]{2,1,0:T(8,128)(2,1)S(1)}, bf16[4,56,1152]{2,1,0:T(8,128)(2,1)}, u32[]{:S(2)}, u32[]{:S(2)}) collective-permute-start(bf16[4,56,1152]{2,1,0:T(8,128)(2,1)S(1)} %pad_maximum_fusion.7.same), channel_id=1, source_target_pairs={{0,64},{1,65},{2,66},{3,67},{4,68},{5,69},{6,70},{7,71},{8,72},{9,... | collective-permute-start | bytes 1548296 | tf_op jit(solution)/shard_map/ppermute | solution.py:27
  42.3 3.8 %refresh_own.1 = bf16[8,56,1152]{2,1,0:T(8,128)(2,1)} custom-call(bf16[4,56,1152]{2,1,0:T(8,128)(2,1)} %copy-done.23, bf16[4,56,1152]{2,1,0:T(8,128)(2,1)} %copy-done.25, bf16[128,56,1152]{2,1,0:T(8,128)(2,1)} %bitcast.8), custom_call_target="tpu_custom_call" | custom-call | tf_op jit(solution)/shard_map/refresh_own/pallas_call | solution.py:93
  46.2 2.8 %collective-permute-start.11 = (bf16[448,1152]{1,0:T(8,128)(2,1)}, bf16[448,1152]{1,0:T(8,128)(2,1)}, u32[]{:S(2)}, u32[]{:S(2)}) collective-permute-start(bf16[448,1152]{1,0:T(8,128)(2,1)} %bitcast.10), channel_id=1, source_target_pairs={{0,8},{1,9},{2,10},{3,11},{4,12},{5,13},{6,14},{7,15},{8,0},{9,1},... | collective-permute-start | bytes 3096584 | tf_op jit(solution)/shard_map/ppermute | solution.py:27
  49.0 4.3 %collective-permute-done.13.same = bf16[4,56,1152]{2,1,0:T(8,128)(2,1)} collective-permute-done((bf16[4,56,1152]{2,1,0:T(8,128)(2,1)S(1)}, bf16[4,56,1152]{2,1,0:T(8,128)(2,1)}, u32[]{:S(2)}, u32[]{:S(2)}) %collective-permute-start.13) | collective-permute-done | bytes 516128 | tf_op jit(solution)/shard_map/ppermute | solution.py:27
  53.3 3.9 %refresh_far.1 = bf16[8,56,1152]{2,1,0:T(8,128)(2,1)} custom-call(bf16[4,56,1152]{2,1,0:T(8,128)(2,1)} %collective-permute-done.13.same, bf16[4,56,1152]{2,1,0:T(8,128)(2,1)} %copy-done.24, bf16[128,56,1152]{2,1,0:T(8,128)(2,1)} %bitcast.9), custom_call_target="tpu_custom_call" | custom-call | tf_op jit(solution)/shard_map/refresh_far/pallas_call | solution.py:93
  57.1 2.6 %collective-permute-start.17 = (bf16[448,1152]{1,0:T(8,128)(2,1)}, bf16[448,1152]{1,0:T(8,128)(2,1)S(1)}, u32[]{:S(2)}, u32[]{:S(2)}) collective-permute-start(bf16[448,1152]{1,0:T(8,128)(2,1)} %bitcast.15), channel_id=1, source_target_pairs={{0,8},{1,9},{2,10},{3,11},{4,12},{5,13},{6,14},{7,15},{8,0},{9,1},... | collective-permute-start | bytes 3096584 | tf_op jit(solution)/shard_map/ppermute | solution.py:27
  59.7 2.7 %collective-permute-start.10 = (bf16[448,1152]{1,0:T(8,128)(2,1)S(1)}, bf16[448,1152]{1,0:T(8,128)(2,1)S(1)}, u32[]{:S(2)}, u32[]{:S(2)}) collective-permute-start(bf16[448,1152]{1,0:T(8,128)(2,1)S(1)} %bitcast.14), channel_id=1, source_target_pairs={{0,16},{1,17},{2,18},{3,19},{4,20},{5,21},{6,22},{7,23},{8,56},{9,... | collective-permute-start | bytes 3096584 | tf_op jit(solution)/shard_map/ppermute | solution.py:27
  67.5 6.5 %collective-permute-done.10.refs_12_.refs_4_ = bf16[448,1152]{1,0:T(8,128)(2,1)S(1)} collective-permute-done((bf16[448,1152]{1,0:T(8,128)(2,1)S(1)}, bf16[448,1152]{1,0:T(8,128)(2,1)S(1)}, u32[]{:S(2)}, u32[]{:S(2)}) %collective-permute-start.10) | collective-permute-done | bytes 1032224 | tf_op jit(solution)/shard_map/ppermute | solution.py:27
  74.0 3.4 %collective-permute-start.18 = (bf16[2,448,1152]{2,1,0:T(8,128)(2,1)S(1)}, bf16[2,448,1152]{2,1,0:T(8,128)(2,1)S(1)}, u32[]{:S(2)}, u32[]{:S(2)}) collective-permute-start(bf16[2,448,1152]{2,1,0:T(8,128)(2,1)S(1)} %pad_maximum_fusion.refs_16_.refs_8_), channel_id=1, source_target_pairs={{0,16},{1,17},{2,18},{3,19},{4,20},{5,21},{6,22},{7,23},{8,56},{9,... | collective-permute-start | bytes 6193160 | tf_op jit(solution)/shard_map/ppermute | solution.py:27
  77.5 4.4 %collective-permute-done.14 = bf16[384,896]{1,0:T(8,128)(2,1)S(1)} collective-permute-done((bf16[384,896]{1,0:T(8,128)(2,1)S(1)}, bf16[384,896]{1,0:T(8,128)(2,1)S(1)}, u32[]{:S(2)}, u32[]{:S(2)}) %collective-permute-start.14) | collective-permute-done | bytes 688160 | tf_op jit(solution)/shard_map/ppermute | solution.py:27
  82.4 14.3 %collective-permute-done.8.refs_1_ = bf16[800,896]{1,0:T(8,128)(2,1)S(1)} collective-permute-done((bf16[800,896]{1,0:T(8,128)(2,1)}, bf16[800,896]{1,0:T(8,128)(2,1)S(1)}, u32[]{:S(2)}, u32[]{:S(2)}) %collective-permute-start.8) | collective-permute-done | bytes 1433632 | tf_op jit(solution)/shard_map/ppermute | solution.py:27
  96.9 3.0 %collective-permute-start.16 = (bf16[768,896]{1,0:T(8,128)(2,1)S(1)}, bf16[768,896]{1,0:T(8,128)(2,1)S(1)}, u32[]{:S(2)}, u32[]{:S(2)}) collective-permute-start(bf16[768,896]{1,0:T(8,128)(2,1)S(1)} %pad_maximum_fusion.4.refs_3_), channel_id=1, source_target_pairs={{0,6},{1,7},{2,0},{3,1},{4,2},{5,3},{6,4},{7,5},{8,14},{9,15},{10,... | collective-permute-start | bytes 4128776 | tf_op jit(solution)/shard_map/ppermute | solution.py:27
  100.3 11.8 %collective-permute-done.19.refs_9_ = bf16[768,896]{1,0:T(8,128)(2,1)S(1)} collective-permute-done((bf16[768,896]{1,0:T(8,128)(2,1)S(1)}, bf16[768,896]{1,0:T(8,128)(2,1)S(1)}, u32[]{:S(2)}, u32[]{:S(2)}) %collective-permute-start.19) | collective-permute-done | bytes 1376288 | tf_op jit(solution)/shard_map/ppermute | solution.py:27
  112.2 6.1 %collective-permute-done.20.refs_19_.refs_11_ = bf16[448,1152]{1,0:T(8,128)(2,1)S(1)} collective-permute-done((bf16[448,1152]{1,0:T(8,128)(2,1)S(1)}, bf16[448,1152]{1,0:T(8,128)(2,1)S(1)}, u32[]{:S(2)}, u32[]{:S(2)}) %collective-permute-start.20) | collective-permute-done | bytes 1032224 | tf_op jit(solution)/shard_map/ppermute | solution.py:27
  118.2 12.1 %collective-permute-done.15.refs_4_ = bf16[768,896]{1,0:T(8,128)(2,1)S(1)} collective-permute-done((bf16[768,896]{1,0:T(8,128)(2,1)S(1)}, bf16[768,896]{1,0:T(8,128)(2,1)S(1)}, u32[]{:S(2)}, u32[]{:S(2)}) %collective-permute-start.15) | collective-permute-done | bytes 1376288 | tf_op jit(solution)/shard_map/ppermute | solution.py:27
  141.3 10.9 %product_own_half.1.refs_23_ = f32[1024,1152]{1,0:T(8,128)} custom-call(bf16[800,896]{1,0:T(8,128)(2,1)} %pad_maximum_fusion.3.refs_0_, bf16[800,896]{1,0:T(8,128)(2,1)} %copy-done.4, bf16[800,896]{1,0:T(8,128)(2,1)} %copy-done.15, bf16[768,896]{1,0:T(8,128)(2,1)} %copy-done.6, bf16[768,896]{1,0:T(8,128)(2,1)} %copy-done.16, bf16[768,896]{1,0:T(8,128)(2,1)} %copy-done.5, ...), custom_call_target="tpu_custom_call" | custom-call | tf_op jit(solution)/shard_map/product_own_half/pallas_call | solution.py:201
  153.1 2.7 %collective-permute-done.25.refs_20_.refs_12_ = bf16[448,1152]{1,0:T(8,128)(2,1)S(1)} collective-permute-done((bf16[448,1152]{1,0:T(8,128)(2,1)S(1)}, bf16[448,1152]{1,0:T(8,128)(2,1)S(1)}, u32[]{:S(2)}, u32[]{:S(2)}) %collective-permute-start.25) | collective-permute-done | bytes 1032224 | tf_op jit(solution)/shard_map/ppermute | solution.py:27
  158.0 17.7 %product_other_half.1.refs_16_ = f32[1024,1152]{1,0:T(8,128)} custom-call(bf16[800,896]{1,0:T(8,128)(2,1)} %pad_maximum_fusion.3.refs_0_, bf16[800,896]{1,0:T(8,128)(2,1)} %copy-done.4, bf16[800,896]{1,0:T(8,128)(2,1)} %copy-done.15, bf16[768,896]{1,0:T(8,128)(2,1)} %copy-done.6, bf16[768,896]{1,0:T(8,128)(2,1)} %copy-done.16, bf16[768,896]{1,0:T(8,128)(2,1)} %copy-done.5, ...), custom_call_target="tpu_custom_call" | custom-call | tf_op jit(solution)/shard_map/product_other_half/pallas_call | solution.py:201
  175.7 3.5 %collective-permute-done.27.refs_0_ = bf16[1056,896]{1,0:T(8,128)(2,1)} collective-permute-done((bf16[1056,896]{1,0:T(8,128)(2,1)}, bf16[1056,896]{1,0:T(8,128)(2,1)}, u32[]{:S(2)}, u32[]{:S(2)}) %collective-permute-start.27) | collective-permute-done | bytes 1892384 | tf_op jit(solution)/shard_map/ppermute | solution.py:27
  181.1 11.4 %product_rest.1 = bf16[1024,1152]{1,0:T(8,128)(2,1)} custom-call(bf16[1056,896]{1,0:T(8,128)(2,1)} %collective-permute-done.27.refs_0_, bf16[1024,896]{1,0:T(8,128)(2,1)} %collective-permute-done.28.refs_1_, bf16[448,1152]{1,0:T(8,128)(2,1)} %bitcast.13, bf16[448,1152]{1,0:T(8,128)(2,1)} %collective-permute-done.11.refs_11_.refs_3_, ...), custom_call_target="tpu_custom_call" | custom-call | tf_op jit(solution)/shard_map/product_rest/pallas_call | solution.py:248
  (120 shorter events, 41.7 us)
Async XLA Ops:
  3.5 9.8 %collective-permute-start = (bf16[2,56,1152]{2,1,0:T(8,128)(2,1)}, bf16[2,56,1152]{2,1,0:T(8,128)(2,1)S(1)}, u32[]{:S(2)}, u32[]{:S(2)}) collective-permute-start(bf16[2,56,1152]{2,1,0:T(8,128)(2,1)} %get-tuple-element.43), channel_id=1, source_target_pairs={{0,2},{1,3},{2,4},{3,5},{4,6},{5,7},{6,0},{7,1},{8,10},{9,11},{10,... | collective-permute-start | bytes 774152 | tf_op jit(solution)/shard_map/ppermute | solution.py:27
  5.5 13.8 %collective-permute-start.1 = (bf16[2,56,1152]{2,1,0:T(8,128)(2,1)}, bf16[2,56,1152]{2,1,0:T(8,128)(2,1)S(1)}, u32[]{:S(2)}, u32[]{:S(2)}) collective-permute-start(bf16[2,56,1152]{2,1,0:T(8,128)(2,1)} %get-tuple-element.44), channel_id=1, source_target_pairs={{0,4},{1,5},{2,6},{3,7},{4,0},{5,1},{6,2},{7,3},{8,12},{9,13},{10,... | collective-permute-start | bytes 774152 | tf_op jit(solution)/shard_map/ppermute | solution.py:27
  8.0 11.4 %collective-permute-start.2 = (bf16[2,56,1152]{2,1,0:T(8,128)(2,1)}, bf16[2,56,1152]{2,1,0:T(8,128)(2,1)S(1)}, u32[]{:S(2)}, u32[]{:S(2)}) collective-permute-start(bf16[2,56,1152]{2,1,0:T(8,128)(2,1)} %get-tuple-element.45), channel_id=1, source_target_pairs={{0,6},{1,7},{2,0},{3,1},{4,2},{5,3},{6,4},{7,5},{8,14},{9,15},{10,... | collective-permute-start | bytes 774152 | tf_op jit(solution)/shard_map/ppermute | solution.py:27
  11.5 16.5 %collective-permute-start.7 = (bf16[400,896]{1,0:T(8,128)(2,1)S(1)}, bf16[400,896]{1,0:T(8,128)(2,1)S(1)}, u32[]{:S(2)}, u32[]{:S(2)}) collective-permute-start(bf16[400,896]{1,0:T(8,128)(2,1)S(1)} %fusion.3), channel_id=1, source_target_pairs={{0,1},{1,0},{2,3},{3,2},{4,5},{5,4},{6,7},{7,6},{8,9},{9,8},{10,11... | collective-permute-start | bytes 2150408 | tf_op jit(solution)/shard_map/ppermute | solution.py:27
  19.5 19.5 %collective-permute-start.3 = (bf16[4,56,1152]{2,1,0:T(8,128)(2,1)S(1)}, bf16[4,56,1152]{2,1,0:T(8,128)(2,1)S(1)}, u32[]{:S(2)}, u32[]{:S(2)}) collective-permute-start(bf16[4,56,1152]{2,1,0:T(8,128)(2,1)S(1)} %pad_maximum_fusion.6), channel_id=1, source_target_pairs={{0,1},{1,0},{2,3},{3,2},{4,5},{5,4},{6,7},{7,6},{8,9},{9,8},{10,11... | collective-permute-start | bytes 1548296 | tf_op jit(solution)/shard_map/ppermute | solution.py:27
  21.2 17.8 %collective-permute-start.4 = (bf16[4,56,1152]{2,1,0:T(8,128)(2,1)S(1)}, bf16[4,56,1152]{2,1,0:T(8,128)(2,1)S(1)}, u32[]{:S(2)}, u32[]{:S(2)}) collective-permute-start(bf16[4,56,1152]{2,1,0:T(8,128)(2,1)S(1)} %pad_maximum_fusion.6), channel_id=1, source_target_pairs={{0,65},{1,64},{2,67},{3,66},{4,69},{5,68},{6,71},{7,70},{8,73},{9,... | collective-permute-start | bytes 1548296 | tf_op jit(solution)/shard_map/ppermute | solution.py:27
  23.5 11.8 %collective-permute-start.5 = (bf16[256,896]{1,0:T(8,128)(2,1)S(1)}, bf16[256,896]{1,0:T(8,128)(2,1)S(1)}, u32[]{:S(2)}, u32[]{:S(2)}) collective-permute-start(bf16[256,896]{1,0:T(8,128)(2,1)S(1)} %slice.98.refs_6_), channel_id=1, source_target_pairs={{0,2},{1,3},{2,4},{3,5},{4,6},{5,7},{6,0},{7,1},{8,10},{9,11},{10,... | collective-permute-start | bytes 1376264 | tf_op jit(solution)/shard_map/ppermute | solution.py:27
  24.8 10.5 %collective-permute-start.6 = (bf16[256,896]{1,0:T(8,128)(2,1)S(1)}, bf16[256,896]{1,0:T(8,128)(2,1)S(1)}, u32[]{:S(2)}, u32[]{:S(2)}) collective-permute-start(bf16[256,896]{1,0:T(8,128)(2,1)S(1)} %slice.98.refs_6_), channel_id=1, source_target_pairs={{0,6},{1,7},{2,0},{3,1},{4,2},{5,3},{6,4},{7,5},{8,14},{9,15},{10,... | collective-permute-start | bytes 1376264 | tf_op jit(solution)/shard_map/ppermute | solution.py:27
  39.0 14.2 %collective-permute-start.13 = (bf16[4,56,1152]{2,1,0:T(8,128)(2,1)S(1)}, bf16[4,56,1152]{2,1,0:T(8,128)(2,1)}, u32[]{:S(2)}, u32[]{:S(2)}) collective-permute-start(bf16[4,56,1152]{2,1,0:T(8,128)(2,1)S(1)} %pad_maximum_fusion.7.same), channel_id=1, source_target_pairs={{0,64},{1,65},{2,66},{3,67},{4,68},{5,69},{6,70},{7,71},{8,72},{9,... | collective-permute-start | bytes 1548296 | tf_op jit(solution)/shard_map/ppermute | solution.py:27
  46.2 18.9 %collective-permute-start.11 = (bf16[448,1152]{1,0:T(8,128)(2,1)}, bf16[448,1152]{1,0:T(8,128)(2,1)}, u32[]{:S(2)}, u32[]{:S(2)}) collective-permute-start(bf16[448,1152]{1,0:T(8,128)(2,1)} %bitcast.10), channel_id=1, source_target_pairs={{0,8},{1,9},{2,10},{3,11},{4,12},{5,13},{6,14},{7,15},{8,0},{9,1},... | collective-permute-start | bytes 3096584 | tf_op jit(solution)/shard_map/ppermute | solution.py:27
  59.7 14.3 %collective-permute-start.10 = (bf16[448,1152]{1,0:T(8,128)(2,1)S(1)}, bf16[448,1152]{1,0:T(8,128)(2,1)S(1)}, u32[]{:S(2)}, u32[]{:S(2)}) collective-permute-start(bf16[448,1152]{1,0:T(8,128)(2,1)S(1)} %bitcast.14), channel_id=1, source_target_pairs={{0,16},{1,17},{2,18},{3,19},{4,20},{5,21},{6,22},{7,23},{8,56},{9,... | collective-permute-start | bytes 3096584 | tf_op jit(solution)/shard_map/ppermute | solution.py:27
  62.4 34.2 %collective-permute-start.8 = (bf16[800,896]{1,0:T(8,128)(2,1)}, bf16[800,896]{1,0:T(8,128)(2,1)S(1)}, u32[]{:S(2)}, u32[]{:S(2)}) collective-permute-start(bf16[800,896]{1,0:T(8,128)(2,1)} %pad_maximum_fusion.3.refs_0_), channel_id=1, source_target_pairs={{0,2},{1,3},{2,4},{3,5},{4,6},{5,7},{6,0},{7,1},{8,10},{9,11},{10,... | collective-permute-start | bytes 4300808 | tf_op jit(solution)/shard_map/ppermute | solution.py:27
  62.7 33.9 %collective-permute-start.9 = (bf16[800,896]{1,0:T(8,128)(2,1)}, bf16[800,896]{1,0:T(8,128)(2,1)S(1)}, u32[]{:S(2)}, u32[]{:S(2)}) collective-permute-start(bf16[800,896]{1,0:T(8,128)(2,1)} %pad_maximum_fusion.3.refs_0_), channel_id=1, source_target_pairs={{0,6},{1,7},{2,0},{3,1},{4,2},{5,3},{6,4},{7,5},{8,14},{9,15},{10,... | collective-permute-start | bytes 4300808 | tf_op jit(solution)/shard_map/ppermute | solution.py:27
  65.1 31.6 %collective-permute-start.12 = (bf16[448,1152]{1,0:T(8,128)(2,1)}, bf16[448,1152]{1,0:T(8,128)(2,1)S(1)}, u32[]{:S(2)}, u32[]{:S(2)}) collective-permute-start(bf16[448,1152]{1,0:T(8,128)(2,1)} %collective-permute-done.11.refs_11_.refs_3_), channel_id=1, source_target_pairs={{0,16},{1,17},{2,18},{3,19},{4,20},{5,21},{6,22},{7,23},{8,56},{9,... | collective-permute-start | bytes 3096584 | tf_op jit(solution)/shard_map/ppermute | solution.py:27
  65.6 16.4 %collective-permute-start.14 = (bf16[384,896]{1,0:T(8,128)(2,1)S(1)}, bf16[384,896]{1,0:T(8,128)(2,1)S(1)}, u32[]{:S(2)}, u32[]{:S(2)}) collective-permute-start(bf16[384,896]{1,0:T(8,128)(2,1)S(1)} %get-tuple-element.54), channel_id=1, source_target_pairs={{0,1},{1,0},{2,3},{3,2},{4,5},{5,4},{6,7},{7,6},{8,9},{9,8},{10,11... | collective-permute-start | bytes 2064392 | tf_op jit(solution)/shard_map/ppermute | solution.py:27
  74.0 56.3 %collective-permute-start.18 = (bf16[2,448,1152]{2,1,0:T(8,128)(2,1)S(1)}, bf16[2,448,1152]{2,1,0:T(8,128)(2,1)S(1)}, u32[]{:S(2)}, u32[]{:S(2)}) collective-permute-start(bf16[2,448,1152]{2,1,0:T(8,128)(2,1)S(1)} %pad_maximum_fusion.refs_16_.refs_8_), channel_id=1, source_target_pairs={{0,16},{1,17},{2,18},{3,19},{4,20},{5,21},{6,22},{7,23},{8,56},{9,... | collective-permute-start | bytes 6193160 | tf_op jit(solution)/shard_map/ppermute | solution.py:27
  82.0 30.2 %collective-permute-start.19 = (bf16[768,896]{1,0:T(8,128)(2,1)S(1)}, bf16[768,896]{1,0:T(8,128)(2,1)S(1)}, u32[]{:S(2)}, u32[]{:S(2)}) collective-permute-start(bf16[768,896]{1,0:T(8,128)(2,1)S(1)} %pad_maximum_fusion.5), channel_id=1, source_target_pairs={{0,1},{1,0},{2,3},{3,2},{4,5},{5,4},{6,7},{7,6},{8,9},{9,8},{10,11... | collective-permute-start | bytes 4128776 | tf_op jit(solution)/shard_map/ppermute | solution.py:27
  96.8 33.5 %collective-permute-start.15 = (bf16[768,896]{1,0:T(8,128)(2,1)S(1)}, bf16[768,896]{1,0:T(8,128)(2,1)S(1)}, u32[]{:S(2)}, u32[]{:S(2)}) collective-permute-start(bf16[768,896]{1,0:T(8,128)(2,1)S(1)} %pad_maximum_fusion.4.refs_3_), channel_id=1, source_target_pairs={{0,2},{1,3},{2,4},{3,5},{4,6},{5,7},{6,0},{7,1},{8,10},{9,11},{10,... | collective-permute-start | bytes 4128776 | tf_op jit(solution)/shard_map/ppermute | solution.py:27
  96.9 33.4 %collective-permute-start.16 = (bf16[768,896]{1,0:T(8,128)(2,1)S(1)}, bf16[768,896]{1,0:T(8,128)(2,1)S(1)}, u32[]{:S(2)}, u32[]{:S(2)}) collective-permute-start(bf16[768,896]{1,0:T(8,128)(2,1)S(1)} %pad_maximum_fusion.4.refs_3_), channel_id=1, source_target_pairs={{0,6},{1,7},{2,0},{3,1},{4,2},{5,3},{6,4},{7,5},{8,14},{9,15},{10,... | collective-permute-start | bytes 4128776 | tf_op jit(solution)/shard_map/ppermute | solution.py:27
  99.9 18.3 %collective-permute-start.20 = (bf16[448,1152]{1,0:T(8,128)(2,1)S(1)}, bf16[448,1152]{1,0:T(8,128)(2,1)S(1)}, u32[]{:S(2)}, u32[]{:S(2)}) collective-permute-start(bf16[448,1152]{1,0:T(8,128)(2,1)S(1)} %collective-permute-done.10.refs_12_.refs_4_), channel_id=1, source_target_pairs={{0,16},{1,17},{2,18},{3,19},{4,20},{5,21},{6,22},{7,23},{8,56},{9,... | collective-permute-start | bytes 3096584 | tf_op jit(solution)/shard_map/ppermute | solution.py:27
  131.5 8.5 %collective-permute-start.24 = (bf16[2,448,1152]{2,1,0:T(8,128)(2,1)S(1)}, bf16[2,448,1152]{2,1,0:T(8,128)(2,1)S(1)}, u32[]{:S(2)}, u32[]{:S(2)}) collective-permute-start(bf16[2,448,1152]{2,1,0:T(8,128)(2,1)S(1)} %collective-permute-done.18.refs_17_.refs_9_), channel_id=1, source_target_pairs={{0,8},{1,9},{2,10},{3,11},{4,12},{5,13},{6,14},{7,15},{8,0},{9,1},... | collective-permute-start | bytes 6193160 | tf_op jit(solution)/shard_map/ppermute | solution.py:27
  132.2 20.0 %collective-permute-start.21 = (bf16[448,1152]{1,0:T(8,128)(2,1)S(1)}, bf16[448,1152]{1,0:T(8,128)(2,1)}, u32[]{:S(2)}, u32[]{:S(2)}) collective-permute-start(bf16[448,1152]{1,0:T(8,128)(2,1)S(1)} %slice_bitcast_fusion), channel_id=1, source_target_pairs={{0,16},{1,17},{2,18},{3,19},{4,20},{5,21},{6,22},{7,23},{8,56},{9,... | collective-permute-start | bytes 3096584 | tf_op jit(solution)/shard_map/ppermute | solution.py:27
  134.8 44.4 %collective-permute-start.27 = (bf16[1056,896]{1,0:T(8,128)(2,1)}, bf16[1056,896]{1,0:T(8,128)(2,1)}, u32[]{:S(2)}, u32[]{:S(2)}) collective-permute-start(bf16[1056,896]{1,0:T(8,128)(2,1)} %pad_maximum_fusion.1), channel_id=1, source_target_pairs={{0,2},{1,3},{2,4},{3,5},{4,6},{5,7},{6,0},{7,1},{8,10},{9,11},{10,... | collective-permute-start | bytes 5677064 | tf_op jit(solution)/shard_map/ppermute | solution.py:27
  137.4 43.8 %collective-permute-start.28 = (bf16[1024,896]{1,0:T(8,128)(2,1)}, bf16[1024,896]{1,0:T(8,128)(2,1)}, u32[]{:S(2)}, u32[]{:S(2)}) collective-permute-start(bf16[1024,896]{1,0:T(8,128)(2,1)} %pad_maximum_fusion.2), channel_id=1, source_target_pairs={{0,6},{1,7},{2,0},{3,1},{4,2},{5,3},{6,4},{7,5},{8,14},{9,15},{10,... | collective-permute-start | bytes 5505032 | tf_op jit(solution)/shard_map/ppermute | solution.py:27
  (32 other events, 489.2 us)

commit v3 on v2

--- a/solution.py
+++ b/solution.py
@@ -12,12 +12,11 @@
 FREE = pl.CostEstimate(flops=0, bytes_accessed=0, transcendentals=0)
 
 
-def links(x=0, z_lo=0, z_hi=0, y_by_core=0, core=0):
+def links(x=0, z_lo=0, z_hi=0, y=0, core=0):
     pairs = []
     for f in range(16):
         for t in range(8):
-            along = y_by_core if f % 2 == 0 else -y_by_core
-            f2 = (((f // 8) + z_hi) % 2) * 8 + (((f // 2) % 4 + along) % 4) * 2 + (f + core) % 2
+            f2 = (((f // 8) + z_hi) % 2) * 8 + (((f // 2) % 4 + y) % 4) * 2 + (f + core) % 2
             t2 = ((t // 2 + x) % 4) * 2 + (t + z_lo) % 2
             pairs.append((f * 8 + t, f2 * 8 + t2))
     return pairs
@@ -120,15 +119,14 @@
 def start_weights(block, held, pieces, spots, sem):
     _, _, y, z_hi, core = position()
     piece = held.shape[0] // 4
-    for which, index, step, other_core, other_hi in spots:
-        y2 = lax.rem(y + jnp.where(core == 0, step, -step) + 4, 4)
+    for which, step, other_core, other_hi in spots:
+        y2 = lax.rem(y + step + 4, 4)
         part = lax.rem(y2, 2) * 2 + lax.rem(core + other_core, 2)
 
         @pl.when(lax.rem(z_hi + other_hi, 2) * 2 + y2 // 2 == block)
-        def _(which=which, index=index, part=part):
-            source = pieces[which] if index is None else pieces[which].at[index]
+        def _(which=which, part=part):
             target = held.at[pl.ds(pl.multiple_of(part * piece, 16), piece)]
-            pltpu.make_async_copy(source, target, sem).start()
+            pltpu.make_async_copy(pieces[which], target, sem).start()
 
 
 def start_tokens(held, pieces, spots, sem):
@@ -144,76 +142,55 @@
     pltpu.make_async_copy(held, held, sem).wait()
 
 
-def product_kernel(own_half, n_tok, n_wt, token_spots, weight_spots, *refs):
+def product_kernel(n_tok, n_wt, token_spots, weight_spots, *refs):
     tokens, weights = refs[:n_tok], refs[n_tok : n_tok + n_wt]
-    before = None if own_half else refs[n_tok + n_wt]
-    out, xbuf, wbuf, acc, xsem, wsem, asem = refs[n_tok + n_wt + (0 if own_half else 1) :]
-    x, _, y, _, _ = position()
-    blocks = [2 * k + (y // 2 if own_half else 1 - y // 2) for k in range(2)]
-    wanted = [block != lax.rem(x + 2, 4) for block in blocks]
-    if not own_half:
-        load = pltpu.make_async_copy(before, acc, asem)
-        load.start()
-    for k in range(2):
-
-        @pl.when(wanted[k])
-        def _(k=k):
-            start_weights(blocks[k], wbuf.at[k], weights, weight_spots, wsem.at[k])
-
-        for j in range(3):
-
-            @pl.when(blocks[k] == lax.rem(x + STEPS[j] + 4, 4))
-            def _(k=k, j=j):
-                start_tokens(xbuf.at[k], tokens, token_spots[j], xsem.at[k])
-
-    if not own_half:
-        load.wait()
-    else:
-
-        @pl.when(jnp.logical_not(wanted[0]))
-        def _():
-            acc[...] = jnp.zeros_like(acc)
-
-    for k in range(2):
-
-        @pl.when(wanted[k])
-        def _(k=k):
-            wait_all(xbuf.at[k], xsem.at[k])
-            wait_all(wbuf.at[k], wsem.at[k])
-
-            @pl.loop(0, acc.shape[0] // TILE)
-            def _(i):
-                here = pl.ds(pl.multiple_of(i * TILE, TILE), TILE)
-                part = jnp.dot(xbuf[k, here], wbuf[k], preferred_element_type=jnp.float32)
-                if k == 0 and own_half:
-                    acc[here] = part
-                else:
-                    acc[here] += part
+    out, xbuf, wbuf, acc, xsem, wsem, asem = refs[n_tok + n_wt :]
+    x = position()[0]
+
+    def start(j):
+        start_weights(lax.rem(x + STEPS[j] + 4, 4), wbuf.at[j], weights, weight_spots, wsem.at[j])
+        start_tokens(xbuf.at[j], tokens, token_spots[j], xsem.at[j])
+
+    start(0)
+    for j in range(3):
+        wait_all(xbuf.at[j], xsem.at[j])
+        wait_all(wbuf.at[j], wsem.at[j])
+        if j < 2:
+            start(j + 1)
+
+        @pl.loop(0, acc.shape[0] // TILE)
+        def _(i, j=j):
+            here = pl.ds(pl.multiple_of(i * TILE, TILE), TILE)
+            part = jnp.dot(xbuf[j, here], wbuf[j], preferred_element_type=jnp.float32)
+            if j == 0:
+                acc[here] = part
+            else:
+                acc[here] += part
 
     store = pltpu.make_async_copy(acc, out, asem)
     store.start()
     store.wait()
 
 
-def product(own_half, before, tokens, token_spots, weights, weight_spots, rows, depth, name):
+def product(tokens, token_spots, weights, weight_spots, rows, depth):
     width = weights[0].shape[-1]
-    operands = [*tokens, *weights] + ([] if own_half else [before])
+    operands = [*tokens, *weights]
     return pl.pallas_call(
-        functools.partial(product_kernel, own_half, len(tokens), len(weights), token_spots, weight_spots),
+        functools.partial(product_kernel, len(tokens), len(weights), token_spots, weight_spots),
         out_shape=jax.ShapeDtypeStruct((rows, width), jnp.float32),
         in_specs=[HBM] * len(operands),
         out_specs=HBM,
         scratch_shapes=[
-            pltpu.VMEM((2, rows, depth), jnp.bfloat16),
-            pltpu.VMEM((2, depth, width), jnp.bfloat16),
+            pltpu.VMEM((3, rows, depth), jnp.bfloat16),
+            pltpu.VMEM((3, depth, width), jnp.bfloat16),
             pltpu.VMEM((rows, width), jnp.float32),
-            pltpu.SemaphoreType.DMA((2,)),
-            pltpu.SemaphoreType.DMA((2,)),
+            pltpu.SemaphoreType.DMA((3,)),
+            pltpu.SemaphoreType.DMA((3,)),
             pltpu.SemaphoreType.DMA,
         ],
         compiler_params=pltpu.CompilerParams(vmem_limit_bytes=SCOPED),
         cost_estimate=FREE,
-        name=name,
+        name="product_most",
     )(*operands)
 
 
@@ -276,7 +253,7 @@
     total = features * 8
     block, width = rollout_weight.shape[0] // 16, rollout_weight.shape[1]
     base = rollout_weight.reshape(128, block // 8, width)
-    n_a, n_b, n_c = 3 * count // 8, 3 * count // 8, count // 4
+    n_a, n_b, n_c = count // 4, 7 * count // 16, 5 * count // 16
     at_b, at_c, extra = n_a, n_a + n_b, 16
     depth = 2 * features
 
@@ -301,28 +278,29 @@
     left_a, right_a = shift(pair_a, x=1), shift(pair_a, x=-1)
     far = shift(same_z, z_hi=1)
     own = refresh(same, near, base, 0, "refresh_own")
-    own_pair = [own, shift(own, core=1)]
-    own_next = [shift(v, y_by_core=1) for v in own_pair]
+    own_l, own_r = shift(own, y=1), shift(own, y=-1)
     mine_bz, far = gate(mine_b, far)
     theirs_b = shift(mine_bz, z_lo=1)
     other_hi = refresh(far, across, base, 1, "refresh_far")
-    far_pair = jnp.stack([other_hi, shift(other_hi, core=1)])
-
-    left_a, right_a, *own_next, theirs_b = gate(left_a, right_a, *own_next, theirs_b)
+
+    left_a, right_a, own_l, own_r, right_c = gate(left_a, right_a, own_l, own_r, right_c)
+    opposite_a, opposite_c = shift(left_a, x=1), shift(right_c, x=-1)
+    far_l, far_r = shift(other_hi, y=1), shift(other_hi, y=-1)
     pair_b = jnp.concatenate([mine_b, theirs_b], axis=0)
     left_b, right_b = shift(pair_b, x=1), shift(pair_b, x=-1)
-    far_next = shift(far_pair, y_by_core=1)
-    own_opp = shift(own_next[0], y_by_core=1)
-    theirs_c = shift(jnp.concatenate([mine_c, left_c, right_c], axis=0), z_lo=1)
-
-    left_b, right_b, far_next, theirs_c, own_opp, *own_next = gate(
-        left_b, right_b, far_next, theirs_c, own_opp, *own_next
+    three_c, theirs_b = gate(jnp.concatenate([mine_c, left_c, right_c], axis=0), theirs_b)
+    theirs_c = shift(three_c, z_lo=1)
+    own_lf, far_l, far_r = gate(own_l, far_l, far_r)
+    own_o, far_o = shift(own_lf, y=1), shift(far_r, y=-1)
+    rings = [own, own_l, own_r, other_hi, far_l, far_r]
+    swaps = [shift(v, core=1) for v in rings]
+
+    left_b, right_b, theirs_c, own_o, far_o, opposite_a, opposite_c = gate(
+        left_b, right_b, theirs_c, own_o, far_o, opposite_a, opposite_c
     )
-    up = shift(jnp.concatenate([left_a, theirs_c[n_c : 2 * n_c]], axis=0), x=1)
-    down = shift(jnp.concatenate([right_b, right_c], axis=0), x=-1)
-    far_opp = shift(far_next[0], y_by_core=1)
-    far_swap = shift(far_next, core=1)
-    own_swap = [shift(v, core=1) for v in own_next]
+    cut = (2 * n_b - n_c) // 32 * 16
+    up = shift(jnp.concatenate([theirs_c[n_c : 2 * n_c], left_b[:cut]], axis=0), x=1)
+    down = shift(right_b[cut:], x=-1)
 
     tokens_all = [pair_a, left_a, right_a, pair_b, left_b, right_b, mine_c, left_c, right_c, theirs_c]
     token_spots = []
@@ -330,33 +308,21 @@
         spots = [(j, 0, side, side * (n_a + extra), n_a) for side in (0, 1)]
         spots += [(3 + j, at_b, side, side * n_b, n_b) for side in (0, 1)]
         token_spots.append(spots + [(6 + j, at_c, 0, 0, n_c), (9, at_c, 1, j * n_c, n_c)])
-    weights = [*own_pair, *own_next, *own_swap, far_pair, far_next, far_swap]
-    weight_spots = []
-    for k, (step, cores) in enumerate(((0, (0, 1)), (-1, (0, 1)), (1, (1, 0)))):
-        for index in (0, 1):
-            weight_spots.append((2 * k + index, None, step, cores[index], 0))
-            weight_spots.append((6 + k, index, step, cores[index], 1))
-    partial = product(True, None, tokens_all, token_spots, weights, weight_spots, count, depth, "product_own_half")
-
-    own_opp, far_opp, partial, far_swap, *own_swap = gate(own_opp, far_opp, partial, far_swap, *own_swap)
-    weights = [*own_pair, *own_next, *own_swap, far_pair, far_next, far_swap]
-    weights += [own_opp, shift(own_opp, core=1), far_opp, shift(far_opp, core=1)]
-    weight_spots += [(9 + 2 * hi + c, None, 2, c, hi) for hi in (0, 1) for c in (0, 1)]
-    partial = product(
-        False, partial, tokens_all, token_spots, weights, weight_spots, count, depth, "product_other_half"
-    )
-
-    partial, up = gate(partial, up)
+    weights = [*rings, *swaps, own_o, far_o, shift(own_o, core=1), shift(far_o, core=1)]
+    weight_spots = [(6 * c + 3 * hi + k, STEPS[k], c, hi) for c in (0, 1) for hi in (0, 1) for k in range(3)]
+    weight_spots += [(12 + 2 * c + hi, 2, c, hi) for c in (0, 1) for hi in (0, 1)]
+    partial = product(tokens_all, token_spots, weights, weight_spots, count, depth)
+
     tail = sum(
         v[at : at + 4].astype(jnp.float32)
-        for v in (pair_a, left_a, right_a, up)
+        for v in (pair_a, left_a, right_a, opposite_a)
         for at in (n_a, 2 * n_a + extra)
     ).reshape(2, 2 * features)
     inv = lax.rsqrt((tail[0] + tail[1])[:count] / total + 1e-06)[:, None]
     spots = [(0, 0, side, side * (n_a + extra), n_a) for side in (0, 1)]
-    spots += [(1, at_b, side, side * n_b, n_b) for side in (0, 1)]
-    spots += [(1, at_c, 0, 2 * n_b, n_c), (0, at_c, 1, 2 * (n_a + extra), n_c)]
-    return finish([up, down], spots, weights, weight_spots, inv, partial, depth)
+    spots += [(1, at_c, 0, 0, n_c), (2, at_c, 1, 0, n_c)]
+    spots += [(2, at_b, 0, n_c, cut), (3, at_b + cut, 0, 0, n_b - cut), (3, at_b, 1, n_b - cut, n_b)]
+    return finish([opposite_a, opposite_c, up, down], spots, weights, weight_spots, inv, partial, depth)
 
 
 def solution(mesh):

time: 193 us -> 176 us (0.912)
  waiting for transfers between devices: 85.2 us -> 65.9 us
  starting transfers between devices: 40.9 us -> 53.2 us
  Pallas kernels: 51.1 us -> 44.3 us
    ppermute x29 -> x33, waiting for transfers between devices: 85.2 us -> 65.9 us  [shift(): return lax.ppermute(value, ('fsdp', 'tp'), links(**step))]
    ppermute x29 -> x33, starting transfers between devices: 40.9 us -> 53.2 us  [shift(): return lax.ppermute(value, ('fsdp', 'tp'), links(**step))]
    pallas_call x2 -> x1, Pallas kernels: 28.6 us -> 21.8 us  [product(): pl.pallas_call(functools.partial(product_kernel, len(tokens), len(weights...]
    unnamed x54 -> x42, local copies, waits for them, and re-layouts: 4.53 us -> 1.4 us
  transfers between devices with their start and end apart: 29 -> 33, of which waited for: 15 -> 13; matrix products, arithmetic and copies ran while one was open for 5% -> 6% of each run, Pallas kernels for 19% -> 17%
where the time goes in v3:
time: 176 us
  waiting for transfers between devices  65.9 us (37%)
  starting transfers between devices  53.2 us (30%)
  Pallas kernels  44.3 us (25%)
  other arithmetic  7.6 us (4%)
  local copies, waits for them, and re-layouts  4.26 us (2%)
    ppermute x33, waiting for transfers between devices, shift(): return lax.ppermute(value, ('fsdp', 'tp'), links(**step))  65.9 us
    ppermute x33, starting transfers between devices, shift(): return lax.ppermute(value, ('fsdp', 'tp'), links(**step))  53.2 us
    pallas_call x1, Pallas kernels, product(): pl.pallas_call(functools.partial(product_kernel, len(tokens), len(weights...  21.8 us
    pallas_call x1, Pallas kernels, finish(): pl.pallas_call(functools.partial(finish_kernel, len(tokens), len(weights)...  11.4 us
    pallas_call x2, Pallas kernels, refresh(): pl.pallas_call(functools.partial(refresh_kernel, other_hi), out_shape=jax...  7.57 us
  transfers between devices with their start and end apart: 33, of which 13 were waited for; matrix products, arithmetic and copies ran while one was open for 6% of the time, Pallas kernels for 17%

profile of v3, /device:TPU:1, one launch (start us, length us, event | category | flops | bytes accessed | tf_op | source)
XLA Modules:
  0.0 175.7 jit_solution(16234022559825062775)
XLA Ops:
  0.0 3.5 %scaled_delta.1 = (bf16[2,56,1152]{2,1,0:T(8,128)(2,1)}, bf16[2,56,1152]{2,1,0:T(8,128)(2,1)}, bf16[2,56,1152]{2,1,0:T(8,128)(2,1)}, bf16[2,56,1152]{2,1,0:T(8,128)(2,1)}) custom-call(s32[56,72]{1,0:T(8,128)} %exps.1, bf16[56,9216]{1,0:T(8,128)(2,1)} %delta.1), custom_call_target="tpu_custom_call" | custom-call | tf_op jit(solution)/shard_map/scaled_delta/pallas_call | solution.py:66
  5.5 2.5 %collective-permute-start.1 = (bf16[2,56,1152]{2,1,0:T(8,128)(2,1)}, bf16[2,56,1152]{2,1,0:T(8,128)(2,1)S(1)}, u32[]{:S(2)}, u32[]{:S(2)}) collective-permute-start(bf16[2,56,1152]{2,1,0:T(8,128)(2,1)} %get-tuple-element.40), channel_id=1, source_target_pairs={{0,4},{1,5},{2,6},{3,7},{4,0},{5,1},{6,2},{7,3},{8,12},{9,13},{10,... | collective-permute-start | bytes 774152 | tf_op jit(solution)/shard_map/ppermute | solution.py:26
  13.2 6.1 %collective-permute-done.1 = bf16[2,56,1152]{2,1,0:T(8,128)(2,1)S(1)} collective-permute-done((bf16[2,56,1152]{2,1,0:T(8,128)(2,1)}, bf16[2,56,1152]{2,1,0:T(8,128)(2,1)S(1)}, u32[]{:S(2)}, u32[]{:S(2)}) %collective-permute-start.1) | collective-permute-done | bytes 258080 | tf_op jit(solution)/shard_map/ppermute | solution.py:26
  24.3 2.2 %collective-permute-start.4 = (bf16[4,56,1152]{2,1,0:T(8,128)(2,1)S(1)}, bf16[4,56,1152]{2,1,0:T(8,128)(2,1)S(1)}, u32[]{:S(2)}, u32[]{:S(2)}) collective-permute-start(bf16[4,56,1152]{2,1,0:T(8,128)(2,1)S(1)} %pad_maximum_fusion.4), channel_id=1, source_target_pairs={{0,65},{1,64},{2,67},{3,66},{4,69},{5,68},{6,71},{7,70},{8,73},{9,... | collective-permute-start | bytes 1548296 | tf_op jit(solution)/shard_map/ppermute | solution.py:26
  28.4 6.1 %collective-permute-done.3.other = bf16[4,56,1152]{2,1,0:T(8,128)(2,1)S(1)} collective-permute-done((bf16[4,56,1152]{2,1,0:T(8,128)(2,1)S(1)}, bf16[4,56,1152]{2,1,0:T(8,128)(2,1)S(1)}, u32[]{:S(2)}, u32[]{:S(2)}) %collective-permute-start.3) | collective-permute-done | bytes 516128 | tf_op jit(solution)/shard_map/ppermute | solution.py:26
  37.5 2.7 %collective-permute-start.13 = (bf16[544,896]{1,0:T(8,128)(2,1)}, bf16[544,896]{1,0:T(8,128)(2,1)}, u32[]{:S(2)}, u32[]{:S(2)}) collective-permute-start(bf16[544,896]{1,0:T(8,128)(2,1)} %pad_maximum_fusion.3.refs_0_), channel_id=1, source_target_pairs={{0,6},{1,7},{2,0},{3,1},{4,2},{5,3},{6,4},{7,5},{8,14},{9,15},{10,... | collective-permute-start | bytes 2924552 | tf_op jit(solution)/shard_map/ppermute | solution.py:26
  42.4 3.8 %refresh_own.1 = bf16[8,56,1152]{2,1,0:T(8,128)(2,1)} custom-call(bf16[4,56,1152]{2,1,0:T(8,128)(2,1)} %pad_maximum_fusion.5.same, bf16[4,56,1152]{2,1,0:T(8,128)(2,1)} %copy-done.19, bf16[128,56,1152]{2,1,0:T(8,128)(2,1)} %bitcast.4), custom_call_target="tpu_custom_call" | custom-call | tf_op jit(solution)/shard_map/refresh_own/pallas_call | solution.py:92
  49.1 2.6 %collective-permute-done.8.same = bf16[4,56,1152]{2,1,0:T(8,128)(2,1)} collective-permute-done((bf16[4,56,1152]{2,1,0:T(8,128)(2,1)}, bf16[4,56,1152]{2,1,0:T(8,128)(2,1)}, u32[]{:S(2)}, u32[]{:S(2)}) %collective-permute-start.8) | collective-permute-done | bytes 516128 | tf_op jit(solution)/shard_map/ppermute | solution.py:26
  51.8 3.8 %refresh_far.1 = bf16[8,56,1152]{2,1,0:T(8,128)(2,1)} custom-call(bf16[4,56,1152]{2,1,0:T(8,128)(2,1)} %collective-permute-done.8.same, bf16[4,56,1152]{2,1,0:T(8,128)(2,1)} %copy-done.18, bf16[128,56,1152]{2,1,0:T(8,128)(2,1)} %bitcast.5), custom_call_target="tpu_custom_call" | custom-call | tf_op jit(solution)/shard_map/refresh_far/pallas_call | solution.py:92
  56.9 2.2 %collective-permute-done.12.refs_1_ = bf16[544,896]{1,0:T(8,128)(2,1)} collective-permute-done((bf16[544,896]{1,0:T(8,128)(2,1)}, bf16[544,896]{1,0:T(8,128)(2,1)}, u32[]{:S(2)}, u32[]{:S(2)}) %collective-permute-start.12) | collective-permute-done | bytes 974880 | tf_op jit(solution)/shard_map/ppermute | solution.py:26
  59.2 2.7 %collective-permute-start.18 = (bf16[448,1152]{1,0:T(8,128)(2,1)}, bf16[448,1152]{1,0:T(8,128)(2,1)}, u32[]{:S(2)}, u32[]{:S(2)}) collective-permute-start(bf16[448,1152]{1,0:T(8,128)(2,1)} %bitcast.12), channel_id=1, source_target_pairs={{0,48},{1,49},{2,50},{3,51},{4,52},{5,53},{6,54},{7,55},{8,56},{9,... | collective-permute-start | bytes 3096584 | tf_op jit(solution)/shard_map/ppermute | solution.py:26
  63.0 5.5 %collective-permute-done.14.refs_11_.refs_5_ = bf16[448,1152]{1,0:T(8,128)(2,1)} collective-permute-done((bf16[448,1152]{1,0:T(8,128)(2,1)}, bf16[448,1152]{1,0:T(8,128)(2,1)}, u32[]{:S(2)}, u32[]{:S(2)}) %collective-permute-start.14) | collective-permute-done | bytes 1032224 | tf_op jit(solution)/shard_map/ppermute | solution.py:26
  68.5 2.7 %collective-permute-start.22 = (bf16[320,896]{1,0:T(8,128)(2,1)}, bf16[320,896]{1,0:T(8,128)(2,1)}, u32[]{:S(2)}, u32[]{:S(2)}) collective-permute-start(bf16[320,896]{1,0:T(8,128)(2,1)} %collective-permute-done.6.refs_8_), channel_id=1, source_target_pairs={{0,6},{1,7},{2,0},{3,1},{4,2},{5,3},{6,4},{7,5},{8,14},{9,15},{10,... | collective-permute-start | bytes 1720328 | tf_op jit(solution)/shard_map/ppermute | solution.py:26
  72.4 4.8 %collective-permute-done.9 = bf16[448,896]{1,0:T(8,128)(2,1)S(1)} collective-permute-done((bf16[448,896]{1,0:T(8,128)(2,1)S(1)}, bf16[448,896]{1,0:T(8,128)(2,1)S(1)}, u32[]{:S(2)}, u32[]{:S(2)}) %collective-permute-start.9) | collective-permute-done | bytes 802848 | tf_op jit(solution)/shard_map/ppermute | solution.py:26
  78.9 11.6 %collective-permute-done.17.refs_14_.refs_8_ = bf16[448,1152]{1,0:T(8,128)(2,1)S(1)} collective-permute-done((bf16[448,1152]{1,0:T(8,128)(2,1)}, bf16[448,1152]{1,0:T(8,128)(2,1)S(1)}, u32[]{:S(2)}, u32[]{:S(2)}) %collective-permute-start.17) | collective-permute-done | bytes 1032224 | tf_op jit(solution)/shard_map/ppermute | solution.py:26
  90.5 2.7 %collective-permute-start.11 = (bf16[896,896]{1,0:T(8,128)(2,1)S(1)}, bf16[896,896]{1,0:T(8,128)(2,1)S(1)}, u32[]{:S(2)}, u32[]{:S(2)}) collective-permute-start(bf16[896,896]{1,0:T(8,128)(2,1)S(1)} %pad_maximum_fusion.1.refs_3_), channel_id=1, source_target_pairs={{0,6},{1,7},{2,0},{3,1},{4,2},{5,3},{6,4},{7,5},{8,14},{9,15},{10,... | collective-permute-start | bytes 4816904 | tf_op jit(solution)/shard_map/ppermute | solution.py:26
  93.3 2.6 %collective-permute-start.20 = (bf16[448,1152]{1,0:T(8,128)(2,1)}, bf16[448,1152]{1,0:T(8,128)(2,1)}, u32[]{:S(2)}, u32[]{:S(2)}) collective-permute-start(bf16[448,1152]{1,0:T(8,128)(2,1)} %collective-permute-done.18.refs_15_.refs_9_), channel_id=1, source_target_pairs={{0,48},{1,49},{2,50},{3,51},{4,52},{5,53},{6,54},{7,55},{8,56},{9,... | collective-permute-start | bytes 3096584 | tf_op jit(solution)/shard_map/ppermute | solution.py:26
  95.9 17.9 %collective-permute-done.19.refs_22_.refs_16_ = bf16[448,1152]{1,0:T(8,128)(2,1)S(1)} collective-permute-done((bf16[448,1152]{1,0:T(8,128)(2,1)}, bf16[448,1152]{1,0:T(8,128)(2,1)S(1)}, u32[]{:S(2)}, u32[]{:S(2)}) %collective-permute-start.19) | collective-permute-done | bytes 1032224 | tf_op jit(solution)/shard_map/ppermute | solution.py:26
  113.8 6.0 %collective-permute-start.25 = (bf16[448,1152]{1,0:T(8,128)(2,1)S(1)}, bf16[448,1152]{1,0:T(8,128)(2,1)S(1)}, u32[]{:S(2)}, u32[]{:S(2)}) collective-permute-start(bf16[448,1152]{1,0:T(8,128)(2,1)S(1)} %bitcast.10), channel_id=1, source_target_pairs={{0,8},{1,9},{2,10},{3,11},{4,12},{5,13},{6,14},{7,15},{8,0},{9,1},... | collective-permute-start | bytes 3096584 | tf_op jit(solution)/shard_map/ppermute | solution.py:26
  120.0 3.8 %collective-permute-done.10.refs_4_ = bf16[896,896]{1,0:T(8,128)(2,1)S(1)} collective-permute-done((bf16[896,896]{1,0:T(8,128)(2,1)S(1)}, bf16[896,896]{1,0:T(8,128)(2,1)S(1)}, u32[]{:S(2)}, u32[]{:S(2)}) %collective-permute-start.10) | collective-permute-done | bytes 1605664 | tf_op jit(solution)/shard_map/ppermute | solution.py:26
  123.8 5.5 %collective-permute-start.26 = (bf16[448,1152]{1,0:T(8,128)(2,1)}, bf16[448,1152]{1,0:T(8,128)(2,1)S(1)}, u32[]{:S(2)}, u32[]{:S(2)}) collective-permute-start(bf16[448,1152]{1,0:T(8,128)(2,1)} %collective-permute-done.14.refs_11_.refs_5_), channel_id=1, source_target_pairs={{0,8},{1,9},{2,10},{3,11},{4,12},{5,13},{6,14},{7,15},{8,0},{9,1},... | collective-permute-start | bytes 3096584 | tf_op jit(solution)/shard_map/ppermute | solution.py:26
  132.5 2.7 %collective-permute-start.24 = (bf16[608,896]{1,0:T(8,128)(2,1)}, bf16[608,896]{1,0:T(8,128)(2,1)}, u32[]{:S(2)}, u32[]{:S(2)}) collective-permute-start(bf16[608,896]{1,0:T(8,128)(2,1)} %slice.90), channel_id=1, source_target_pairs={{0,6},{1,7},{2,0},{3,1},{4,2},{5,3},{6,4},{7,5},{8,14},{9,15},{10,... | collective-permute-start | bytes 3268616 | tf_op jit(solution)/shard_map/ppermute | solution.py:26
  142.3 21.8 %product_most.1.refs_21_ = f32[1024,1152]{1,0:T(8,128)} custom-call(bf16[544,896]{1,0:T(8,128)(2,1)} %pad_maximum_fusion.3.refs_0_, bf16[544,896]{1,0:T(8,128)(2,1)} %collective-permute-done.12.refs_1_, bf16[544,896]{1,0:T(8,128)(2,1)} %collective-permute-done.13.refs_2_, bf16[896,896]{1,0:T(8,128)(2,1)} %copy-done.2, bf16[896,896]{1,0:T(8,128)(2,1)} %copy-done.15, ...), custom_call_target="tpu_custom_call" | custom-call | tf_op jit(solution)/shard_map/product_most/pallas_call | solution.py:178
  164.1 11.4 %product_rest.1 = bf16[1024,1152]{1,0:T(8,128)(2,1)} custom-call(bf16[544,896]{1,0:T(8,128)(2,1)} %copy-done.17, bf16[320,896]{1,0:T(8,128)(2,1)} %collective-permute-done.22.refs_1_, bf16[608,896]{1,0:T(8,128)(2,1)} %collective-permute-done.23.refs_2_, bf16[608,896]{1,0:T(8,128)(2,1)} %collective-permute-done.24.refs_3_, bf16[448,1152]{1,0:T(8,128)(2,1)} %bitcast.9, ...), custom_call_target="tpu_custom_call" | custom-call | tf_op jit(solution)/shard_map/product_rest/pallas_call | solution.py:225
  (115 shorter events, 37.9 us)
Async XLA Ops:
  5.5 13.8 %collective-permute-start.1 = (bf16[2,56,1152]{2,1,0:T(8,128)(2,1)}, bf16[2,56,1152]{2,1,0:T(8,128)(2,1)S(1)}, u32[]{:S(2)}, u32[]{:S(2)}) collective-permute-start(bf16[2,56,1152]{2,1,0:T(8,128)(2,1)} %get-tuple-element.40), channel_id=1, source_target_pairs={{0,4},{1,5},{2,6},{3,7},{4,0},{5,1},{6,2},{7,3},{8,12},{9,13},{10,... | collective-permute-start | bytes 774152 | tf_op jit(solution)/shard_map/ppermute | solution.py:26
  11.4 16.0 %collective-permute-start.7 = (bf16[272,896]{1,0:T(8,128)(2,1)S(1)}, bf16[272,896]{1,0:T(8,128)(2,1)S(1)}, u32[]{:S(2)}, u32[]{:S(2)}) collective-permute-start(bf16[272,896]{1,0:T(8,128)(2,1)S(1)} %fusion.3), channel_id=1, source_target_pairs={{0,1},{1,0},{2,3},{3,2},{4,5},{5,4},{6,7},{7,6},{8,9},{9,8},{10,11... | collective-permute-start | bytes 1462280 | tf_op jit(solution)/shard_map/ppermute | solution.py:26
  19.3 17.4 %collective-permute-start.5 = (bf16[320,896]{1,0:T(8,128)(2,1)S(1)}, bf16[320,896]{1,0:T(8,128)(2,1)S(1)}, u32[]{:S(2)}, u32[]{:S(2)}) collective-permute-start(bf16[320,896]{1,0:T(8,128)(2,1)S(1)} %slice.103.refs_6_), channel_id=1, source_target_pairs={{0,2},{1,3},{2,4},{3,5},{4,6},{5,7},{6,0},{7,1},{8,10},{9,11},{10,... | collective-permute-start | bytes 1720328 | tf_op jit(solution)/shard_map/ppermute | solution.py:26
  20.3 16.4 %collective-permute-start.6 = (bf16[320,896]{1,0:T(8,128)(2,1)S(1)}, bf16[320,896]{1,0:T(8,128)(2,1)}, u32[]{:S(2)}, u32[]{:S(2)}) collective-permute-start(bf16[320,896]{1,0:T(8,128)(2,1)S(1)} %slice.103.refs_6_), channel_id=1, source_target_pairs={{0,6},{1,7},{2,0},{3,1},{4,2},{5,3},{6,4},{7,5},{8,14},{9,15},{10,... | collective-permute-start | bytes 1720328 | tf_op jit(solution)/shard_map/ppermute | solution.py:26
  22.4 12.2 %collective-permute-start.3 = (bf16[4,56,1152]{2,1,0:T(8,128)(2,1)S(1)}, bf16[4,56,1152]{2,1,0:T(8,128)(2,1)S(1)}, u32[]{:S(2)}, u32[]{:S(2)}) collective-permute-start(bf16[4,56,1152]{2,1,0:T(8,128)(2,1)S(1)} %pad_maximum_fusion.4), channel_id=1, source_target_pairs={{0,1},{1,0},{2,3},{3,2},{4,5},{5,4},{6,7},{7,6},{8,9},{9,8},{10,11... | collective-permute-start | bytes 1548296 | tf_op jit(solution)/shard_map/ppermute | solution.py:26
  24.3 12.4 %collective-permute-start.4 = (bf16[4,56,1152]{2,1,0:T(8,128)(2,1)S(1)}, bf16[4,56,1152]{2,1,0:T(8,128)(2,1)S(1)}, u32[]{:S(2)}, u32[]{:S(2)}) collective-permute-start(bf16[4,56,1152]{2,1,0:T(8,128)(2,1)S(1)} %pad_maximum_fusion.4), channel_id=1, source_target_pairs={{0,65},{1,64},{2,67},{3,66},{4,69},{5,68},{6,71},{7,70},{8,73},{9,... | collective-permute-start | bytes 1548296 | tf_op jit(solution)/shard_map/ppermute | solution.py:26
  37.5 21.6 %collective-permute-start.12 = (bf16[544,896]{1,0:T(8,128)(2,1)}, bf16[544,896]{1,0:T(8,128)(2,1)}, u32[]{:S(2)}, u32[]{:S(2)}) collective-permute-start(bf16[544,896]{1,0:T(8,128)(2,1)} %pad_maximum_fusion.3.refs_0_), channel_id=1, source_target_pairs={{0,2},{1,3},{2,4},{3,5},{4,6},{5,7},{6,0},{7,1},{8,10},{9,11},{10,... | collective-permute-start | bytes 2924552 | tf_op jit(solution)/shard_map/ppermute | solution.py:26
  37.5 24.4 %collective-permute-start.13 = (bf16[544,896]{1,0:T(8,128)(2,1)}, bf16[544,896]{1,0:T(8,128)(2,1)}, u32[]{:S(2)}, u32[]{:S(2)}) collective-permute-start(bf16[544,896]{1,0:T(8,128)(2,1)} %pad_maximum_fusion.3.refs_0_), channel_id=1, source_target_pairs={{0,6},{1,7},{2,0},{3,1},{4,2},{5,3},{6,4},{7,5},{8,14},{9,15},{10,... | collective-permute-start | bytes 2924552 | tf_op jit(solution)/shard_map/ppermute | solution.py:26
  46.2 22.3 %collective-permute-start.14 = (bf16[448,1152]{1,0:T(8,128)(2,1)}, bf16[448,1152]{1,0:T(8,128)(2,1)}, u32[]{:S(2)}, u32[]{:S(2)}) collective-permute-start(bf16[448,1152]{1,0:T(8,128)(2,1)} %bitcast.6), channel_id=1, source_target_pairs={{0,16},{1,17},{2,18},{3,19},{4,20},{5,21},{6,22},{7,23},{8,24},{9,... | collective-permute-start | bytes 3096584 | tf_op jit(solution)/shard_map/ppermute | solution.py:26
  47.5 21.0 %collective-permute-start.15 = (bf16[448,1152]{1,0:T(8,128)(2,1)}, bf16[448,1152]{1,0:T(8,128)(2,1)}, u32[]{:S(2)}, u32[]{:S(2)}) collective-permute-start(bf16[448,1152]{1,0:T(8,128)(2,1)} %bitcast.7), channel_id=1, source_target_pairs={{0,48},{1,49},{2,50},{3,51},{4,52},{5,53},{6,54},{7,55},{8,56},{9,... | collective-permute-start | bytes 3096584 | tf_op jit(solution)/shard_map/ppermute | solution.py:26
  55.6 34.9 %collective-permute-start.17 = (bf16[448,1152]{1,0:T(8,128)(2,1)}, bf16[448,1152]{1,0:T(8,128)(2,1)S(1)}, u32[]{:S(2)}, u32[]{:S(2)}) collective-permute-start(bf16[448,1152]{1,0:T(8,128)(2,1)} %bitcast.11), channel_id=1, source_target_pairs={{0,16},{1,17},{2,18},{3,19},{4,20},{5,21},{6,22},{7,23},{8,24},{9,... | collective-permute-start | bytes 3096584 | tf_op jit(solution)/shard_map/ppermute | solution.py:26
  59.2 31.4 %collective-permute-start.18 = (bf16[448,1152]{1,0:T(8,128)(2,1)}, bf16[448,1152]{1,0:T(8,128)(2,1)}, u32[]{:S(2)}, u32[]{:S(2)}) collective-permute-start(bf16[448,1152]{1,0:T(8,128)(2,1)} %bitcast.12), channel_id=1, source_target_pairs={{0,48},{1,49},{2,50},{3,51},{4,52},{5,53},{6,54},{7,55},{8,56},{9,... | collective-permute-start | bytes 3096584 | tf_op jit(solution)/shard_map/ppermute | solution.py:26
  61.9 15.3 %collective-permute-start.9 = (bf16[448,896]{1,0:T(8,128)(2,1)S(1)}, bf16[448,896]{1,0:T(8,128)(2,1)S(1)}, u32[]{:S(2)}, u32[]{:S(2)}) collective-permute-start(bf16[448,896]{1,0:T(8,128)(2,1)S(1)} %slice.102), channel_id=1, source_target_pairs={{0,1},{1,0},{2,3},{3,2},{4,5},{5,4},{6,7},{7,6},{8,9},{9,8},{10,11... | collective-permute-start | bytes 2408456 | tf_op jit(solution)/shard_map/ppermute | solution.py:26
  68.5 24.8 %collective-permute-start.21 = (bf16[544,896]{1,0:T(8,128)(2,1)}, bf16[544,896]{1,0:T(8,128)(2,1)S(1)}, u32[]{:S(2)}, u32[]{:S(2)}) collective-permute-start(bf16[544,896]{1,0:T(8,128)(2,1)} %collective-permute-done.12.refs_1_), channel_id=1, source_target_pairs={{0,2},{1,3},{2,4},{3,5},{4,6},{5,7},{6,0},{7,1},{8,10},{9,11},{10,... | collective-permute-start | bytes 2924552 | tf_op jit(solution)/shard_map/ppermute | solution.py:26
  68.5 24.7 %collective-permute-start.22 = (bf16[320,896]{1,0:T(8,128)(2,1)}, bf16[320,896]{1,0:T(8,128)(2,1)}, u32[]{:S(2)}, u32[]{:S(2)}) collective-permute-start(bf16[320,896]{1,0:T(8,128)(2,1)} %collective-permute-done.6.refs_8_), channel_id=1, source_target_pairs={{0,6},{1,7},{2,0},{3,1},{4,2},{5,3},{6,4},{7,5},{8,14},{9,15},{10,... | collective-permute-start | bytes 1720328 | tf_op jit(solution)/shard_map/ppermute | solution.py:26
  77.2 52.1 %collective-permute-start.16 = (bf16[960,896]{1,0:T(8,128)(2,1)S(1)}, bf16[960,896]{1,0:T(8,128)(2,1)S(1)}, u32[]{:S(2)}, u32[]{:S(2)}) collective-permute-start(bf16[960,896]{1,0:T(8,128)(2,1)S(1)} %pad_maximum_fusion), channel_id=1, source_target_pairs={{0,1},{1,0},{2,3},{3,2},{4,5},{5,4},{6,7},{7,6},{8,9},{9,8},{10,11... | collective-permute-start | bytes 5160968 | tf_op jit(solution)/shard_map/ppermute | solution.py:26
  90.5 33.3 %collective-permute-start.10 = (bf16[896,896]{1,0:T(8,128)(2,1)S(1)}, bf16[896,896]{1,0:T(8,128)(2,1)S(1)}, u32[]{:S(2)}, u32[]{:S(2)}) collective-permute-start(bf16[896,896]{1,0:T(8,128)(2,1)S(1)} %pad_maximum_fusion.1.refs_3_), channel_id=1, source_target_pairs={{0,2},{1,3},{2,4},{3,5},{4,6},{5,7},{6,0},{7,1},{8,10},{9,11},{10,... | collective-permute-start | bytes 4816904 | tf_op jit(solution)/shard_map/ppermute | solution.py:26
  90.5 38.7 %collective-permute-start.11 = (bf16[896,896]{1,0:T(8,128)(2,1)S(1)}, bf16[896,896]{1,0:T(8,128)(2,1)S(1)}, u32[]{:S(2)}, u32[]{:S(2)}) collective-permute-start(bf16[896,896]{1,0:T(8,128)(2,1)S(1)} %pad_maximum_fusion.1.refs_3_), channel_id=1, source_target_pairs={{0,6},{1,7},{2,0},{3,1},{4,2},{5,3},{6,4},{7,5},{8,14},{9,15},{10,... | collective-permute-start | bytes 4816904 | tf_op jit(solution)/shard_map/ppermute | solution.py:26
  93.2 20.6 %collective-permute-start.19 = (bf16[448,1152]{1,0:T(8,128)(2,1)}, bf16[448,1152]{1,0:T(8,128)(2,1)S(1)}, u32[]{:S(2)}, u32[]{:S(2)}) collective-permute-start(bf16[448,1152]{1,0:T(8,128)(2,1)} %collective-permute-done.14.refs_11_.refs_5_), channel_id=1, source_target_pairs={{0,16},{1,17},{2,18},{3,19},{4,20},{5,21},{6,22},{7,23},{8,24},{9,... | collective-permute-start | bytes 3096584 | tf_op jit(solution)/shard_map/ppermute | solution.py:26
  93.3 26.6 %collective-permute-start.20 = (bf16[448,1152]{1,0:T(8,128)(2,1)}, bf16[448,1152]{1,0:T(8,128)(2,1)}, u32[]{:S(2)}, u32[]{:S(2)}) collective-permute-start(bf16[448,1152]{1,0:T(8,128)(2,1)} %collective-permute-done.18.refs_15_.refs_9_), channel_id=1, source_target_pairs={{0,48},{1,49},{2,50},{3,51},{4,52},{5,53},{6,54},{7,55},{8,56},{9,... | collective-permute-start | bytes 3096584 | tf_op jit(solution)/shard_map/ppermute | solution.py:26
  113.8 18.7 %collective-permute-start.25 = (bf16[448,1152]{1,0:T(8,128)(2,1)S(1)}, bf16[448,1152]{1,0:T(8,128)(2,1)S(1)}, u32[]{:S(2)}, u32[]{:S(2)}) collective-permute-start(bf16[448,1152]{1,0:T(8,128)(2,1)S(1)} %bitcast.10), channel_id=1, source_target_pairs={{0,8},{1,9},{2,10},{3,11},{4,12},{5,13},{6,14},{7,15},{8,0},{9,1},... | collective-permute-start | bytes 3096584 | tf_op jit(solution)/shard_map/ppermute | solution.py:26
  119.9 12.6 %collective-permute-start.28 = (bf16[448,1152]{1,0:T(8,128)(2,1)S(1)}, bf16[448,1152]{1,0:T(8,128)(2,1)S(1)}, u32[]{:S(2)}, u32[]{:S(2)}) collective-permute-start(bf16[448,1152]{1,0:T(8,128)(2,1)S(1)} %bitcast.15), channel_id=1, source_target_pairs={{0,8},{1,9},{2,10},{3,11},{4,12},{5,13},{6,14},{7,15},{8,0},{9,1},... | collective-permute-start | bytes 3096584 | tf_op jit(solution)/shard_map/ppermute | solution.py:26
  132.5 31.6 %collective-permute-start.23 = (bf16[608,896]{1,0:T(8,128)(2,1)}, bf16[608,896]{1,0:T(8,128)(2,1)}, u32[]{:S(2)}, u32[]{:S(2)}) collective-permute-start(bf16[608,896]{1,0:T(8,128)(2,1)} %pad_maximum_fusion.2), channel_id=1, source_target_pairs={{0,2},{1,3},{2,4},{3,5},{4,6},{5,7},{6,0},{7,1},{8,10},{9,11},{10,... | collective-permute-start | bytes 3268616 | tf_op jit(solution)/shard_map/ppermute | solution.py:26
  132.5 31.6 %collective-permute-start.24 = (bf16[608,896]{1,0:T(8,128)(2,1)}, bf16[608,896]{1,0:T(8,128)(2,1)}, u32[]{:S(2)}, u32[]{:S(2)}) collective-permute-start(bf16[608,896]{1,0:T(8,128)(2,1)} %slice.90), channel_id=1, source_target_pairs={{0,6},{1,7},{2,0},{3,1},{4,2},{5,3},{6,4},{7,5},{8,14},{9,15},{10,... | collective-permute-start | bytes 3268616 | tf_op jit(solution)/shard_map/ppermute | solution.py:26
  (30 other events, 464.5 us)

commit v4 on v3

--- a/solution.py
+++ b/solution.py
@@ -38,26 +38,23 @@
     return total
 
 
-def scale_kernel(exps, delta, *outs):
-    groups = exps.shape[1]
+def scale_kernel(exps, delta, *refs):
+    outs, held, sems = refs[:4], refs[4], refs[5]
     scale = power_two(exps[...])
     x, z_lo, _, _, _ = position()
-    width = outs[0].shape[2]
-    per = width // 128
-    scaled = []
-    for owner in range(8):
-        columns = []
-        for g in range(per):
-            at = owner * per + g
-            piece = delta[:, at * 128 : (at + 1) * 128].astype(jnp.float32) * scale[:, at : at + 1]
-            columns.append(piece.astype(jnp.bfloat16))
-        block = jnp.concatenate(columns, axis=1)
-        j = lax.rem(owner // 2 - x + 4, 4)
-        half = jnp.where(z_lo == owner % 2, 0, 1)
-        for k in range(4):
-            @pl.when(j == k)
-            def _(k=k, block=block, half=half):
-                outs[k][half] = block
+    width = held.shape[2]
+    for g in range(exps.shape[1]):
+        piece = delta[:, g * 128 : (g + 1) * 128].astype(jnp.float32) * scale[:, g : g + 1]
+        owner, at = divmod(g * 128, width)
+        held[owner, :, at : at + 128] = piece.astype(jnp.bfloat16)
+    copies = []
+    for j in range(4):
+        for half in (0, 1):
+            owner = lax.rem(x + j, 4) * 2 + (z_lo if half == 0 else 1 - z_lo)
+            copies.append(pltpu.make_async_copy(held.at[owner], outs[j].at[half], sems.at[2 * j + half]))
+            copies[-1].start()
+    for copy in copies:
+        copy.wait()
 
 
 def scaled_delta(exps, delta):
@@ -67,7 +64,8 @@
         scale_kernel,
         out_shape=[jax.ShapeDtypeStruct((2, rows, width), jnp.bfloat16)] * 4,
         in_specs=[pl.BlockSpec(memory_space=pltpu.VMEM)] * 2,
-        out_specs=[pl.BlockSpec(memory_space=pltpu.VMEM)] * 4,
+        out_specs=[pl.BlockSpec(memory_space=pltpu.HBM)] * 4,
+        scratch_shapes=[pltpu.VMEM((8, rows, width), jnp.bfloat16), pltpu.SemaphoreType.DMA((8,))],
         compiler_params=pltpu.CompilerParams(vmem_limit_bytes=SCOPED),
         cost_estimate=FREE,
         name="scaled_delta",
@@ -196,7 +194,7 @@
 
 def finish_kernel(n_tok, n_wt, token_spots, weight_spots, *refs):
     tokens, weights = refs[:n_tok], refs[n_tok : n_tok + n_wt]
-    inv, before, out, xbuf, wbuf, acc, xsem, wsem, asem = refs[n_tok + n_wt :]
+    inv, before, out, xbuf, wbuf, acc, result, xsem, wsem, asem, osem = refs[n_tok + n_wt :]
     x = position()[0]
     start_weights(lax.rem(x + 2, 4), wbuf, weights, weight_spots, wsem)
     tiles = acc.shape[0] // TILE
@@ -212,12 +210,17 @@
         loads.append(pltpu.make_async_copy(before.at[here], acc.at[here], asem.at[i]))
         loads[i].start()
     wait_all(wbuf, wsem)
+    stores = []
     for i in range(tiles):
         here = pl.ds(i * TILE, TILE)
         wait_all(xbuf.at[here], xsem.at[i])
         loads[i].wait()
         part = jnp.dot(xbuf[here], wbuf[...], preferred_element_type=jnp.float32)
-        out[here] = silu((acc[here] + part) * inv[here]).astype(out.dtype)
+        result[here] = silu((acc[here] + part) * inv[here]).astype(out.dtype)
+        stores.append(pltpu.make_async_copy(result.at[here], out.at[here], osem.at[i]))
+        stores[i].start()
+    for store in stores:
+        store.wait()
 
 
 def finish(tokens, token_spots, weights, weight_spots, inv, before, depth):
@@ -226,13 +229,15 @@
         functools.partial(finish_kernel, len(tokens), len(weights), token_spots, weight_spots),
         out_shape=jax.ShapeDtypeStruct((rows, width), jnp.bfloat16),
         in_specs=[HBM] * (len(tokens) + len(weights)) + [VMEM, HBM],
-        out_specs=VMEM,
+        out_specs=HBM,
         scratch_shapes=[
             pltpu.VMEM((rows, depth), jnp.bfloat16),
             pltpu.VMEM((depth, width), jnp.bfloat16),
             pltpu.VMEM((rows, width), jnp.float32),
+            pltpu.VMEM((rows, width), jnp.bfloat16),
             pltpu.SemaphoreType.DMA((rows // TILE,)),
             pltpu.SemaphoreType.DMA,
+            pltpu.SemaphoreType.DMA((rows // TILE,)),
             pltpu.SemaphoreType.DMA((rows // TILE,)),
         ],
         compiler_params=pltpu.CompilerParams(vmem_limit_bytes=SCOPED),
@@ -283,10 +288,12 @@
     theirs_b = shift(mine_bz, z_lo=1)
     other_hi = refresh(far, across, base, 1, "refresh_far")
 
-    left_a, right_a, own_l, own_r, right_c = gate(left_a, right_a, own_l, own_r, right_c)
+    left_a, right_a, right_c = gate(left_a, right_a, right_c)
     opposite_a, opposite_c = shift(left_a, x=1), shift(right_c, x=-1)
+    other_hi, left_a, right_a, own_l, own_r = gate(other_hi, left_a, right_a, own_l, own_r)
     far_l, far_r = shift(other_hi, y=1), shift(other_hi, y=-1)
     pair_b = jnp.concatenate([mine_b, theirs_b], axis=0)
+    pair_b, opposite_a, opposite_c = gate(pair_b, opposite_a, opposite_c)
     left_b, right_b = shift(pair_b, x=1), shift(pair_b, x=-1)
     three_c, theirs_b = gate(jnp.concatenate([mine_c, left_c, right_c], axis=0), theirs_b)
     theirs_c = shift(three_c, z_lo=1)
@@ -295,8 +302,14 @@
     rings = [own, own_l, own_r, other_hi, far_l, far_r]
     swaps = [shift(v, core=1) for v in rings]
 
-    left_b, right_b, theirs_c, own_o, far_o, opposite_a, opposite_c = gate(
-        left_b, right_b, theirs_c, own_o, far_o, opposite_a, opposite_c
+    tail = sum(
+        v[at : at + 4].astype(jnp.float32)
+        for v in (pair_a, left_a, right_a, opposite_a)
+        for at in (n_a, 2 * n_a + extra)
+    ).reshape(2, 2 * features)
+    inv = lax.rsqrt((tail[0] + tail[1])[:count] / total + 1e-06)[:, None]
+    left_b, right_b, theirs_c, own_o, far_o, opposite_a, opposite_c, inv = gate(
+        left_b, right_b, theirs_c, own_o, far_o, opposite_a, opposite_c, inv
     )
     cut = (2 * n_b - n_c) // 32 * 16
     up = shift(jnp.concatenate([theirs_c[n_c : 2 * n_c], left_b[:cut]], axis=0), x=1)
@@ -313,12 +326,6 @@
     weight_spots += [(12 + 2 * c + hi, 2, c, hi) for c in (0, 1) for hi in (0, 1)]
     partial = product(tokens_all, token_spots, weights, weight_spots, count, depth)
 
-    tail = sum(
-        v[at : at + 4].astype(jnp.float32)
-        for v in (pair_a, left_a, right_a, opposite_a)
-        for at in (n_a, 2 * n_a + extra)
-    ).reshape(2, 2 * features)
-    inv = lax.rsqrt((tail[0] + tail[1])[:count] / total + 1e-06)[:, None]
     spots = [(0, 0, side, side * (n_a + extra), n_a) for side in (0, 1)]
     spots += [(1, at_c, 0, 0, n_c), (2, at_c, 1, 0, n_c)]
     spots += [(2, at_b, 0, n_c, cut), (3, at_b + cut, 0, 0, n_b - cut), (3, at_b, 1, n_b - cut, n_b)]

time: 176 us -> 170 us (0.966)
  starting transfers between devices: 53.2 us -> 45.9 us
  local copies, waits for them, and re-layouts: 4.26 us -> 9.68 us
  waiting for transfers between devices: 65.9 us -> 62.7 us
    ppermute x33, starting transfers between devices: 53.2 us -> 45.9 us  [shift(): return lax.ppermute(value, ('fsdp', 'tp'), links(**step))]
    unnamed x42 -> x40, local copies, waits for them, and re-layouts: 1.4 us -> 5.21 us
    ppermute x33, waiting for transfers between devices: 65.9 us -> 62.7 us  [shift(): return lax.ppermute(value, ('fsdp', 'tp'), links(**step))]
    slice x3, local copies, waits for them, and re-layouts: 0.09 us -> 2.14 us  [local(): same = jnp.stack([g[0] for g in got])]
  transfers between devices with their start and end apart: 33 -> 33, of which waited for: 13 -> 11; matrix products, arithmetic and copies ran while one was open for 6% -> 7% of each run, Pallas kernels for 17% -> 17%
where the time goes in v4:
time: 170 us
  waiting for transfers between devices  62.7 us (37%)
  starting transfers between devices  45.9 us (27%)
  Pallas kernels  43.2 us (25%)
  local copies, waits for them, and re-layouts  9.68 us (6%)
  other arithmetic  7.54 us (4%)
    ppermute x33, waiting for transfers between devices, shift(): return lax.ppermute(value, ('fsdp', 'tp'), links(**step))  62.7 us
    ppermute x33, starting transfers between devices, shift(): return lax.ppermute(value, ('fsdp', 'tp'), links(**step))  45.9 us
    pallas_call x1, Pallas kernels, product(): pl.pallas_call(functools.partial(product_kernel, len(tokens), len(weights...  21.8 us
    pallas_call x1, Pallas kernels, finish(): pl.pallas_call(functools.partial(finish_kernel, len(tokens), len(weights)...  10.9 us
    pallas_call x2, Pallas kernels, refresh(): pl.pallas_call(functools.partial(refresh_kernel, other_hi), out_shape=jax...  7.57 us
    unnamed x40, local copies, waits for them, and re-layouts  5.21 us
  transfers between devices with their start and end apart: 33, of which 11 were waited for; matrix products, arithmetic and copies ran while one was open for 7% of the time, Pallas kernels for 17%

profile of v4, /device:TPU:1, one launch (start us, length us, event | category | flops | bytes accessed | tf_op | source)
XLA Modules:
  0.0 169.5 jit_solution(1874843711966812215)
XLA Ops:
  0.0 3.0 %scaled_delta.1 = (bf16[2,56,1152]{2,1,0:T(8,128)(2,1)}, bf16[2,56,1152]{2,1,0:T(8,128)(2,1)}, bf16[2,56,1152]{2,1,0:T(8,128)(2,1)}, bf16[2,56,1152]{2,1,0:T(8,128)(2,1)}) custom-call(s32[56,72]{1,0:T(8,128)} %exps.1, bf16[56,9216]{1,0:T(8,128)(2,1)} %delta.1), custom_call_target="tpu_custom_call" | custom-call | tf_op jit(solution)/shard_map/scaled_delta/pallas_call | solution.py:63
  3.0 2.1 %collective-permute-start = (bf16[2,56,1152]{2,1,0:T(8,128)(2,1)}, bf16[2,56,1152]{2,1,0:T(8,128)(2,1)S(1)}, u32[]{:S(2)}, u32[]{:S(2)}) collective-permute-start(bf16[2,56,1152]{2,1,0:T(8,128)(2,1)} %get-tuple-element.46), channel_id=1, source_target_pairs={{0,2},{1,3},{2,4},{3,5},{4,6},{5,7},{6,0},{7,1},{8,10},{9,11},{10,... | collective-permute-start | bytes 774152 | tf_op jit(solution)/shard_map/ppermute | solution.py:26
  5.1 2.5 %collective-permute-start.1 = (bf16[2,56,1152]{2,1,0:T(8,128)(2,1)}, bf16[2,56,1152]{2,1,0:T(8,128)(2,1)S(1)}, u32[]{:S(2)}, u32[]{:S(2)}) collective-permute-start(bf16[2,56,1152]{2,1,0:T(8,128)(2,1)} %get-tuple-element.47), channel_id=1, source_target_pairs={{0,4},{1,5},{2,6},{3,7},{4,0},{5,1},{6,2},{7,3},{8,12},{9,13},{10,... | collective-permute-start | bytes 774152 | tf_op jit(solution)/shard_map/ppermute | solution.py:26
  8.7 2.1 %fusion.1 = (f32[1024]{0:T(1024)S(1)}, bf16[1024,896]{1,0:T(8,128)(2,1)S(1)}) fusion(bf16[1024,896]{1,0:T(8,128)(2,1)} %param.5, f32[896]{0:T(1024)} %param.6), kind=kLoop, calls=%fused_computation.3 | loop fusion | flops 4586496 | bytes 3677696 | tf_op jit(solution)/shard_map/reduce_sum | solution.py:269
  11.0 1.7 %collective-permute-start.7 = (bf16[272,896]{1,0:T(8,128)(2,1)S(1)}, bf16[272,896]{1,0:T(8,128)(2,1)S(1)}, u32[]{:S(2)}, u32[]{:S(2)}) collective-permute-start(bf16[272,896]{1,0:T(8,128)(2,1)S(1)} %fusion.3), channel_id=1, source_target_pairs={{0,1},{1,0},{2,3},{3,2},{4,5},{5,4},{6,7},{7,6},{8,9},{9,8},{10,11... | collective-permute-start | bytes 1462280 | tf_op jit(solution)/shard_map/ppermute | solution.py:26
  12.8 6.1 %collective-permute-done.1 = bf16[2,56,1152]{2,1,0:T(8,128)(2,1)S(1)} collective-permute-done((bf16[2,56,1152]{2,1,0:T(8,128)(2,1)}, bf16[2,56,1152]{2,1,0:T(8,128)(2,1)S(1)}, u32[]{:S(2)}, u32[]{:S(2)}) %collective-permute-start.1) | collective-permute-done | bytes 258080 | tf_op jit(solution)/shard_map/ppermute | solution.py:26
  20.2 2.1 %collective-permute-start.6 = (bf16[320,896]{1,0:T(8,128)(2,1)S(1)}, bf16[320,896]{1,0:T(8,128)(2,1)S(1)}, u32[]{:S(2)}, u32[]{:S(2)}) collective-permute-start(bf16[320,896]{1,0:T(8,128)(2,1)S(1)} %slice.103.refs_6_), channel_id=1, source_target_pairs={{0,6},{1,7},{2,0},{3,1},{4,2},{5,3},{6,4},{7,5},{8,14},{9,15},{10,... | collective-permute-start | bytes 1720328 | tf_op jit(solution)/shard_map/ppermute | solution.py:26
  26.2 2.2 %collective-permute-start.4 = (bf16[4,56,1152]{2,1,0:T(8,128)(2,1)S(1)}, bf16[4,56,1152]{2,1,0:T(8,128)(2,1)S(1)}, u32[]{:S(2)}, u32[]{:S(2)}) collective-permute-start(bf16[4,56,1152]{2,1,0:T(8,128)(2,1)S(1)} %pad_maximum_fusion.4), channel_id=1, source_target_pairs={{0,65},{1,64},{2,67},{3,66},{4,69},{5,68},{6,71},{7,70},{8,73},{9,... | collective-permute-start | bytes 1548296 | tf_op jit(solution)/shard_map/ppermute | solution.py:26
  30.4 5.7 %collective-permute-done.3.other = bf16[4,56,1152]{2,1,0:T(8,128)(2,1)S(1)} collective-permute-done((bf16[4,56,1152]{2,1,0:T(8,128)(2,1)S(1)}, bf16[4,56,1152]{2,1,0:T(8,128)(2,1)S(1)}, u32[]{:S(2)}, u32[]{:S(2)}) %collective-permute-start.3) | collective-permute-done | bytes 516128 | tf_op jit(solution)/shard_map/ppermute | solution.py:26
  36.1 2.2 %collective-permute-done.4.other = bf16[4,56,1152]{2,1,0:T(8,128)(2,1)S(1)} collective-permute-done((bf16[4,56,1152]{2,1,0:T(8,128)(2,1)S(1)}, bf16[4,56,1152]{2,1,0:T(8,128)(2,1)S(1)}, u32[]{:S(2)}, u32[]{:S(2)}) %collective-permute-start.4) | collective-permute-done | bytes 516128 | tf_op jit(solution)/shard_map/ppermute | solution.py:26
  39.1 2.7 %collective-permute-start.11 = (bf16[544,896]{1,0:T(8,128)(2,1)}, bf16[544,896]{1,0:T(8,128)(2,1)}, u32[]{:S(2)}, u32[]{:S(2)}) collective-permute-start(bf16[544,896]{1,0:T(8,128)(2,1)} %pad_maximum_fusion.3.refs_0_), channel_id=1, source_target_pairs={{0,6},{1,7},{2,0},{3,1},{4,2},{5,3},{6,4},{7,5},{8,14},{9,15},{10,... | collective-permute-start | bytes 2924552 | tf_op jit(solution)/shard_map/ppermute | solution.py:26
  41.8 3.8 %refresh_own.1 = bf16[8,56,1152]{2,1,0:T(8,128)(2,1)} custom-call(bf16[4,56,1152]{2,1,0:T(8,128)(2,1)} %pad_maximum_fusion.5.same, bf16[4,56,1152]{2,1,0:T(8,128)(2,1)} %copy-done.16, bf16[128,56,1152]{2,1,0:T(8,128)(2,1)} %bitcast.4), custom_call_target="tpu_custom_call" | custom-call | tf_op jit(solution)/shard_map/refresh_own/pallas_call | solution.py:90
  48.5 2.1 %collective-permute-start.8 = (bf16[4,56,1152]{2,1,0:T(8,128)(2,1)}, bf16[4,56,1152]{2,1,0:T(8,128)(2,1)}, u32[]{:S(2)}, u32[]{:S(2)}) collective-permute-start(bf16[4,56,1152]{2,1,0:T(8,128)(2,1)} %pad_maximum_fusion.5.same), channel_id=1, source_target_pairs={{0,64},{1,65},{2,66},{3,67},{4,68},{5,69},{6,70},{7,71},{8,72},{9,... | collective-permute-start | bytes 1548296 | tf_op jit(solution)/shard_map/ppermute | solution.py:26
  50.7 9.8 %collective-permute-done.10.refs_1_ = bf16[544,896]{1,0:T(8,128)(2,1)} collective-permute-done((bf16[544,896]{1,0:T(8,128)(2,1)}, bf16[544,896]{1,0:T(8,128)(2,1)}, u32[]{:S(2)}, u32[]{:S(2)}) %collective-permute-start.10) | collective-permute-done | bytes 974880 | tf_op jit(solution)/shard_map/ppermute | solution.py:26
  64.0 3.8 %refresh_far.1 = bf16[8,56,1152]{2,1,0:T(8,128)(2,1)} custom-call(bf16[4,56,1152]{2,1,0:T(8,128)(2,1)} %collective-permute-done.8.same, bf16[4,56,1152]{2,1,0:T(8,128)(2,1)} %copy-done.15, bf16[128,56,1152]{2,1,0:T(8,128)(2,1)} %bitcast.5), custom_call_target="tpu_custom_call" | custom-call | tf_op jit(solution)/shard_map/refresh_far/pallas_call | solution.py:90
  70.9 6.7 %collective-permute-done.9 = bf16[448,896]{1,0:T(8,128)(2,1)} collective-permute-done((bf16[448,896]{1,0:T(8,128)(2,1)S(1)}, bf16[448,896]{1,0:T(8,128)(2,1)}, u32[]{:S(2)}, u32[]{:S(2)}) %collective-permute-start.9) | collective-permute-done | bytes 802848 | tf_op jit(solution)/shard_map/ppermute | solution.py:26
  81.7 1.8 %collective-permute-start.15 = (bf16[896,896]{1,0:T(8,128)(2,1)S(1)}, bf16[896,896]{1,0:T(8,128)(2,1)S(1)}, u32[]{:S(2)}, u32[]{:S(2)}) collective-permute-start(bf16[896,896]{1,0:T(8,128)(2,1)S(1)} %pad_maximum_fusion.1.refs_3_), channel_id=1, source_target_pairs={{0,6},{1,7},{2,0},{3,1},{4,2},{5,3},{6,4},{7,5},{8,14},{9,15},{10,... | collective-permute-start | bytes 4816904 | tf_op jit(solution)/shard_map/ppermute | solution.py:26
  83.5 5.6 %collective-permute-done.19.refs_14_.refs_8_ = bf16[448,1152]{1,0:T(8,128)(2,1)} collective-permute-done((bf16[448,1152]{1,0:T(8,128)(2,1)}, bf16[448,1152]{1,0:T(8,128)(2,1)}, u32[]{:S(2)}, u32[]{:S(2)}) %collective-permute-start.19) | collective-permute-done | bytes 1032224 | tf_op jit(solution)/shard_map/ppermute | solution.py:26
  91.7 21.8 %collective-permute-done.16.refs_9_ = bf16[960,896]{1,0:T(8,128)(2,1)S(1)} collective-permute-done((bf16[960,896]{1,0:T(8,128)(2,1)S(1)}, bf16[960,896]{1,0:T(8,128)(2,1)S(1)}, u32[]{:S(2)}, u32[]{:S(2)}) %collective-permute-start.16) | collective-permute-done | bytes 1720352 | tf_op jit(solution)/shard_map/ppermute | solution.py:26
  113.5 5.4 %collective-permute-start.25 = (bf16[448,1152]{1,0:T(8,128)(2,1)S(1)}, bf16[448,1152]{1,0:T(8,128)(2,1)}, u32[]{:S(2)}, u32[]{:S(2)}) collective-permute-start(bf16[448,1152]{1,0:T(8,128)(2,1)S(1)} %bitcast.10), channel_id=1, source_target_pairs={{0,8},{1,9},{2,10},{3,11},{4,12},{5,13},{6,14},{7,15},{8,0},{9,1},... | collective-permute-start | bytes 3096584 | tf_op jit(solution)/shard_map/ppermute | solution.py:26
  128.0 1.8 %collective-permute-start.24 = (bf16[608,896]{1,0:T(8,128)(2,1)}, bf16[608,896]{1,0:T(8,128)(2,1)}, u32[]{:S(2)}, u32[]{:S(2)}) collective-permute-start(bf16[608,896]{1,0:T(8,128)(2,1)} %slice.101), channel_id=1, source_target_pairs={{0,6},{1,7},{2,0},{3,1},{4,2},{5,3},{6,4},{7,5},{8,14},{9,15},{10,... | collective-permute-start | bytes 3268616 | tf_op jit(solution)/shard_map/ppermute | solution.py:26
  133.2 2.5 %collective-permute-done.31.refs_24_.refs_18_ = bf16[448,1152]{1,0:T(8,128)(2,1)S(1)} collective-permute-done((bf16[448,1152]{1,0:T(8,128)(2,1)}, bf16[448,1152]{1,0:T(8,128)(2,1)S(1)}, u32[]{:S(2)}, u32[]{:S(2)}) %collective-permute-start.31) | collective-permute-done | bytes 1032224 | tf_op jit(solution)/shard_map/ppermute | solution.py:26
  136.7 21.8 %product_most.1.refs_21_ = f32[1024,1152]{1,0:T(8,128)} custom-call(bf16[544,896]{1,0:T(8,128)(2,1)} %pad_maximum_fusion.3.refs_0_, bf16[544,896]{1,0:T(8,128)(2,1)} %collective-permute-done.10.refs_1_, bf16[544,896]{1,0:T(8,128)(2,1)} %collective-permute-done.11.refs_2_, bf16[896,896]{1,0:T(8,128)(2,1)} %copy-done.2, bf16[896,896]{1,0:T(8,128)(2,1)} %copy-done.11, ...), custom_call_target="tpu_custom_call" | custom-call | tf_op jit(solution)/shard_map/product_most/pallas_call | solution.py:176
  158.5 10.9 %product_rest.1 = bf16[1024,1152]{1,0:T(8,128)(2,1)} custom-call(bf16[544,896]{1,0:T(8,128)(2,1)} %collective-permute-done.12.refs_0_, bf16[320,896]{1,0:T(8,128)(2,1)} %collective-permute-done.13.refs_1_, bf16[608,896]{1,0:T(8,128)(2,1)} %collective-permute-done.23.refs_2_, bf16[608,896]{1,0:T(8,128)(2,1)} %collective-permute-done.24.refs_3_, ...), custom_call_target="tpu_custom_call" | custom-call | tf_op jit(solution)/shard_map/product_rest/pallas_call | solution.py:228
  (115 shorter events, 39.0 us)
Async XLA Ops:
  5.1 13.8 %collective-permute-start.1 = (bf16[2,56,1152]{2,1,0:T(8,128)(2,1)}, bf16[2,56,1152]{2,1,0:T(8,128)(2,1)S(1)}, u32[]{:S(2)}, u32[]{:S(2)}) collective-permute-start(bf16[2,56,1152]{2,1,0:T(8,128)(2,1)} %get-tuple-element.47), channel_id=1, source_target_pairs={{0,4},{1,5},{2,6},{3,7},{4,0},{5,1},{6,2},{7,3},{8,12},{9,13},{10,... | collective-permute-start | bytes 774152 | tf_op jit(solution)/shard_map/ppermute | solution.py:26
  11.0 18.4 %collective-permute-start.7 = (bf16[272,896]{1,0:T(8,128)(2,1)S(1)}, bf16[272,896]{1,0:T(8,128)(2,1)S(1)}, u32[]{:S(2)}, u32[]{:S(2)}) collective-permute-start(bf16[272,896]{1,0:T(8,128)(2,1)S(1)} %fusion.3), channel_id=1, source_target_pairs={{0,1},{1,0},{2,3},{3,2},{4,5},{5,4},{6,7},{7,6},{8,9},{9,8},{10,11... | collective-permute-start | bytes 1462280 | tf_op jit(solution)/shard_map/ppermute | solution.py:26
  19.6 18.7 %collective-permute-start.5 = (bf16[320,896]{1,0:T(8,128)(2,1)S(1)}, bf16[320,896]{1,0:T(8,128)(2,1)S(1)}, u32[]{:S(2)}, u32[]{:S(2)}) collective-permute-start(bf16[320,896]{1,0:T(8,128)(2,1)S(1)} %slice.103.refs_6_), channel_id=1, source_target_pairs={{0,2},{1,3},{2,4},{3,5},{4,6},{5,7},{6,0},{7,1},{8,10},{9,11},{10,... | collective-permute-start | bytes 1720328 | tf_op jit(solution)/shard_map/ppermute | solution.py:26
  20.2 18.1 %collective-permute-start.6 = (bf16[320,896]{1,0:T(8,128)(2,1)S(1)}, bf16[320,896]{1,0:T(8,128)(2,1)S(1)}, u32[]{:S(2)}, u32[]{:S(2)}) collective-permute-start(bf16[320,896]{1,0:T(8,128)(2,1)S(1)} %slice.103.refs_6_), channel_id=1, source_target_pairs={{0,6},{1,7},{2,0},{3,1},{4,2},{5,3},{6,4},{7,5},{8,14},{9,15},{10,... | collective-permute-start | bytes 1720328 | tf_op jit(solution)/shard_map/ppermute | solution.py:26
  24.5 11.6 %collective-permute-start.3 = (bf16[4,56,1152]{2,1,0:T(8,128)(2,1)S(1)}, bf16[4,56,1152]{2,1,0:T(8,128)(2,1)S(1)}, u32[]{:S(2)}, u32[]{:S(2)}) collective-permute-start(bf16[4,56,1152]{2,1,0:T(8,128)(2,1)S(1)} %pad_maximum_fusion.4), channel_id=1, source_target_pairs={{0,1},{1,0},{2,3},{3,2},{4,5},{5,4},{6,7},{7,6},{8,9},{9,8},{10,11... | collective-permute-start | bytes 1548296 | tf_op jit(solution)/shard_map/ppermute | solution.py:26
  26.2 12.1 %collective-permute-start.4 = (bf16[4,56,1152]{2,1,0:T(8,128)(2,1)S(1)}, bf16[4,56,1152]{2,1,0:T(8,128)(2,1)S(1)}, u32[]{:S(2)}, u32[]{:S(2)}) collective-permute-start(bf16[4,56,1152]{2,1,0:T(8,128)(2,1)S(1)} %pad_maximum_fusion.4), channel_id=1, source_target_pairs={{0,65},{1,64},{2,67},{3,66},{4,69},{5,68},{6,71},{7,70},{8,73},{9,... | collective-permute-start | bytes 1548296 | tf_op jit(solution)/shard_map/ppermute | solution.py:26
  39.1 21.3 %collective-permute-start.10 = (bf16[544,896]{1,0:T(8,128)(2,1)}, bf16[544,896]{1,0:T(8,128)(2,1)}, u32[]{:S(2)}, u32[]{:S(2)}) collective-permute-start(bf16[544,896]{1,0:T(8,128)(2,1)} %pad_maximum_fusion.3.refs_0_), channel_id=1, source_target_pairs={{0,2},{1,3},{2,4},{3,5},{4,6},{5,7},{6,0},{7,1},{8,10},{9,11},{10,... | collective-permute-start | bytes 2924552 | tf_op jit(solution)/shard_map/ppermute | solution.py:26
  39.1 21.3 %collective-permute-start.11 = (bf16[544,896]{1,0:T(8,128)(2,1)}, bf16[544,896]{1,0:T(8,128)(2,1)}, u32[]{:S(2)}, u32[]{:S(2)}) collective-permute-start(bf16[544,896]{1,0:T(8,128)(2,1)} %pad_maximum_fusion.3.refs_0_), channel_id=1, source_target_pairs={{0,6},{1,7},{2,0},{3,1},{4,2},{5,3},{6,4},{7,5},{8,14},{9,15},{10,... | collective-permute-start | bytes 2924552 | tf_op jit(solution)/shard_map/ppermute | solution.py:26
  45.6 22.2 %collective-permute-start.17 = (bf16[448,1152]{1,0:T(8,128)(2,1)}, bf16[448,1152]{1,0:T(8,128)(2,1)}, u32[]{:S(2)}, u32[]{:S(2)}) collective-permute-start(bf16[448,1152]{1,0:T(8,128)(2,1)} %bitcast.6), channel_id=1, source_target_pairs={{0,16},{1,17},{2,18},{3,19},{4,20},{5,21},{6,22},{7,23},{8,24},{9,... | collective-permute-start | bytes 3096584 | tf_op jit(solution)/shard_map/ppermute | solution.py:26
  47.0 20.8 %collective-permute-start.18 = (bf16[448,1152]{1,0:T(8,128)(2,1)}, bf16[448,1152]{1,0:T(8,128)(2,1)}, u32[]{:S(2)}, u32[]{:S(2)}) collective-permute-start(bf16[448,1152]{1,0:T(8,128)(2,1)} %bitcast.7), channel_id=1, source_target_pairs={{0,48},{1,49},{2,50},{3,51},{4,52},{5,53},{6,54},{7,55},{8,56},{9,... | collective-permute-start | bytes 3096584 | tf_op jit(solution)/shard_map/ppermute | solution.py:26
  48.5 13.2 %collective-permute-start.8 = (bf16[4,56,1152]{2,1,0:T(8,128)(2,1)}, bf16[4,56,1152]{2,1,0:T(8,128)(2,1)}, u32[]{:S(2)}, u32[]{:S(2)}) collective-permute-start(bf16[4,56,1152]{2,1,0:T(8,128)(2,1)} %pad_maximum_fusion.5.same), channel_id=1, source_target_pairs={{0,64},{1,65},{2,66},{3,67},{4,68},{5,69},{6,70},{7,71},{8,72},{9,... | collective-permute-start | bytes 1548296 | tf_op jit(solution)/shard_map/ppermute | solution.py:26
  60.4 20.4 %collective-permute-start.12 = (bf16[544,896]{1,0:T(8,128)(2,1)}, bf16[544,896]{1,0:T(8,128)(2,1)}, u32[]{:S(2)}, u32[]{:S(2)}) collective-permute-start(bf16[544,896]{1,0:T(8,128)(2,1)} %collective-permute-done.10.refs_1_), channel_id=1, source_target_pairs={{0,2},{1,3},{2,4},{3,5},{4,6},{5,7},{6,0},{7,1},{8,10},{9,11},{10,... | collective-permute-start | bytes 2924552 | tf_op jit(solution)/shard_map/ppermute | solution.py:26
  61.7 15.8 %collective-permute-start.9 = (bf16[448,896]{1,0:T(8,128)(2,1)S(1)}, bf16[448,896]{1,0:T(8,128)(2,1)}, u32[]{:S(2)}, u32[]{:S(2)}) collective-permute-start(bf16[448,896]{1,0:T(8,128)(2,1)S(1)} %slice.102), channel_id=1, source_target_pairs={{0,1},{1,0},{2,3},{3,2},{4,5},{5,4},{6,7},{7,6},{8,9},{9,8},{10,11... | collective-permute-start | bytes 2408456 | tf_op jit(solution)/shard_map/ppermute | solution.py:26
  62.6 17.3 %collective-permute-start.13 = (bf16[320,896]{1,0:T(8,128)(2,1)}, bf16[320,896]{1,0:T(8,128)(2,1)}, u32[]{:S(2)}, u32[]{:S(2)}) collective-permute-start(bf16[320,896]{1,0:T(8,128)(2,1)} %copy-done.13), channel_id=1, source_target_pairs={{0,6},{1,7},{2,0},{3,1},{4,2},{5,3},{6,4},{7,5},{8,14},{9,15},{10,... | collective-permute-start | bytes 1720328 | tf_op jit(solution)/shard_map/ppermute | solution.py:26
  67.8 21.2 %collective-permute-start.19 = (bf16[448,1152]{1,0:T(8,128)(2,1)}, bf16[448,1152]{1,0:T(8,128)(2,1)}, u32[]{:S(2)}, u32[]{:S(2)}) collective-permute-start(bf16[448,1152]{1,0:T(8,128)(2,1)} %bitcast.11), channel_id=1, source_target_pairs={{0,16},{1,17},{2,18},{3,19},{4,20},{5,21},{6,22},{7,23},{8,24},{9,... | collective-permute-start | bytes 3096584 | tf_op jit(solution)/shard_map/ppermute | solution.py:26
  69.2 19.9 %collective-permute-start.20 = (bf16[448,1152]{1,0:T(8,128)(2,1)}, bf16[448,1152]{1,0:T(8,128)(2,1)S(1)}, u32[]{:S(2)}, u32[]{:S(2)}) collective-permute-start(bf16[448,1152]{1,0:T(8,128)(2,1)} %bitcast.12), channel_id=1, source_target_pairs={{0,48},{1,49},{2,50},{3,51},{4,52},{5,53},{6,54},{7,55},{8,56},{9,... | collective-permute-start | bytes 3096584 | tf_op jit(solution)/shard_map/ppermute | solution.py:26
  77.5 36.0 %collective-permute-start.16 = (bf16[960,896]{1,0:T(8,128)(2,1)S(1)}, bf16[960,896]{1,0:T(8,128)(2,1)S(1)}, u32[]{:S(2)}, u32[]{:S(2)}) collective-permute-start(bf16[960,896]{1,0:T(8,128)(2,1)S(1)} %pad_maximum_fusion), channel_id=1, source_target_pairs={{0,1},{1,0},{2,3},{3,2},{4,5},{5,4},{6,7},{7,6},{8,9},{9,8},{10,11... | collective-permute-start | bytes 5160968 | tf_op jit(solution)/shard_map/ppermute | solution.py:26
  80.8 38.6 %collective-permute-start.14 = (bf16[896,896]{1,0:T(8,128)(2,1)S(1)}, bf16[896,896]{1,0:T(8,128)(2,1)S(1)}, u32[]{:S(2)}, u32[]{:S(2)}) collective-permute-start(bf16[896,896]{1,0:T(8,128)(2,1)S(1)} %pad_maximum_fusion.1.refs_3_), channel_id=1, source_target_pairs={{0,2},{1,3},{2,4},{3,5},{4,6},{5,7},{6,0},{7,1},{8,10},{9,11},{10,... | collective-permute-start | bytes 4816904 | tf_op jit(solution)/shard_map/ppermute | solution.py:26
  81.7 38.6 %collective-permute-start.15 = (bf16[896,896]{1,0:T(8,128)(2,1)S(1)}, bf16[896,896]{1,0:T(8,128)(2,1)S(1)}, u32[]{:S(2)}, u32[]{:S(2)}) collective-permute-start(bf16[896,896]{1,0:T(8,128)(2,1)S(1)} %pad_maximum_fusion.1.refs_3_), channel_id=1, source_target_pairs={{0,6},{1,7},{2,0},{3,1},{4,2},{5,3},{6,4},{7,5},{8,14},{9,15},{10,... | collective-permute-start | bytes 4816904 | tf_op jit(solution)/shard_map/ppermute | solution.py:26
  89.0 29.9 %collective-permute-start.21 = (bf16[448,1152]{1,0:T(8,128)(2,1)}, bf16[448,1152]{1,0:T(8,128)(2,1)}, u32[]{:S(2)}, u32[]{:S(2)}) collective-permute-start(bf16[448,1152]{1,0:T(8,128)(2,1)} %collective-permute-done.17.refs_11_.refs_5_), channel_id=1, source_target_pairs={{0,16},{1,17},{2,18},{3,19},{4,20},{5,21},{6,22},{7,23},{8,24},{9,... | collective-permute-start | bytes 3096584 | tf_op jit(solution)/shard_map/ppermute | solution.py:26
  90.0 29.0 %collective-permute-start.22 = (bf16[448,1152]{1,0:T(8,128)(2,1)S(1)}, bf16[448,1152]{1,0:T(8,128)(2,1)}, u32[]{:S(2)}, u32[]{:S(2)}) collective-permute-start(bf16[448,1152]{1,0:T(8,128)(2,1)S(1)} %collective-permute-done.20.refs_15_.refs_9_), channel_id=1, source_target_pairs={{0,48},{1,49},{2,50},{3,51},{4,52},{5,53},{6,54},{7,55},{8,56},{9,... | collective-permute-start | bytes 3096584 | tf_op jit(solution)/shard_map/ppermute | solution.py:26
  113.5 13.6 %collective-permute-start.25 = (bf16[448,1152]{1,0:T(8,128)(2,1)S(1)}, bf16[448,1152]{1,0:T(8,128)(2,1)}, u32[]{:S(2)}, u32[]{:S(2)}) collective-permute-start(bf16[448,1152]{1,0:T(8,128)(2,1)S(1)} %bitcast.10), channel_id=1, source_target_pairs={{0,8},{1,9},{2,10},{3,11},{4,12},{5,13},{6,14},{7,15},{8,0},{9,1},... | collective-permute-start | bytes 3096584 | tf_op jit(solution)/shard_map/ppermute | solution.py:26
  127.1 31.3 %collective-permute-start.23 = (bf16[608,896]{1,0:T(8,128)(2,1)}, bf16[608,896]{1,0:T(8,128)(2,1)}, u32[]{:S(2)}, u32[]{:S(2)}) collective-permute-start(bf16[608,896]{1,0:T(8,128)(2,1)} %pad_maximum_fusion.2), channel_id=1, source_target_pairs={{0,2},{1,3},{2,4},{3,5},{4,6},{5,7},{6,0},{7,1},{8,10},{9,11},{10,... | collective-permute-start | bytes 3268616 | tf_op jit(solution)/shard_map/ppermute | solution.py:26
  128.0 30.5 %collective-permute-start.24 = (bf16[608,896]{1,0:T(8,128)(2,1)}, bf16[608,896]{1,0:T(8,128)(2,1)}, u32[]{:S(2)}, u32[]{:S(2)}) collective-permute-start(bf16[608,896]{1,0:T(8,128)(2,1)} %slice.101), channel_id=1, source_target_pairs={{0,6},{1,7},{2,0},{3,1},{4,2},{5,3},{6,4},{7,5},{8,14},{9,15},{10,... | collective-permute-start | bytes 3268616 | tf_op jit(solution)/shard_map/ppermute | solution.py:26
  (31 other events, 396.8 us)

commit v5 on v4

--- a/solution.py
+++ b/solution.py
@@ -140,34 +140,45 @@
     pltpu.make_async_copy(held, held, sem).wait()
 
 
+def tile_spots(spots, i):
+    parts = []
+    for which, row, side, first, size in spots:
+        low, high = max(row, i * TILE), min(row + size, (i + 1) * TILE)
+        if low < high:
+            parts.append((which, low, side, first + low - row, high - low))
+    return parts
+
+
 def product_kernel(n_tok, n_wt, token_spots, weight_spots, *refs):
     tokens, weights = refs[:n_tok], refs[n_tok : n_tok + n_wt]
     out, xbuf, wbuf, acc, xsem, wsem, asem = refs[n_tok + n_wt :]
     x = position()[0]
+    tiles = acc.shape[0] // TILE
 
     def start(j):
         start_weights(lax.rem(x + STEPS[j] + 4, 4), wbuf.at[j], weights, weight_spots, wsem.at[j])
-        start_tokens(xbuf.at[j], tokens, token_spots[j], xsem.at[j])
+        for i in range(tiles):
+            start_tokens(xbuf.at[j], tokens, tile_spots(token_spots[j], i), xsem.at[j, i])
 
     start(0)
     for j in range(3):
-        wait_all(xbuf.at[j], xsem.at[j])
         wait_all(wbuf.at[j], wsem.at[j])
         if j < 2:
             start(j + 1)
 
-        @pl.loop(0, acc.shape[0] // TILE)
+        @pl.loop(0, tiles)
         def _(i, j=j):
             here = pl.ds(pl.multiple_of(i * TILE, TILE), TILE)
+            wait_all(xbuf.at[j, here], xsem.at[j, i])
             part = jnp.dot(xbuf[j, here], wbuf[j], preferred_element_type=jnp.float32)
             if j == 0:
                 acc[here] = part
             else:
                 acc[here] += part
-
-    store = pltpu.make_async_copy(acc, out, asem)
-    store.start()
-    store.wait()
+            if j == 2:
+                pltpu.make_async_copy(acc.at[here], out.at[here], asem).start()
+
+    pltpu.make_async_copy(acc, out, asem).wait()
 
 
 def product(tokens, token_spots, weights, weight_spots, rows, depth):
@@ -182,7 +193,7 @@
             pltpu.VMEM((3, rows, depth), jnp.bfloat16),
             pltpu.VMEM((3, depth, width), jnp.bfloat16),
             pltpu.VMEM((rows, width), jnp.float32),
-            pltpu.SemaphoreType.DMA((3,)),
+            pltpu.SemaphoreType.DMA((3, rows // TILE)),
             pltpu.SemaphoreType.DMA((3,)),
             pltpu.SemaphoreType.DMA,
         ],
@@ -200,11 +211,7 @@
     tiles = acc.shape[0] // TILE
     loads = []
     for i in range(tiles):
-        spots = []
-        for which, row, side, first, size in token_spots:
-            low, high = max(row, i * TILE), min(row + size, (i + 1) * TILE)
-            if low < high:
-                spots.append((which, low, side, first + low - row, high - low))
+        spots = tile_spots(token_spots, i)
         start_tokens(xbuf, tokens, spots, xsem.at[i])
         here = pl.ds(i * TILE, TILE)
         loads.append(pltpu.make_async_copy(before.at[here], acc.at[here], asem.at[i]))
@@ -297,20 +304,18 @@
     left_b, right_b = shift(pair_b, x=1), shift(pair_b, x=-1)
     three_c, theirs_b = gate(jnp.concatenate([mine_c, left_c, right_c], axis=0), theirs_b)
     theirs_c = shift(three_c, z_lo=1)
-    own_lf, far_l, far_r = gate(own_l, far_l, far_r)
-    own_o, far_o = shift(own_lf, y=1), shift(far_r, y=-1)
-    rings = [own, own_l, own_r, other_hi, far_l, far_r]
-    swaps = [shift(v, core=1) for v in rings]
-
     tail = sum(
         v[at : at + 4].astype(jnp.float32)
         for v in (pair_a, left_a, right_a, opposite_a)
         for at in (n_a, 2 * n_a + extra)
     ).reshape(2, 2 * features)
     inv = lax.rsqrt((tail[0] + tail[1])[:count] / total + 1e-06)[:, None]
-    left_b, right_b, theirs_c, own_o, far_o, opposite_a, opposite_c, inv = gate(
-        left_b, right_b, theirs_c, own_o, far_o, opposite_a, opposite_c, inv
-    )
+    own_lf, far_l, far_r, inv = gate(own_l, far_l, far_r, inv)
+    own_o, far_o = shift(own_lf, y=1), shift(far_r, y=-1)
+    rings = [own, own_l, own_r, other_hi, far_l, far_r]
+    swaps = [shift(v, core=1) for v in rings]
+
+    left_b, right_b, theirs_c, own_o, far_o = gate(left_b, right_b, theirs_c, own_o, far_o)
     cut = (2 * n_b - n_c) // 32 * 16
     up = shift(jnp.concatenate([theirs_c[n_c : 2 * n_c], left_b[:cut]], axis=0), x=1)
     down = shift(right_b[cut:], x=-1)

time: 170 us -> 167 us (0.982)
  waiting for transfers between devices: 62.7 us -> 58.2 us
  other arithmetic: 7.54 us -> 9.87 us
    ppermute x33, waiting for transfers between devices: 62.7 us -> 58.2 us  [shift(): return lax.ppermute(value, ('fsdp', 'tp'), links(**step))]
    slice x3, local copies, waits for them, and re-layouts: 2.14 us -> 0.09 us  [local(): same = jnp.stack([g[0] for g in got])]
    unnamed x40 -> x36, local copies, waits for them, and re-layouts: 5.21 us -> 3.87 us
  transfers between devices with their start and end apart: 33 -> 33, of which waited for: 11 -> 11; matrix products, arithmetic and copies ran while one was open for 7% -> 9% of each run, Pallas kernels for 17% -> 17%
where the time goes in v5:
time: 167 us; the launch traced here: 166 us
  waiting for transfers between devices  58.2 us (35%)
  starting transfers between devices  46.1 us (28%)
  Pallas kernels  42 us (25%)
  other arithmetic  9.87 us (6%)
  local copies, waits for them, and re-layouts  9.66 us (6%)
    ppermute x33, waiting for transfers between devices, shift(): return lax.ppermute(value, ('fsdp', 'tp'), links(**step))  58.2 us
    ppermute x33, starting transfers between devices, shift(): return lax.ppermute(value, ('fsdp', 'tp'), links(**step))  46.1 us
    pallas_call x1, Pallas kernels, product(): pl.pallas_call(functools.partial(product_kernel, len(tokens), len(weights...  20.3 us
    pallas_call x1, Pallas kernels, finish(): pl.pallas_call(functools.partial(finish_kernel, len(tokens), len(weights)...  11.1 us
    pallas_call x2, Pallas kernels, refresh(): pl.pallas_call(functools.partial(refresh_kernel, other_hi), out_shape=jax...  7.63 us
    unnamed x36, local copies, waits for them, and re-layouts  3.87 us
  transfers between devices with their start and end apart: 33, of which 11 were waited for; matrix products, arithmetic and copies ran while one was open for 9% of the time, Pallas kernels for 17%

profile of v5, /device:TPU:1, one launch (start us, length us, event | category | flops | bytes accessed | tf_op | source)
XLA Modules:
  0.0 166.3 jit_solution(5454648831888524706)
XLA Ops:
  0.0 3.0 %scaled_delta.1 = (bf16[2,56,1152]{2,1,0:T(8,128)(2,1)}, bf16[2,56,1152]{2,1,0:T(8,128)(2,1)}, bf16[2,56,1152]{2,1,0:T(8,128)(2,1)}, bf16[2,56,1152]{2,1,0:T(8,128)(2,1)}) custom-call(s32[56,72]{1,0:T(8,128)} %exps.1, bf16[56,9216]{1,0:T(8,128)(2,1)} %delta.1), custom_call_target="tpu_custom_call" | custom-call | tf_op jit(solution)/shard_map/scaled_delta/pallas_call | solution.py:63
  3.0 2.1 %collective-permute-start = (bf16[2,56,1152]{2,1,0:T(8,128)(2,1)}, bf16[2,56,1152]{2,1,0:T(8,128)(2,1)S(1)}, u32[]{:S(2)}, u32[]{:S(2)}) collective-permute-start(bf16[2,56,1152]{2,1,0:T(8,128)(2,1)} %get-tuple-element.44), channel_id=1, source_target_pairs={{0,2},{1,3},{2,4},{3,5},{4,6},{5,7},{6,0},{7,1},{8,10},{9,11},{10,... | collective-permute-start | bytes 774152 | tf_op jit(solution)/shard_map/ppermute | solution.py:26
  5.1 2.5 %collective-permute-start.1 = (bf16[2,56,1152]{2,1,0:T(8,128)(2,1)}, bf16[2,56,1152]{2,1,0:T(8,128)(2,1)S(1)}, u32[]{:S(2)}, u32[]{:S(2)}) collective-permute-start(bf16[2,56,1152]{2,1,0:T(8,128)(2,1)} %get-tuple-element.45), channel_id=1, source_target_pairs={{0,4},{1,5},{2,6},{3,7},{4,0},{5,1},{6,2},{7,3},{8,12},{9,13},{10,... | collective-permute-start | bytes 774152 | tf_op jit(solution)/shard_map/ppermute | solution.py:26
  8.7 2.1 %fusion.1 = (f32[1024]{0:T(1024)S(1)}, bf16[1024,896]{1,0:T(8,128)(2,1)S(1)}) fusion(bf16[1024,896]{1,0:T(8,128)(2,1)} %param.5, f32[896]{0:T(1024)} %param.6), kind=kLoop, calls=%fused_computation.3 | loop fusion | flops 4586496 | bytes 3677696 | tf_op jit(solution)/shard_map/reduce_sum | solution.py:276
  12.8 6.1 %collective-permute-done.1 = bf16[2,56,1152]{2,1,0:T(8,128)(2,1)S(1)} collective-permute-done((bf16[2,56,1152]{2,1,0:T(8,128)(2,1)}, bf16[2,56,1152]{2,1,0:T(8,128)(2,1)S(1)}, u32[]{:S(2)}, u32[]{:S(2)}) %collective-permute-start.1) | collective-permute-done | bytes 258080 | tf_op jit(solution)/shard_map/ppermute | solution.py:26
  22.0 1.8 %collective-permute-start.3 = (bf16[4,56,1152]{2,1,0:T(8,128)(2,1)S(1)}, bf16[4,56,1152]{2,1,0:T(8,128)(2,1)S(1)}, u32[]{:S(2)}, u32[]{:S(2)}) collective-permute-start(bf16[4,56,1152]{2,1,0:T(8,128)(2,1)S(1)} %pad_maximum_fusion.4), channel_id=1, source_target_pairs={{0,1},{1,0},{2,3},{3,2},{4,5},{5,4},{6,7},{7,6},{8,9},{9,8},{10,11... | collective-permute-start | bytes 1548296 | tf_op jit(solution)/shard_map/ppermute | solution.py:26
  23.8 2.2 %collective-permute-start.4 = (bf16[4,56,1152]{2,1,0:T(8,128)(2,1)S(1)}, bf16[4,56,1152]{2,1,0:T(8,128)(2,1)S(1)}, u32[]{:S(2)}, u32[]{:S(2)}) collective-permute-start(bf16[4,56,1152]{2,1,0:T(8,128)(2,1)S(1)} %pad_maximum_fusion.4), channel_id=1, source_target_pairs={{0,65},{1,64},{2,67},{3,66},{4,69},{5,68},{6,71},{7,70},{8,73},{9,... | collective-permute-start | bytes 1548296 | tf_op jit(solution)/shard_map/ppermute | solution.py:26
  28.0 6.1 %collective-permute-done.3.other = bf16[4,56,1152]{2,1,0:T(8,128)(2,1)S(1)} collective-permute-done((bf16[4,56,1152]{2,1,0:T(8,128)(2,1)S(1)}, bf16[4,56,1152]{2,1,0:T(8,128)(2,1)S(1)}, u32[]{:S(2)}, u32[]{:S(2)}) %collective-permute-start.3) | collective-permute-done | bytes 516128 | tf_op jit(solution)/shard_map/ppermute | solution.py:26
  34.0 2.2 %collective-permute-done.4.other = bf16[4,56,1152]{2,1,0:T(8,128)(2,1)S(1)} collective-permute-done((bf16[4,56,1152]{2,1,0:T(8,128)(2,1)S(1)}, bf16[4,56,1152]{2,1,0:T(8,128)(2,1)S(1)}, u32[]{:S(2)}, u32[]{:S(2)}) %collective-permute-start.4) | collective-permute-done | bytes 516128 | tf_op jit(solution)/shard_map/ppermute | solution.py:26
  37.3 2.7 %collective-permute-start.11 = (bf16[544,896]{1,0:T(8,128)(2,1)}, bf16[544,896]{1,0:T(8,128)(2,1)S(1)}, u32[]{:S(2)}, u32[]{:S(2)}) collective-permute-start(bf16[544,896]{1,0:T(8,128)(2,1)} %pad_maximum_fusion.3.refs_0_), channel_id=1, source_target_pairs={{0,6},{1,7},{2,0},{3,1},{4,2},{5,3},{6,4},{7,5},{8,14},{9,15},{10,... | collective-permute-start | bytes 2924552 | tf_op jit(solution)/shard_map/ppermute | solution.py:26
  39.9 2.1 %collective-permute-start.8 = (bf16[4,56,1152]{2,1,0:T(8,128)(2,1)}, bf16[4,56,1152]{2,1,0:T(8,128)(2,1)}, u32[]{:S(2)}, u32[]{:S(2)}) collective-permute-start(bf16[4,56,1152]{2,1,0:T(8,128)(2,1)} %pad_maximum_fusion.5.same), channel_id=1, source_target_pairs={{0,64},{1,65},{2,66},{3,67},{4,68},{5,69},{6,70},{7,71},{8,72},{9,... | collective-permute-start | bytes 1548296 | tf_op jit(solution)/shard_map/ppermute | solution.py:26
  42.0 3.8 %refresh_own.1 = bf16[8,56,1152]{2,1,0:T(8,128)(2,1)} custom-call(bf16[4,56,1152]{2,1,0:T(8,128)(2,1)} %pad_maximum_fusion.5.same, bf16[4,56,1152]{2,1,0:T(8,128)(2,1)} %copy-done.16, bf16[128,56,1152]{2,1,0:T(8,128)(2,1)} %bitcast.4), custom_call_target="tpu_custom_call" | custom-call | tf_op jit(solution)/shard_map/refresh_own/pallas_call | solution.py:90
  48.7 10.2 %collective-permute-done.10.refs_1_ = bf16[544,896]{1,0:T(8,128)(2,1)} collective-permute-done((bf16[544,896]{1,0:T(8,128)(2,1)}, bf16[544,896]{1,0:T(8,128)(2,1)}, u32[]{:S(2)}, u32[]{:S(2)}) %collective-permute-start.10) | collective-permute-done | bytes 974880 | tf_op jit(solution)/shard_map/ppermute | solution.py:26
  61.7 1.9 %collective-permute-start.13 = (bf16[320,896]{1,0:T(8,128)(2,1)}, bf16[320,896]{1,0:T(8,128)(2,1)}, u32[]{:S(2)}, u32[]{:S(2)}) collective-permute-start(bf16[320,896]{1,0:T(8,128)(2,1)} %copy-done.12), channel_id=1, source_target_pairs={{0,6},{1,7},{2,0},{3,1},{4,2},{5,3},{6,4},{7,5},{8,14},{9,15},{10,... | collective-permute-start | bytes 1720328 | tf_op jit(solution)/shard_map/ppermute | solution.py:26
  63.6 3.8 %refresh_far.1 = bf16[8,56,1152]{2,1,0:T(8,128)(2,1)} custom-call(bf16[4,56,1152]{2,1,0:T(8,128)(2,1)} %collective-permute-done.8.same, bf16[4,56,1152]{2,1,0:T(8,128)(2,1)} %copy-done.15, bf16[128,56,1152]{2,1,0:T(8,128)(2,1)} %bitcast.5), custom_call_target="tpu_custom_call" | custom-call | tf_op jit(solution)/shard_map/refresh_far/pallas_call | solution.py:90
  72.1 4.6 %collective-permute-done.9 = bf16[448,896]{1,0:T(8,128)(2,1)} collective-permute-done((bf16[448,896]{1,0:T(8,128)(2,1)S(1)}, bf16[448,896]{1,0:T(8,128)(2,1)}, u32[]{:S(2)}, u32[]{:S(2)}) %collective-permute-start.9) | collective-permute-done | bytes 802848 | tf_op jit(solution)/shard_map/ppermute | solution.py:26
  77.9 2.4 %pad_maximum_fusion.1.refs_3_ = bf16[896,896]{1,0:T(8,128)(2,1)} fusion(bf16[448,896]{1,0:T(8,128)(2,1)} %collective-permute-done.9, bf16[448,896]{1,0:T(8,128)(2,1)S(1)} %slice.102), kind=kLoop, calls=%fused_computation.5 | loop fusion | flops 3211264 | bytes 3211264 | tf_op jit(solution)/shard_map/concatenate | solution.py:302
  84.2 4.9 %collective-permute-done.19.refs_14_.refs_8_ = bf16[448,1152]{1,0:T(8,128)(2,1)} collective-permute-done((bf16[448,1152]{1,0:T(8,128)(2,1)}, bf16[448,1152]{1,0:T(8,128)(2,1)}, u32[]{:S(2)}, u32[]{:S(2)}) %collective-permute-start.19) | collective-permute-done | bytes 1032224 | tf_op jit(solution)/shard_map/ppermute | solution.py:26
  91.8 21.0 %collective-permute-done.16.refs_9_ = bf16[960,896]{1,0:T(8,128)(2,1)} collective-permute-done((bf16[960,896]{1,0:T(8,128)(2,1)}, bf16[960,896]{1,0:T(8,128)(2,1)}, u32[]{:S(2)}, u32[]{:S(2)}) %collective-permute-start.16) | collective-permute-done | bytes 1720352 | tf_op jit(solution)/shard_map/ppermute | solution.py:26
  112.8 5.4 %collective-permute-start.25 = (bf16[448,1152]{1,0:T(8,128)(2,1)S(1)}, bf16[448,1152]{1,0:T(8,128)(2,1)S(1)}, u32[]{:S(2)}, u32[]{:S(2)}) collective-permute-start(bf16[448,1152]{1,0:T(8,128)(2,1)S(1)} %bitcast.10), channel_id=1, source_target_pairs={{0,8},{1,9},{2,10},{3,11},{4,12},{5,13},{6,14},{7,15},{8,0},{9,1},... | collective-permute-start | bytes 3096584 | tf_op jit(solution)/shard_map/ppermute | solution.py:26
  122.1 2.3 %slice.101 = bf16[608,896]{1,0:T(8,128)(2,1)} slice(bf16[896,896]{1,0:T(8,128)(2,1)} %collective-permute-done.15.refs_5_), slice={[288:896], [0:896]} | slice | bytes 2179072 | tf_op jit(solution)/shard_map/slice | solution.py:321
  126.2 2.0 %collective-permute-start.24 = (bf16[608,896]{1,0:T(8,128)(2,1)}, bf16[608,896]{1,0:T(8,128)(2,1)}, u32[]{:S(2)}, u32[]{:S(2)}) collective-permute-start(bf16[608,896]{1,0:T(8,128)(2,1)} %slice.101), channel_id=1, source_target_pairs={{0,6},{1,7},{2,0},{3,1},{4,2},{5,3},{6,4},{7,5},{8,14},{9,15},{10,... | collective-permute-start | bytes 3268616 | tf_op jit(solution)/shard_map/ppermute | solution.py:26
  134.7 20.3 %product_most.1.refs_21_ = f32[1024,1152]{1,0:T(8,128)} custom-call(bf16[544,896]{1,0:T(8,128)(2,1)} %pad_maximum_fusion.3.refs_0_, bf16[544,896]{1,0:T(8,128)(2,1)} %collective-permute-done.10.refs_1_, bf16[544,896]{1,0:T(8,128)(2,1)} %copy-done.14, bf16[896,896]{1,0:T(8,128)(2,1)} %pad_maximum_fusion.1.refs_3_, ...), custom_call_target="tpu_custom_call" | custom-call | tf_op jit(solution)/shard_map/product_most/pallas_call | solution.py:187
  155.0 11.1 %product_rest.1 = bf16[1024,1152]{1,0:T(8,128)(2,1)} custom-call(bf16[544,896]{1,0:T(8,128)(2,1)} %collective-permute-done.12.refs_0_, bf16[320,896]{1,0:T(8,128)(2,1)} %collective-permute-done.13.refs_1_, bf16[608,896]{1,0:T(8,128)(2,1)} %collective-permute-done.23.refs_2_, bf16[608,896]{1,0:T(8,128)(2,1)} %collective-permute-done.24.refs_3_, ...), custom_call_target="tpu_custom_call" | custom-call | tf_op jit(solution)/shard_map/product_rest/pallas_call | solution.py:235
  (109 shorter events, 39.3 us)
Async XLA Ops:
  5.1 13.8 %collective-permute-start.1 = (bf16[2,56,1152]{2,1,0:T(8,128)(2,1)}, bf16[2,56,1152]{2,1,0:T(8,128)(2,1)S(1)}, u32[]{:S(2)}, u32[]{:S(2)}) collective-permute-start(bf16[2,56,1152]{2,1,0:T(8,128)(2,1)} %get-tuple-element.45), channel_id=1, source_target_pairs={{0,4},{1,5},{2,6},{3,7},{4,0},{5,1},{6,2},{7,3},{8,12},{9,13},{10,... | collective-permute-start | bytes 774152 | tf_op jit(solution)/shard_map/ppermute | solution.py:26
  11.0 16.0 %collective-permute-start.7 = (bf16[272,896]{1,0:T(8,128)(2,1)S(1)}, bf16[272,896]{1,0:T(8,128)(2,1)S(1)}, u32[]{:S(2)}, u32[]{:S(2)}) collective-permute-start(bf16[272,896]{1,0:T(8,128)(2,1)S(1)} %fusion.3), channel_id=1, source_target_pairs={{0,1},{1,0},{2,3},{3,2},{4,5},{5,4},{6,7},{7,6},{8,9},{9,8},{10,11... | collective-permute-start | bytes 1462280 | tf_op jit(solution)/shard_map/ppermute | solution.py:26
  18.9 17.4 %collective-permute-start.5 = (bf16[320,896]{1,0:T(8,128)(2,1)S(1)}, bf16[320,896]{1,0:T(8,128)(2,1)S(1)}, u32[]{:S(2)}, u32[]{:S(2)}) collective-permute-start(bf16[320,896]{1,0:T(8,128)(2,1)S(1)} %slice.103.refs_6_), channel_id=1, source_target_pairs={{0,2},{1,3},{2,4},{3,5},{4,6},{5,7},{6,0},{7,1},{8,10},{9,11},{10,... | collective-permute-start | bytes 1720328 | tf_op jit(solution)/shard_map/ppermute | solution.py:26
  20.1 16.2 %collective-permute-start.6 = (bf16[320,896]{1,0:T(8,128)(2,1)S(1)}, bf16[320,896]{1,0:T(8,128)(2,1)S(1)}, u32[]{:S(2)}, u32[]{:S(2)}) collective-permute-start(bf16[320,896]{1,0:T(8,128)(2,1)S(1)} %slice.103.refs_6_), channel_id=1, source_target_pairs={{0,6},{1,7},{2,0},{3,1},{4,2},{5,3},{6,4},{7,5},{8,14},{9,15},{10,... | collective-permute-start | bytes 1720328 | tf_op jit(solution)/shard_map/ppermute | solution.py:26
  22.0 12.0 %collective-permute-start.3 = (bf16[4,56,1152]{2,1,0:T(8,128)(2,1)S(1)}, bf16[4,56,1152]{2,1,0:T(8,128)(2,1)S(1)}, u32[]{:S(2)}, u32[]{:S(2)}) collective-permute-start(bf16[4,56,1152]{2,1,0:T(8,128)(2,1)S(1)} %pad_maximum_fusion.4), channel_id=1, source_target_pairs={{0,1},{1,0},{2,3},{3,2},{4,5},{5,4},{6,7},{7,6},{8,9},{9,8},{10,11... | collective-permute-start | bytes 1548296 | tf_op jit(solution)/shard_map/ppermute | solution.py:26
  23.8 12.4 %collective-permute-start.4 = (bf16[4,56,1152]{2,1,0:T(8,128)(2,1)S(1)}, bf16[4,56,1152]{2,1,0:T(8,128)(2,1)S(1)}, u32[]{:S(2)}, u32[]{:S(2)}) collective-permute-start(bf16[4,56,1152]{2,1,0:T(8,128)(2,1)S(1)} %pad_maximum_fusion.4), channel_id=1, source_target_pairs={{0,65},{1,64},{2,67},{3,66},{4,69},{5,68},{6,71},{7,70},{8,73},{9,... | collective-permute-start | bytes 1548296 | tf_op jit(solution)/shard_map/ppermute | solution.py:26
  37.3 21.7 %collective-permute-start.10 = (bf16[544,896]{1,0:T(8,128)(2,1)}, bf16[544,896]{1,0:T(8,128)(2,1)}, u32[]{:S(2)}, u32[]{:S(2)}) collective-permute-start(bf16[544,896]{1,0:T(8,128)(2,1)} %pad_maximum_fusion.3.refs_0_), channel_id=1, source_target_pairs={{0,2},{1,3},{2,4},{3,5},{4,6},{5,7},{6,0},{7,1},{8,10},{9,11},{10,... | collective-permute-start | bytes 2924552 | tf_op jit(solution)/shard_map/ppermute | solution.py:26
  37.3 21.7 %collective-permute-start.11 = (bf16[544,896]{1,0:T(8,128)(2,1)}, bf16[544,896]{1,0:T(8,128)(2,1)S(1)}, u32[]{:S(2)}, u32[]{:S(2)}) collective-permute-start(bf16[544,896]{1,0:T(8,128)(2,1)} %pad_maximum_fusion.3.refs_0_), channel_id=1, source_target_pairs={{0,6},{1,7},{2,0},{3,1},{4,2},{5,3},{6,4},{7,5},{8,14},{9,15},{10,... | collective-permute-start | bytes 2924552 | tf_op jit(solution)/shard_map/ppermute | solution.py:26
  39.9 20.8 %collective-permute-start.8 = (bf16[4,56,1152]{2,1,0:T(8,128)(2,1)}, bf16[4,56,1152]{2,1,0:T(8,128)(2,1)}, u32[]{:S(2)}, u32[]{:S(2)}) collective-permute-start(bf16[4,56,1152]{2,1,0:T(8,128)(2,1)} %pad_maximum_fusion.5.same), channel_id=1, source_target_pairs={{0,64},{1,65},{2,66},{3,67},{4,68},{5,69},{6,70},{7,71},{8,72},{9,... | collective-permute-start | bytes 1548296 | tf_op jit(solution)/shard_map/ppermute | solution.py:26
  45.8 22.2 %collective-permute-start.17 = (bf16[448,1152]{1,0:T(8,128)(2,1)}, bf16[448,1152]{1,0:T(8,128)(2,1)}, u32[]{:S(2)}, u32[]{:S(2)}) collective-permute-start(bf16[448,1152]{1,0:T(8,128)(2,1)} %bitcast.6), channel_id=1, source_target_pairs={{0,16},{1,17},{2,18},{3,19},{4,20},{5,21},{6,22},{7,23},{8,24},{9,... | collective-permute-start | bytes 3096584 | tf_op jit(solution)/shard_map/ppermute | solution.py:26
  47.2 20.9 %collective-permute-start.18 = (bf16[448,1152]{1,0:T(8,128)(2,1)}, bf16[448,1152]{1,0:T(8,128)(2,1)}, u32[]{:S(2)}, u32[]{:S(2)}) collective-permute-start(bf16[448,1152]{1,0:T(8,128)(2,1)} %bitcast.7), channel_id=1, source_target_pairs={{0,48},{1,49},{2,50},{3,51},{4,52},{5,53},{6,54},{7,55},{8,56},{9,... | collective-permute-start | bytes 3096584 | tf_op jit(solution)/shard_map/ppermute | solution.py:26
  59.9 20.7 %collective-permute-start.12 = (bf16[544,896]{1,0:T(8,128)(2,1)}, bf16[544,896]{1,0:T(8,128)(2,1)}, u32[]{:S(2)}, u32[]{:S(2)}) collective-permute-start(bf16[544,896]{1,0:T(8,128)(2,1)} %collective-permute-done.10.refs_1_), channel_id=1, source_target_pairs={{0,2},{1,3},{2,4},{3,5},{4,6},{5,7},{6,0},{7,1},{8,10},{9,11},{10,... | collective-permute-start | bytes 2924552 | tf_op jit(solution)/shard_map/ppermute | solution.py:26
  60.8 16.0 %collective-permute-start.9 = (bf16[448,896]{1,0:T(8,128)(2,1)S(1)}, bf16[448,896]{1,0:T(8,128)(2,1)}, u32[]{:S(2)}, u32[]{:S(2)}) collective-permute-start(bf16[448,896]{1,0:T(8,128)(2,1)S(1)} %slice.102), channel_id=1, source_target_pairs={{0,1},{1,0},{2,3},{3,2},{4,5},{5,4},{6,7},{7,6},{8,9},{9,8},{10,11... | collective-permute-start | bytes 2408456 | tf_op jit(solution)/shard_map/ppermute | solution.py:26
  61.7 18.6 %collective-permute-start.13 = (bf16[320,896]{1,0:T(8,128)(2,1)}, bf16[320,896]{1,0:T(8,128)(2,1)}, u32[]{:S(2)}, u32[]{:S(2)}) collective-permute-start(bf16[320,896]{1,0:T(8,128)(2,1)} %copy-done.12), channel_id=1, source_target_pairs={{0,6},{1,7},{2,0},{3,1},{4,2},{5,3},{6,4},{7,5},{8,14},{9,15},{10,... | collective-permute-start | bytes 1720328 | tf_op jit(solution)/shard_map/ppermute | solution.py:26
  68.1 21.0 %collective-permute-start.19 = (bf16[448,1152]{1,0:T(8,128)(2,1)}, bf16[448,1152]{1,0:T(8,128)(2,1)}, u32[]{:S(2)}, u32[]{:S(2)}) collective-permute-start(bf16[448,1152]{1,0:T(8,128)(2,1)} %bitcast.11), channel_id=1, source_target_pairs={{0,16},{1,17},{2,18},{3,19},{4,20},{5,21},{6,22},{7,23},{8,24},{9,... | collective-permute-start | bytes 3096584 | tf_op jit(solution)/shard_map/ppermute | solution.py:26
  69.1 20.0 %collective-permute-start.20 = (bf16[448,1152]{1,0:T(8,128)(2,1)}, bf16[448,1152]{1,0:T(8,128)(2,1)}, u32[]{:S(2)}, u32[]{:S(2)}) collective-permute-start(bf16[448,1152]{1,0:T(8,128)(2,1)} %bitcast.12), channel_id=1, source_target_pairs={{0,48},{1,49},{2,50},{3,51},{4,52},{5,53},{6,54},{7,55},{8,56},{9,... | collective-permute-start | bytes 3096584 | tf_op jit(solution)/shard_map/ppermute | solution.py:26
  76.7 36.0 %collective-permute-start.16 = (bf16[960,896]{1,0:T(8,128)(2,1)}, bf16[960,896]{1,0:T(8,128)(2,1)}, u32[]{:S(2)}, u32[]{:S(2)}) collective-permute-start(bf16[960,896]{1,0:T(8,128)(2,1)} %pad_maximum_fusion), channel_id=1, source_target_pairs={{0,1},{1,0},{2,3},{3,2},{4,5},{5,4},{6,7},{7,6},{8,9},{9,8},{10,11... | collective-permute-start | bytes 5160968 | tf_op jit(solution)/shard_map/ppermute | solution.py:26
  80.6 38.1 %collective-permute-start.14 = (bf16[896,896]{1,0:T(8,128)(2,1)}, bf16[896,896]{1,0:T(8,128)(2,1)}, u32[]{:S(2)}, u32[]{:S(2)}) collective-permute-start(bf16[896,896]{1,0:T(8,128)(2,1)} %pad_maximum_fusion.1.refs_3_), channel_id=1, source_target_pairs={{0,2},{1,3},{2,4},{3,5},{4,6},{5,7},{6,0},{7,1},{8,10},{9,11},{10,... | collective-permute-start | bytes 4816904 | tf_op jit(solution)/shard_map/ppermute | solution.py:26
  81.7 38.1 %collective-permute-start.15 = (bf16[896,896]{1,0:T(8,128)(2,1)}, bf16[896,896]{1,0:T(8,128)(2,1)}, u32[]{:S(2)}, u32[]{:S(2)}) collective-permute-start(bf16[896,896]{1,0:T(8,128)(2,1)} %pad_maximum_fusion.1.refs_3_), channel_id=1, source_target_pairs={{0,6},{1,7},{2,0},{3,1},{4,2},{5,3},{6,4},{7,5},{8,14},{9,15},{10,... | collective-permute-start | bytes 4816904 | tf_op jit(solution)/shard_map/ppermute | solution.py:26
  89.1 29.1 %collective-permute-start.21 = (bf16[448,1152]{1,0:T(8,128)(2,1)}, bf16[448,1152]{1,0:T(8,128)(2,1)S(1)}, u32[]{:S(2)}, u32[]{:S(2)}) collective-permute-start(bf16[448,1152]{1,0:T(8,128)(2,1)} %collective-permute-done.17.refs_11_.refs_5_), channel_id=1, source_target_pairs={{0,16},{1,17},{2,18},{3,19},{4,20},{5,21},{6,22},{7,23},{8,24},{9,... | collective-permute-start | bytes 3096584 | tf_op jit(solution)/shard_map/ppermute | solution.py:26
  90.5 27.8 %collective-permute-start.22 = (bf16[448,1152]{1,0:T(8,128)(2,1)}, bf16[448,1152]{1,0:T(8,128)(2,1)}, u32[]{:S(2)}, u32[]{:S(2)}) collective-permute-start(bf16[448,1152]{1,0:T(8,128)(2,1)} %collective-permute-done.20.refs_15_.refs_9_), channel_id=1, source_target_pairs={{0,48},{1,49},{2,50},{3,51},{4,52},{5,53},{6,54},{7,55},{8,56},{9,... | collective-permute-start | bytes 3096584 | tf_op jit(solution)/shard_map/ppermute | solution.py:26
  112.8 12.7 %collective-permute-start.25 = (bf16[448,1152]{1,0:T(8,128)(2,1)S(1)}, bf16[448,1152]{1,0:T(8,128)(2,1)S(1)}, u32[]{:S(2)}, u32[]{:S(2)}) collective-permute-start(bf16[448,1152]{1,0:T(8,128)(2,1)S(1)} %bitcast.10), channel_id=1, source_target_pairs={{0,8},{1,9},{2,10},{3,11},{4,12},{5,13},{6,14},{7,15},{8,0},{9,1},... | collective-permute-start | bytes 3096584 | tf_op jit(solution)/shard_map/ppermute | solution.py:26
  125.5 29.6 %collective-permute-start.23 = (bf16[608,896]{1,0:T(8,128)(2,1)}, bf16[608,896]{1,0:T(8,128)(2,1)}, u32[]{:S(2)}, u32[]{:S(2)}) collective-permute-start(bf16[608,896]{1,0:T(8,128)(2,1)} %pad_maximum_fusion.2), channel_id=1, source_target_pairs={{0,2},{1,3},{2,4},{3,5},{4,6},{5,7},{6,0},{7,1},{8,10},{9,11},{10,... | collective-permute-start | bytes 3268616 | tf_op jit(solution)/shard_map/ppermute | solution.py:26
  126.2 28.9 %collective-permute-start.24 = (bf16[608,896]{1,0:T(8,128)(2,1)}, bf16[608,896]{1,0:T(8,128)(2,1)}, u32[]{:S(2)}, u32[]{:S(2)}) collective-permute-start(bf16[608,896]{1,0:T(8,128)(2,1)} %slice.101), channel_id=1, source_target_pairs={{0,6},{1,7},{2,0},{3,1},{4,2},{5,3},{6,4},{7,5},{8,14},{9,15},{10,... | collective-permute-start | bytes 3268616 | tf_op jit(solution)/shard_map/ppermute | solution.py:26
  (27 other events, 296.3 us)

commit v6 on v5

--- a/solution.py
+++ b/solution.py
@@ -111,7 +111,8 @@
 
 
 def silu(hidden):
-    return hidden / (1.0 + jnp.exp(-hidden))
+    half = 0.5 * hidden
+    return half + half * jnp.tanh(half)
 
 
 def start_weights(block, held, pieces, spots, sem):
@@ -223,7 +224,7 @@
         wait_all(xbuf.at[here], xsem.at[i])
         loads[i].wait()
         part = jnp.dot(xbuf[here], wbuf[...], preferred_element_type=jnp.float32)
-        result[here] = silu((acc[here] + part) * inv[here]).astype(out.dtype)
+        result[here] = silu((acc[here] + part) * inv[here, 0:1]).astype(out.dtype)
         stores.append(pltpu.make_async_copy(result.at[here], out.at[here], osem.at[i]))
         stores[i].start()
     for store in stores:
@@ -309,7 +310,7 @@
         for v in (pair_a, left_a, right_a, opposite_a)
         for at in (n_a, 2 * n_a + extra)
     ).reshape(2, 2 * features)
-    inv = lax.rsqrt((tail[0] + tail[1])[:count] / total + 1e-06)[:, None]
+    inv = jnp.broadcast_to(lax.rsqrt((tail[0] + tail[1])[:count] / total + 1e-06)[:, None], (count, 128))
     own_lf, far_l, far_r, inv = gate(own_l, far_l, far_r, inv)
     own_o, far_o = shift(own_lf, y=1), shift(far_r, y=-1)
     rings = [own, own_l, own_r, other_hi, far_l, far_r]

time: 167 us -> 169 us (1.012)
    unnamed x36 -> x40, local copies, waits for them, and re-layouts: 3.87 us -> 3.74 us
  transfers between devices with their start and end apart: 33 -> 33, of which waited for: 11 -> 12; matrix products, arithmetic and copies ran while one was open for 9% -> 9% of each run, Pallas kernels for 17% -> 17%
where the time goes in v6:
time: 169 us; the launch traced here: 168 us
  waiting for transfers between devices  59.7 us (35%)
  starting transfers between devices  46.3 us (27%)
  Pallas kernels  41.8 us (25%)
  other arithmetic  9.86 us (6%)
  local copies, waits for them, and re-layouts  9.51 us (6%)
    ppermute x33, waiting for transfers between devices, shift(): return lax.ppermute(value, ('fsdp', 'tp'), links(**step))  59.7 us
    ppermute x33, starting transfers between devices, shift(): return lax.ppermute(value, ('fsdp', 'tp'), links(**step))  46.3 us
    pallas_call x1, Pallas kernels, product(): pl.pallas_call(functools.partial(product_kernel, len(tokens), len(weights...  20.3 us
    pallas_call x1, Pallas kernels, finish(): pl.pallas_call(functools.partial(finish_kernel, len(tokens), len(weights)...  10.9 us
    pallas_call x2, Pallas kernels, refresh(): pl.pallas_call(functools.partial(refresh_kernel, other_hi), out_shape=jax...  7.64 us
    unnamed x40, local copies, waits for them, and re-layouts  3.74 us
  transfers between devices with their start and end apart: 33, of which 12 were waited for; matrix products, arithmetic and copies ran while one was open for 9% of the time, Pallas kernels for 17%

profile of v6, /device:TPU:1, one launch (start us, length us, event | category | flops | bytes accessed | tf_op | source)
XLA Modules:
  0.0 167.7 jit_solution(4037619576845915592)
XLA Ops:
  0.0 3.0 %scaled_delta.1 = (bf16[2,56,1152]{2,1,0:T(8,128)(2,1)}, bf16[2,56,1152]{2,1,0:T(8,128)(2,1)}, bf16[2,56,1152]{2,1,0:T(8,128)(2,1)}, bf16[2,56,1152]{2,1,0:T(8,128)(2,1)}) custom-call(s32[56,72]{1,0:T(8,128)} %exps.1, bf16[56,9216]{1,0:T(8,128)(2,1)} %delta.1), custom_call_target="tpu_custom_call" | custom-call | tf_op jit(solution)/shard_map/scaled_delta/pallas_call | solution.py:63
  3.0 2.1 %collective-permute-start = (bf16[2,56,1152]{2,1,0:T(8,128)(2,1)}, bf16[2,56,1152]{2,1,0:T(8,128)(2,1)S(1)}, u32[]{:S(2)}, u32[]{:S(2)}) collective-permute-start(bf16[2,56,1152]{2,1,0:T(8,128)(2,1)} %get-tuple-element.44), channel_id=1, source_target_pairs={{0,2},{1,3},{2,4},{3,5},{4,6},{5,7},{6,0},{7,1},{8,10},{9,11},{10,... | collective-permute-start | bytes 774152 | tf_op jit(solution)/shard_map/ppermute | solution.py:26
  5.1 2.5 %collective-permute-start.1 = (bf16[2,56,1152]{2,1,0:T(8,128)(2,1)}, bf16[2,56,1152]{2,1,0:T(8,128)(2,1)S(1)}, u32[]{:S(2)}, u32[]{:S(2)}) collective-permute-start(bf16[2,56,1152]{2,1,0:T(8,128)(2,1)} %get-tuple-element.45), channel_id=1, source_target_pairs={{0,4},{1,5},{2,6},{3,7},{4,0},{5,1},{6,2},{7,3},{8,12},{9,13},{10,... | collective-permute-start | bytes 774152 | tf_op jit(solution)/shard_map/ppermute | solution.py:26
  8.7 2.1 %fusion.1 = (f32[1024]{0:T(1024)S(1)}, bf16[1024,896]{1,0:T(8,128)(2,1)S(1)}) fusion(bf16[1024,896]{1,0:T(8,128)(2,1)} %param.5, f32[896]{0:T(1024)} %param.6), kind=kLoop, calls=%fused_computation.3 | loop fusion | flops 4586496 | bytes 3677696 | tf_op jit(solution)/shard_map/reduce_sum | solution.py:277
  12.8 6.1 %collective-permute-done.1 = bf16[2,56,1152]{2,1,0:T(8,128)(2,1)S(1)} collective-permute-done((bf16[2,56,1152]{2,1,0:T(8,128)(2,1)}, bf16[2,56,1152]{2,1,0:T(8,128)(2,1)S(1)}, u32[]{:S(2)}, u32[]{:S(2)}) %collective-permute-start.1) | collective-permute-done | bytes 258080 | tf_op jit(solution)/shard_map/ppermute | solution.py:26
  23.8 2.2 %collective-permute-start.4 = (bf16[4,56,1152]{2,1,0:T(8,128)(2,1)S(1)}, bf16[4,56,1152]{2,1,0:T(8,128)(2,1)S(1)}, u32[]{:S(2)}, u32[]{:S(2)}) collective-permute-start(bf16[4,56,1152]{2,1,0:T(8,128)(2,1)S(1)} %pad_maximum_fusion.4), channel_id=1, source_target_pairs={{0,65},{1,64},{2,67},{3,66},{4,69},{5,68},{6,71},{7,70},{8,73},{9,... | collective-permute-start | bytes 1548296 | tf_op jit(solution)/shard_map/ppermute | solution.py:26
  28.0 6.0 %collective-permute-done.3.other = bf16[4,56,1152]{2,1,0:T(8,128)(2,1)S(1)} collective-permute-done((bf16[4,56,1152]{2,1,0:T(8,128)(2,1)S(1)}, bf16[4,56,1152]{2,1,0:T(8,128)(2,1)S(1)}, u32[]{:S(2)}, u32[]{:S(2)}) %collective-permute-start.3) | collective-permute-done | bytes 516128 | tf_op jit(solution)/shard_map/ppermute | solution.py:26
  34.0 2.2 %collective-permute-done.4.other = bf16[4,56,1152]{2,1,0:T(8,128)(2,1)S(1)} collective-permute-done((bf16[4,56,1152]{2,1,0:T(8,128)(2,1)S(1)}, bf16[4,56,1152]{2,1,0:T(8,128)(2,1)S(1)}, u32[]{:S(2)}, u32[]{:S(2)}) %collective-permute-start.4) | collective-permute-done | bytes 516128 | tf_op jit(solution)/shard_map/ppermute | solution.py:26
  37.2 2.7 %collective-permute-start.11 = (bf16[544,896]{1,0:T(8,128)(2,1)}, bf16[544,896]{1,0:T(8,128)(2,1)S(1)}, u32[]{:S(2)}, u32[]{:S(2)}) collective-permute-start(bf16[544,896]{1,0:T(8,128)(2,1)} %pad_maximum_fusion.3.refs_0_), channel_id=1, source_target_pairs={{0,6},{1,7},{2,0},{3,1},{4,2},{5,3},{6,4},{7,5},{8,14},{9,15},{10,... | collective-permute-start | bytes 2924552 | tf_op jit(solution)/shard_map/ppermute | solution.py:26
  39.9 2.1 %collective-permute-start.8 = (bf16[4,56,1152]{2,1,0:T(8,128)(2,1)}, bf16[4,56,1152]{2,1,0:T(8,128)(2,1)}, u32[]{:S(2)}, u32[]{:S(2)}) collective-permute-start(bf16[4,56,1152]{2,1,0:T(8,128)(2,1)} %pad_maximum_fusion.5.same), channel_id=1, source_target_pairs={{0,64},{1,65},{2,66},{3,67},{4,68},{5,69},{6,70},{7,71},{8,72},{9,... | collective-permute-start | bytes 1548296 | tf_op jit(solution)/shard_map/ppermute | solution.py:26
  42.0 3.8 %refresh_own.1 = bf16[8,56,1152]{2,1,0:T(8,128)(2,1)} custom-call(bf16[4,56,1152]{2,1,0:T(8,128)(2,1)} %pad_maximum_fusion.5.same, bf16[4,56,1152]{2,1,0:T(8,128)(2,1)} %copy-done.18, bf16[128,56,1152]{2,1,0:T(8,128)(2,1)} %bitcast.3), custom_call_target="tpu_custom_call" | custom-call | tf_op jit(solution)/shard_map/refresh_own/pallas_call | solution.py:90
  48.7 10.2 %collective-permute-done.10.refs_1_ = bf16[544,896]{1,0:T(8,128)(2,1)} collective-permute-done((bf16[544,896]{1,0:T(8,128)(2,1)}, bf16[544,896]{1,0:T(8,128)(2,1)}, u32[]{:S(2)}, u32[]{:S(2)}) %collective-permute-start.10) | collective-permute-done | bytes 974880 | tf_op jit(solution)/shard_map/ppermute | solution.py:26
  63.6 3.8 %refresh_far.1 = bf16[8,56,1152]{2,1,0:T(8,128)(2,1)} custom-call(bf16[4,56,1152]{2,1,0:T(8,128)(2,1)} %collective-permute-done.8.same, bf16[4,56,1152]{2,1,0:T(8,128)(2,1)} %copy-done.17, bf16[128,56,1152]{2,1,0:T(8,128)(2,1)} %bitcast.4), custom_call_target="tpu_custom_call" | custom-call | tf_op jit(solution)/shard_map/refresh_far/pallas_call | solution.py:90
  72.1 4.7 %collective-permute-done.9 = bf16[448,896]{1,0:T(8,128)(2,1)} collective-permute-done((bf16[448,896]{1,0:T(8,128)(2,1)S(1)}, bf16[448,896]{1,0:T(8,128)(2,1)}, u32[]{:S(2)}, u32[]{:S(2)}) %collective-permute-start.9) | collective-permute-done | bytes 802848 | tf_op jit(solution)/shard_map/ppermute | solution.py:26
  77.9 2.4 %pad_maximum_fusion.1.refs_3_ = bf16[896,896]{1,0:T(8,128)(2,1)} fusion(bf16[448,896]{1,0:T(8,128)(2,1)} %collective-permute-done.9, bf16[448,896]{1,0:T(8,128)(2,1)S(1)} %slice.102), kind=kLoop, calls=%fused_computation.5 | loop fusion | flops 3211264 | bytes 3211264 | tf_op jit(solution)/shard_map/concatenate | solution.py:303
  84.2 4.9 %collective-permute-done.19.refs_14_.refs_8_ = bf16[448,1152]{1,0:T(8,128)(2,1)} collective-permute-done((bf16[448,1152]{1,0:T(8,128)(2,1)}, bf16[448,1152]{1,0:T(8,128)(2,1)}, u32[]{:S(2)}, u32[]{:S(2)}) %collective-permute-start.19) | collective-permute-done | bytes 1032224 | tf_op jit(solution)/shard_map/ppermute | solution.py:26
  92.7 20.0 %collective-permute-done.16.refs_9_ = bf16[960,896]{1,0:T(8,128)(2,1)} collective-permute-done((bf16[960,896]{1,0:T(8,128)(2,1)}, bf16[960,896]{1,0:T(8,128)(2,1)}, u32[]{:S(2)}, u32[]{:S(2)}) %collective-permute-start.16) | collective-permute-done | bytes 1720352 | tf_op jit(solution)/shard_map/ppermute | solution.py:26
  112.8 5.4 %collective-permute-start.25 = (bf16[448,1152]{1,0:T(8,128)(2,1)S(1)}, bf16[448,1152]{1,0:T(8,128)(2,1)S(1)}, u32[]{:S(2)}, u32[]{:S(2)}) collective-permute-start(bf16[448,1152]{1,0:T(8,128)(2,1)S(1)} %bitcast.9), channel_id=1, source_target_pairs={{0,8},{1,9},{2,10},{3,11},{4,12},{5,13},{6,14},{7,15},{8,0},{9,1},... | collective-permute-start | bytes 3096584 | tf_op jit(solution)/shard_map/ppermute | solution.py:26
  122.1 2.3 %slice.101 = bf16[608,896]{1,0:T(8,128)(2,1)} slice(bf16[896,896]{1,0:T(8,128)(2,1)} %collective-permute-done.15.refs_5_), slice={[288:896], [0:896]} | slice | bytes 2179072 | tf_op jit(solution)/shard_map/slice | solution.py:322
  126.2 2.0 %collective-permute-start.24 = (bf16[608,896]{1,0:T(8,128)(2,1)}, bf16[608,896]{1,0:T(8,128)(2,1)}, u32[]{:S(2)}, u32[]{:S(2)}) collective-permute-start(bf16[608,896]{1,0:T(8,128)(2,1)} %slice.101), channel_id=1, source_target_pairs={{0,6},{1,7},{2,0},{3,1},{4,2},{5,3},{6,4},{7,5},{8,14},{9,15},{10,... | collective-permute-start | bytes 3268616 | tf_op jit(solution)/shard_map/ppermute | solution.py:26
  129.9 2.1 %collective-permute-done.30.refs_21_.refs_15_ = bf16[448,1152]{1,0:T(8,128)(2,1)S(1)} collective-permute-done((bf16[448,1152]{1,0:T(8,128)(2,1)}, bf16[448,1152]{1,0:T(8,128)(2,1)S(1)}, u32[]{:S(2)}, u32[]{:S(2)}) %collective-permute-start.30) | collective-permute-done | bytes 1032224 | tf_op jit(solution)/shard_map/ppermute | solution.py:26
  132.0 2.3 %collective-permute-done.31.refs_24_.refs_18_ = bf16[448,1152]{1,0:T(8,128)(2,1)S(1)} collective-permute-done((bf16[448,1152]{1,0:T(8,128)(2,1)S(1)}, bf16[448,1152]{1,0:T(8,128)(2,1)S(1)}, u32[]{:S(2)}, u32[]{:S(2)}) %collective-permute-start.31) | collective-permute-done | bytes 1032224 | tf_op jit(solution)/shard_map/ppermute | solution.py:26
  135.3 20.3 %product_most.1.refs_21_ = f32[1024,1152]{1,0:T(8,128)} custom-call(bf16[544,896]{1,0:T(8,128)(2,1)} %pad_maximum_fusion.3.refs_0_, bf16[544,896]{1,0:T(8,128)(2,1)} %collective-permute-done.10.refs_1_, bf16[544,896]{1,0:T(8,128)(2,1)} %copy-done.16, bf16[896,896]{1,0:T(8,128)(2,1)} %pad_maximum_fusion.1.refs_3_, ...), custom_call_target="tpu_custom_call" | custom-call | tf_op jit(solution)/shard_map/product_most/pallas_call | solution.py:188
  156.6 10.9 %product_rest.1 = bf16[1024,1152]{1,0:T(8,128)(2,1)} custom-call(bf16[544,896]{1,0:T(8,128)(2,1)} %collective-permute-done.12.refs_0_, bf16[320,896]{1,0:T(8,128)(2,1)} %collective-permute-done.13.refs_1_, bf16[608,896]{1,0:T(8,128)(2,1)} %copy-done.15, bf16[608,896]{1,0:T(8,128)(2,1)} %collective-permute-done.24.refs_3_, bf16[448,1152]{1,0:T(8,128)(2,1)} %bitcast.8, ...), custom_call_target="tpu_custom_call" | custom-call | tf_op jit(solution)/shard_map/product_rest/pallas_call | solution.py:236
  (113 shorter events, 41.1 us)
Async XLA Ops:
  5.1 13.8 %collective-permute-start.1 = (bf16[2,56,1152]{2,1,0:T(8,128)(2,1)}, bf16[2,56,1152]{2,1,0:T(8,128)(2,1)S(1)}, u32[]{:S(2)}, u32[]{:S(2)}) collective-permute-start(bf16[2,56,1152]{2,1,0:T(8,128)(2,1)} %get-tuple-element.45), channel_id=1, source_target_pairs={{0,4},{1,5},{2,6},{3,7},{4,0},{5,1},{6,2},{7,3},{8,12},{9,13},{10,... | collective-permute-start | bytes 774152 | tf_op jit(solution)/shard_map/ppermute | solution.py:26
  11.0 16.0 %collective-permute-start.7 = (bf16[272,896]{1,0:T(8,128)(2,1)S(1)}, bf16[272,896]{1,0:T(8,128)(2,1)S(1)}, u32[]{:S(2)}, u32[]{:S(2)}) collective-permute-start(bf16[272,896]{1,0:T(8,128)(2,1)S(1)} %fusion.3), channel_id=1, source_target_pairs={{0,1},{1,0},{2,3},{3,2},{4,5},{5,4},{6,7},{7,6},{8,9},{9,8},{10,11... | collective-permute-start | bytes 1462280 | tf_op jit(solution)/shard_map/ppermute | solution.py:26
  18.9 17.4 %collective-permute-start.5 = (bf16[320,896]{1,0:T(8,128)(2,1)S(1)}, bf16[320,896]{1,0:T(8,128)(2,1)S(1)}, u32[]{:S(2)}, u32[]{:S(2)}) collective-permute-start(bf16[320,896]{1,0:T(8,128)(2,1)S(1)} %slice.103.refs_6_), channel_id=1, source_target_pairs={{0,2},{1,3},{2,4},{3,5},{4,6},{5,7},{6,0},{7,1},{8,10},{9,11},{10,... | collective-permute-start | bytes 1720328 | tf_op jit(solution)/shard_map/ppermute | solution.py:26
  20.1 16.2 %collective-permute-start.6 = (bf16[320,896]{1,0:T(8,128)(2,1)S(1)}, bf16[320,896]{1,0:T(8,128)(2,1)S(1)}, u32[]{:S(2)}, u32[]{:S(2)}) collective-permute-start(bf16[320,896]{1,0:T(8,128)(2,1)S(1)} %slice.103.refs_6_), channel_id=1, source_target_pairs={{0,6},{1,7},{2,0},{3,1},{4,2},{5,3},{6,4},{7,5},{8,14},{9,15},{10,... | collective-permute-start | bytes 1720328 | tf_op jit(solution)/shard_map/ppermute | solution.py:26
  22.0 12.0 %collective-permute-start.3 = (bf16[4,56,1152]{2,1,0:T(8,128)(2,1)S(1)}, bf16[4,56,1152]{2,1,0:T(8,128)(2,1)S(1)}, u32[]{:S(2)}, u32[]{:S(2)}) collective-permute-start(bf16[4,56,1152]{2,1,0:T(8,128)(2,1)S(1)} %pad_maximum_fusion.4), channel_id=1, source_target_pairs={{0,1},{1,0},{2,3},{3,2},{4,5},{5,4},{6,7},{7,6},{8,9},{9,8},{10,11... | collective-permute-start | bytes 1548296 | tf_op jit(solution)/shard_map/ppermute | solution.py:26
  23.8 12.4 %collective-permute-start.4 = (bf16[4,56,1152]{2,1,0:T(8,128)(2,1)S(1)}, bf16[4,56,1152]{2,1,0:T(8,128)(2,1)S(1)}, u32[]{:S(2)}, u32[]{:S(2)}) collective-permute-start(bf16[4,56,1152]{2,1,0:T(8,128)(2,1)S(1)} %pad_maximum_fusion.4), channel_id=1, source_target_pairs={{0,65},{1,64},{2,67},{3,66},{4,69},{5,68},{6,71},{7,70},{8,73},{9,... | collective-permute-start | bytes 1548296 | tf_op jit(solution)/shard_map/ppermute | solution.py:26
  37.2 21.7 %collective-permute-start.10 = (bf16[544,896]{1,0:T(8,128)(2,1)}, bf16[544,896]{1,0:T(8,128)(2,1)}, u32[]{:S(2)}, u32[]{:S(2)}) collective-permute-start(bf16[544,896]{1,0:T(8,128)(2,1)} %pad_maximum_fusion.3.refs_0_), channel_id=1, source_target_pairs={{0,2},{1,3},{2,4},{3,5},{4,6},{5,7},{6,0},{7,1},{8,10},{9,11},{10,... | collective-permute-start | bytes 2924552 | tf_op jit(solution)/shard_map/ppermute | solution.py:26
  37.2 21.7 %collective-permute-start.11 = (bf16[544,896]{1,0:T(8,128)(2,1)}, bf16[544,896]{1,0:T(8,128)(2,1)S(1)}, u32[]{:S(2)}, u32[]{:S(2)}) collective-permute-start(bf16[544,896]{1,0:T(8,128)(2,1)} %pad_maximum_fusion.3.refs_0_), channel_id=1, source_target_pairs={{0,6},{1,7},{2,0},{3,1},{4,2},{5,3},{6,4},{7,5},{8,14},{9,15},{10,... | collective-permute-start | bytes 2924552 | tf_op jit(solution)/shard_map/ppermute | solution.py:26
  39.9 20.9 %collective-permute-start.8 = (bf16[4,56,1152]{2,1,0:T(8,128)(2,1)}, bf16[4,56,1152]{2,1,0:T(8,128)(2,1)}, u32[]{:S(2)}, u32[]{:S(2)}) collective-permute-start(bf16[4,56,1152]{2,1,0:T(8,128)(2,1)} %pad_maximum_fusion.5.same), channel_id=1, source_target_pairs={{0,64},{1,65},{2,66},{3,67},{4,68},{5,69},{6,70},{7,71},{8,72},{9,... | collective-permute-start | bytes 1548296 | tf_op jit(solution)/shard_map/ppermute | solution.py:26
  45.8 22.2 %collective-permute-start.17 = (bf16[448,1152]{1,0:T(8,128)(2,1)}, bf16[448,1152]{1,0:T(8,128)(2,1)}, u32[]{:S(2)}, u32[]{:S(2)}) collective-permute-start(bf16[448,1152]{1,0:T(8,128)(2,1)} %bitcast.5), channel_id=1, source_target_pairs={{0,16},{1,17},{2,18},{3,19},{4,20},{5,21},{6,22},{7,23},{8,24},{9,... | collective-permute-start | bytes 3096584 | tf_op jit(solution)/shard_map/ppermute | solution.py:26
  47.2 20.9 %collective-permute-start.18 = (bf16[448,1152]{1,0:T(8,128)(2,1)}, bf16[448,1152]{1,0:T(8,128)(2,1)}, u32[]{:S(2)}, u32[]{:S(2)}) collective-permute-start(bf16[448,1152]{1,0:T(8,128)(2,1)} %bitcast.6), channel_id=1, source_target_pairs={{0,48},{1,49},{2,50},{3,51},{4,52},{5,53},{6,54},{7,55},{8,56},{9,... | collective-permute-start | bytes 3096584 | tf_op jit(solution)/shard_map/ppermute | solution.py:26
  59.9 20.7 %collective-permute-start.12 = (bf16[544,896]{1,0:T(8,128)(2,1)}, bf16[544,896]{1,0:T(8,128)(2,1)}, u32[]{:S(2)}, u32[]{:S(2)}) collective-permute-start(bf16[544,896]{1,0:T(8,128)(2,1)} %collective-permute-done.10.refs_1_), channel_id=1, source_target_pairs={{0,2},{1,3},{2,4},{3,5},{4,6},{5,7},{6,0},{7,1},{8,10},{9,11},{10,... | collective-permute-start | bytes 2924552 | tf_op jit(solution)/shard_map/ppermute | solution.py:26
  60.8 16.0 %collective-permute-start.9 = (bf16[448,896]{1,0:T(8,128)(2,1)S(1)}, bf16[448,896]{1,0:T(8,128)(2,1)}, u32[]{:S(2)}, u32[]{:S(2)}) collective-permute-start(bf16[448,896]{1,0:T(8,128)(2,1)S(1)} %slice.102), channel_id=1, source_target_pairs={{0,1},{1,0},{2,3},{3,2},{4,5},{5,4},{6,7},{7,6},{8,9},{9,8},{10,11... | collective-permute-start | bytes 2408456 | tf_op jit(solution)/shard_map/ppermute | solution.py:26
  61.7 18.6 %collective-permute-start.13 = (bf16[320,896]{1,0:T(8,128)(2,1)}, bf16[320,896]{1,0:T(8,128)(2,1)}, u32[]{:S(2)}, u32[]{:S(2)}) collective-permute-start(bf16[320,896]{1,0:T(8,128)(2,1)} %copy-done.13), channel_id=1, source_target_pairs={{0,6},{1,7},{2,0},{3,1},{4,2},{5,3},{6,4},{7,5},{8,14},{9,15},{10,... | collective-permute-start | bytes 1720328 | tf_op jit(solution)/shard_map/ppermute | solution.py:26
  68.1 21.0 %collective-permute-start.19 = (bf16[448,1152]{1,0:T(8,128)(2,1)}, bf16[448,1152]{1,0:T(8,128)(2,1)}, u32[]{:S(2)}, u32[]{:S(2)}) collective-permute-start(bf16[448,1152]{1,0:T(8,128)(2,1)} %bitcast.10), channel_id=1, source_target_pairs={{0,16},{1,17},{2,18},{3,19},{4,20},{5,21},{6,22},{7,23},{8,24},{9,... | collective-permute-start | bytes 3096584 | tf_op jit(solution)/shard_map/ppermute | solution.py:26
  69.0 20.0 %collective-permute-start.20 = (bf16[448,1152]{1,0:T(8,128)(2,1)}, bf16[448,1152]{1,0:T(8,128)(2,1)}, u32[]{:S(2)}, u32[]{:S(2)}) collective-permute-start(bf16[448,1152]{1,0:T(8,128)(2,1)} %bitcast.11), channel_id=1, source_target_pairs={{0,48},{1,49},{2,50},{3,51},{4,52},{5,53},{6,54},{7,55},{8,56},{9,... | collective-permute-start | bytes 3096584 | tf_op jit(solution)/shard_map/ppermute | solution.py:26
  76.8 36.0 %collective-permute-start.16 = (bf16[960,896]{1,0:T(8,128)(2,1)}, bf16[960,896]{1,0:T(8,128)(2,1)}, u32[]{:S(2)}, u32[]{:S(2)}) collective-permute-start(bf16[960,896]{1,0:T(8,128)(2,1)} %pad_maximum_fusion), channel_id=1, source_target_pairs={{0,1},{1,0},{2,3},{3,2},{4,5},{5,4},{6,7},{7,6},{8,9},{9,8},{10,11... | collective-permute-start | bytes 5160968 | tf_op jit(solution)/shard_map/ppermute | solution.py:26
  80.6 38.1 %collective-permute-start.14 = (bf16[896,896]{1,0:T(8,128)(2,1)}, bf16[896,896]{1,0:T(8,128)(2,1)}, u32[]{:S(2)}, u32[]{:S(2)}) collective-permute-start(bf16[896,896]{1,0:T(8,128)(2,1)} %pad_maximum_fusion.1.refs_3_), channel_id=1, source_target_pairs={{0,2},{1,3},{2,4},{3,5},{4,6},{5,7},{6,0},{7,1},{8,10},{9,11},{10,... | collective-permute-start | bytes 4816904 | tf_op jit(solution)/shard_map/ppermute | solution.py:26
  81.7 38.1 %collective-permute-start.15 = (bf16[896,896]{1,0:T(8,128)(2,1)}, bf16[896,896]{1,0:T(8,128)(2,1)}, u32[]{:S(2)}, u32[]{:S(2)}) collective-permute-start(bf16[896,896]{1,0:T(8,128)(2,1)} %pad_maximum_fusion.1.refs_3_), channel_id=1, source_target_pairs={{0,6},{1,7},{2,0},{3,1},{4,2},{5,3},{6,4},{7,5},{8,14},{9,15},{10,... | collective-permute-start | bytes 4816904 | tf_op jit(solution)/shard_map/ppermute | solution.py:26
  90.1 28.1 %collective-permute-start.21 = (bf16[448,1152]{1,0:T(8,128)(2,1)}, bf16[448,1152]{1,0:T(8,128)(2,1)S(1)}, u32[]{:S(2)}, u32[]{:S(2)}) collective-permute-start(bf16[448,1152]{1,0:T(8,128)(2,1)} %collective-permute-done.17.refs_11_.refs_5_), channel_id=1, source_target_pairs={{0,16},{1,17},{2,18},{3,19},{4,20},{5,21},{6,22},{7,23},{8,24},{9,... | collective-permute-start | bytes 3096584 | tf_op jit(solution)/shard_map/ppermute | solution.py:26
  91.4 27.0 %collective-permute-start.22 = (bf16[448,1152]{1,0:T(8,128)(2,1)}, bf16[448,1152]{1,0:T(8,128)(2,1)S(1)}, u32[]{:S(2)}, u32[]{:S(2)}) collective-permute-start(bf16[448,1152]{1,0:T(8,128)(2,1)} %collective-permute-done.20.refs_15_.refs_9_), channel_id=1, source_target_pairs={{0,48},{1,49},{2,50},{3,51},{4,52},{5,53},{6,54},{7,55},{8,56},{9,... | collective-permute-start | bytes 3096584 | tf_op jit(solution)/shard_map/ppermute | solution.py:26
  112.8 12.7 %collective-permute-start.25 = (bf16[448,1152]{1,0:T(8,128)(2,1)S(1)}, bf16[448,1152]{1,0:T(8,128)(2,1)S(1)}, u32[]{:S(2)}, u32[]{:S(2)}) collective-permute-start(bf16[448,1152]{1,0:T(8,128)(2,1)S(1)} %bitcast.9), channel_id=1, source_target_pairs={{0,8},{1,9},{2,10},{3,11},{4,12},{5,13},{6,14},{7,15},{8,0},{9,1},... | collective-permute-start | bytes 3096584 | tf_op jit(solution)/shard_map/ppermute | solution.py:26
  125.5 30.1 %collective-permute-start.23 = (bf16[608,896]{1,0:T(8,128)(2,1)}, bf16[608,896]{1,0:T(8,128)(2,1)S(1)}, u32[]{:S(2)}, u32[]{:S(2)}) collective-permute-start(bf16[608,896]{1,0:T(8,128)(2,1)} %pad_maximum_fusion.2), channel_id=1, source_target_pairs={{0,2},{1,3},{2,4},{3,5},{4,6},{5,7},{6,0},{7,1},{8,10},{9,11},{10,... | collective-permute-start | bytes 3268616 | tf_op jit(solution)/shard_map/ppermute | solution.py:26
  126.2 29.4 %collective-permute-start.24 = (bf16[608,896]{1,0:T(8,128)(2,1)}, bf16[608,896]{1,0:T(8,128)(2,1)}, u32[]{:S(2)}, u32[]{:S(2)}) collective-permute-start(bf16[608,896]{1,0:T(8,128)(2,1)} %slice.101), channel_id=1, source_target_pairs={{0,6},{1,7},{2,0},{3,1},{4,2},{5,3},{6,4},{7,5},{8,14},{9,15},{10,... | collective-permute-start | bytes 3268616 | tf_op jit(solution)/shard_map/ppermute | solution.py:26
  (29 other events, 333.0 us)
